TPU v7x, 32 devices: a whole 2x2x4 slice. The times are simulated.
32 devices in a mesh: group: 2 (over x), store: 4 (over z), tensor: 4 (over y, core).
Axes of the slice: x: 2, y: 2, z: 4, core: 2. Of those that a mesh axis runs over, the one named last changes fastest.
Arguments:
- queries: bfloat16 [2048, 8192], P(('group', 'store'), 'tensor'), parts along dimension 0, may hold values from -110 to 110
- cached_key_slabs: bfloat16 [2048, 8, 24, 128], P(('group', 'store'), 'tensor'), parts along dimension 0, may hold values from -6 to 6, as said below
- cached_value_slabs: bfloat16 [2048, 8, 24, 128], P(('group', 'store'), 'tensor'), parts along dimension 0, may hold values from -6 to 6, as said below
- request_cache_lengths: int32 [2048], P(('group', 'store')), parts along dimension 0, may hold values from 2 to 24, as said below
- output_projection_weight: bfloat16 [8192, 8192], P('tensor'), may hold values from -0.0625 to 0.0625
- adapter_shrink_weight: bfloat16 [32, 64, 8192], P('store', None, 'tensor'), may hold values from -0.0625 to 0.0625
- adapter_expand_weight: bfloat16 [32, 64, 8192], P('store', None, 'tensor'), may hold values from -0.75 to 0.75
- adapter_storage_slot: int32 [32], replicated, may hold values from 0 to 31, as said below
- wanted: int32 [4, 8], replicated, may hold values from 0 to 31, as said below
- request_wanted_entry: int32 [8, 256], P(('group', 'store')), parts along dimension 0, may hold values from 0 to 7, never falling along the last dimension, each value on 1 to 96 neighbouring positions
Outputs:
- mixed: bfloat16 [2048, 8192], P(('group', 'store'), 'tensor'), parts along dimension 0
There are 2 independent parts, one for each index of `group`. A program takes and returns all parts, laid end to end along the dimension named above; an argument that names none is the same for every part. Nothing has to cross between parts.
Inputs may be any that keep to these rules, and one draw needn't show every extreme that they name: `cached_key_slabs`: slots s and t hold equal keys when s * 1 equals t * 1. `cached_value_slabs`: laid out as cached_key_slabs, with the same equal copies. `request_cache_lengths`: some request holds exactly 24 positions. A permutation: adapter a lies in slot adapter_storage_slot[a] of adapter_shrink_weight and adapter_expand_weight, held by store index adapter_storage_slot[a] // 8. `wanted`: each row names 8 different adapters; at most 2 of one row are held by one store index, and exactly 2 by some index in every row. `request_wanted_entry`: never falling along a row; every entry 0 to 7 is used by 1 to 96 requests of a row, one by exactly 96.
All inputs are finite; a program needn't handle non-finite values.
Results may differ from a plain program's by a relative error of at most 0.013.
Values may be sent and summed in bfloat16 or wider, within the bound.
No kernel may reach another device: no remote copies, remote signals or barrier semaphores. Data moves between devices by JAX's collectives and lax.ppermute only.
A program may use at most 384 MiB of HBM per device.

v0:
```python
import math

import jax
import jax.numpy as jnp
from jax import lax
from jax.sharding import PartitionSpec as P

HD = 128
ADAPTER_RANK = 64
USED_PER_STORE = 8
CAP = 2


def attend_local(queries, cached_key_slabs, cached_value_slabs, lengths):
    row_count = cached_key_slabs.shape[0]
    slot_count = cached_key_slabs.shape[1]
    group_size = queries.shape[1] // (slot_count * HD)
    grouped = queries.reshape(row_count, slot_count, group_size, HD)
    scores = jnp.einsum(
        "rsgd,rsld->rsgl", grouped, cached_key_slabs, preferred_element_type=jnp.float32
    ) / math.sqrt(HD)
    visible = jnp.arange(cached_key_slabs.shape[2])[None, :] < lengths[:, None]
    scores = jnp.where(visible[:, None, None, :], scores, -jnp.inf)
    weights = jax.nn.softmax(scores, axis=-1).astype(jnp.bfloat16)
    attended = jnp.einsum(
        "rsgl,rsld->rsgd", weights, cached_value_slabs, preferred_element_type=jnp.float32
    )
    return attended.astype(jnp.bfloat16).reshape(row_count, queries.shape[1])


def shards(
    queries,
    cached_key_slabs,
    cached_value_slabs,
    request_cache_lengths,
    output_projection_weight,
    adapter_shrink_weight,
    adapter_expand_weight,
    adapter_storage_slot,
    wanted,
    request_wanted_entry,
):
    attended = attend_local(queries, cached_key_slabs, cached_value_slabs, request_cache_lengths)
    my_store = lax.axis_index("store")
    per_store = adapter_shrink_weight.shape[0]
    local_model_width = adapter_shrink_weight.shape[2]
    slot_table = jnp.take(adapter_storage_slot, wanted, axis=0)
    holders = slot_table // per_store
    local_index = slot_table % per_store
    same_holder = holders[:, :, None] == holders[:, None, :]
    earlier = jnp.arange(USED_PER_STORE)[None, :] < jnp.arange(USED_PER_STORE)[:, None]
    ranks = jnp.sum(jnp.logical_and(same_holder, earlier[None, :, :]), axis=2)
    mine = holders == my_store
    hit = jnp.logical_and(mine[:, :, None], ranks[:, :, None] == jnp.arange(CAP)[None, None, :])
    send_index = jnp.sum(jnp.where(hit, local_index[:, :, None], 0), axis=1).reshape(-1)
    send_down = jnp.take(adapter_shrink_weight, send_index, axis=0)
    send_up = jnp.take(adapter_expand_weight, send_index, axis=0)
    got_down, got_up = (
        lax.all_to_all(send_down, "store", split_axis=0, concat_axis=0, tiled=True),
        lax.all_to_all(send_up, "store", split_axis=0, concat_axis=0, tiled=True),
    )
    my_holders = lax.dynamic_index_in_dim(holders, my_store, 0, keepdims=False)
    my_ranks = lax.dynamic_index_in_dim(ranks, my_store, 0, keepdims=False)
    places = my_holders * CAP + my_ranks
    used_down = jnp.take(got_down, places, axis=0)
    used_up = jnp.take(got_up, places, axis=0)
    base_part = jnp.dot(attended, output_projection_weight, preferred_element_type=jnp.float32)
    base_output = lax.psum_scatter(base_part, "tensor", scatter_dimension=1, tiled=True)
    request_picks = request_wanted_entry[0]
    selector = request_picks[:, None] == jnp.arange(USED_PER_STORE)[None, :]
    stacked_down = used_down.reshape(USED_PER_STORE * ADAPTER_RANK, local_model_width)
    spread_in = lax.dot_general(
        attended, stacked_down, (((1,), (1,)), ((), ())), preferred_element_type=jnp.float32
    )
    shrink_part = jnp.sum(
        jnp.where(
            selector[:, :, None],
            spread_in.reshape(-1, USED_PER_STORE, ADAPTER_RANK),
            jnp.float32(0.0),
        ),
        axis=1,
    )
    shrink = lax.psum(shrink_part, "tensor")
    shrink_low = shrink.astype(jnp.bfloat16)
    spread_across = jnp.where(
        selector[:, :, None], shrink_low[:, None, :], jnp.zeros((), jnp.bfloat16)
    ).reshape(-1, USED_PER_STORE * ADAPTER_RANK)
    adapter_delta = jnp.dot(
        spread_across,
        used_up.reshape(USED_PER_STORE * ADAPTER_RANK, local_model_width),
        preferred_element_type=jnp.float32,
    )
    return (base_output + adapter_delta).astype(jnp.bfloat16)


def solution(mesh):
    placed = (
        P(("group", "store"), "tensor"),
        P(("group", "store"), "tensor", None, None),
        P(("group", "store"), "tensor", None, None),
        P(("group", "store")),
        P("tensor", None),
        P("store", None, "tensor"),
        P("store", None, "tensor"),
        P(),
        P(),
        P(("group", "store"), None),
    )
    return jax.shard_map(
        shards,
        mesh=mesh,
        in_specs=placed,
        out_specs=P(("group", "store"), "tensor"),
        check_vma=False,
    )
```

profile of v0, /device:TPU:0, one launch (start us, length us, event | category | flops | bytes accessed | tf_op | source)
XLA Modules:
  0.0 179.4 jit_solution(11085241596728034147)
XLA Ops:
  6.5 0.0 copy-start
  6.5 0.0 reduce-scatter.2.cloned.1.call-start
  6.5 0.9 iota_compare_fusion
  7.5 2.5 %copy.12 = bf16[32,8,16,128]{3,2,1,0:T(8,128)(2,1)} copy(bf16[32,8,16,128]{3,1,2,0:T(8,128)(2,1)} %bitcast.26) | data formatting | bytes 2097152
  9.9 5.6 %fusion.35 = (f32[256,2,8]{2,1,0:T(2,128)S(1)}, f32[256,2,8,24]{3,2,1,0:T(8,128)}) fusion(pred[256,24]{1,0:T(8,128)(4,1)S(1)} %iota_compare_fusion, bf16[256,2,8,128]{3,2,1,0:T(8,128)(2,1)} %bitcast.25, bf16[256,2,24,128]{3,2,1,0:T(8,128)(2,1)} %param.13), kind=kOutput, calls=%fused_computation.66 | convolution fusion | flops 25559064 | bytes 4610048 | tf_op jit(solution)/shard_map/sub | solution.py:24
  15.5 0.0 copy-done
  15.5 2.7 %convolution_convert_fusion = bf16[256,2,8,128]{3,2,1,0:T(8,128)(2,1)S(1)} fusion(bf16[256,2,24,128]{3,2,1,0:T(8,128)(2,1)S(1)} %copy-done, f32[256,2,8,24]{3,2,1,0:T(8,128)} %get-tuple-element.13, f32[256,2,8]{2,1,0:T(2,128)S(1)} %get-tuple-element.12), kind=kOutput, calls=%fused_computation.20 | convolution fusion | flops 25886720 | bytes 4603904 | tf_op jit(solution)/shard_map/rsgl,rsld->rsgd/dot_general | solution.py:25
  18.2 0.0 copy-start.3
  18.2 1.0 copy-done.3
  19.2 17.0 %fusion.15 = f32[256,8192]{1,0:T(8,128)} fusion(bf16[2048,8192]{1,0:T(8,128)(2,1)} %param.16, bf16[32,8,16,128]{3,2,1,0:T(8,128)(2,1)S(1)} %bitcast.27), kind=kOutput, calls=%fused_computation.23 | convolution fusion | flops 8589934592 | bytes 42991616 | tf_op jit(solution)/shard_map/dot_general | solution.py:67
  36.2 0.0 copy-start.6
  36.2 0.0 copy-start.2
  36.2 0.0 reduce-scatter.2.cloned.1.call-update
  36.2 0.6 copy-done.6
  36.9 0.1 reshape.176
  37.0 0.0 copy-done.2
  37.0 0.7 gather_fusion
  37.7 0.1 reshape.175
  37.8 0.2 convert_reduce_fusion
  38.0 0.1 select_reduce_fusion
  38.2 0.1 copy.11
  38.3 0.1 reshape.141
  38.4 2.3 %gather_fusion.1 = bf16[8,64,2048]{2,1,0:T(8,128)(2,1)S(1)} fusion(bf16[8,64,2048]{2,1,0:T(8,128)(2,1)} %param.17, s32[1024]{0:T(1024)S(1)} %pad_clamp_fusion.1), kind=kCustom, calls=%fused_computation.clone | custom fusion | bytes 4194336 | tf_op jit(solution)/shard_map/jit(_take)/gather | solution.py:56
  40.7 3.6 %gather_fusion.3 = bf16[8,64,2048]{2,1,0:T(8,128)(2,1)} fusion(bf16[8,64,2048]{2,1,0:T(8,128)(2,1)} %param.18, s32[1024]{0:T(1024)S(1)} %pad_clamp_fusion.1), kind=kCustom, calls=%fused_computation.2.clone | custom fusion | bytes 4194336 | tf_op jit(solution)/shard_map/jit(_take)/gather | solution.py:57
  44.3 3.5 %broadcast_select_fusion.1 = (bf16[8,64,2048]{2,1,0:T(8,128)(2,1)}, bf16[8,64,2048]{2,1,0:T(8,128)(2,1)S(1)}) fusion(bf16[8,64,2048]{2,1,0:T(8,128)(2,1)S(1)} %gather_fusion.1, pred[8]{0:T(512)(128)(4,1)S(1)} %compare_and_fusion.1, bf16[8,64,2048]{2,1,0:T(8,128)(2,1)} %gather_fusion.3), kind=kLoop, calls=%fused_computation.18 | loop fusion | flops 2097152 | bytes 8388616 | tf_op jit(solution)/shard_map/jit(_take)/select_n | solution.py:56
  47.7 54.4 %all_to_all.10 = bf16[8,64,2048]{2,1,0:T(8,128)(2,1)} all-to-all(bf16[8,64,2048]{2,1,0:T(8,128)(2,1)S(1)} %get-tuple-element.11), channel_id=1, replica_groups=mesh['group'=2,'store'=4,'tensor'=4] {'store'}, dimensions={0} | all-to-all | bytes 4194304 | tf_op jit(solution)/shard_map/all_to_all | solution.py:60
  102.1 0.0 copy-start.4
  102.1 3.7 %all-to-all-start = ((bf16[8,64,2048]{2,1,0:T(8,128)(2,1)}), bf16[8,64,2048]{2,1,0:T(8,128)(2,1)S(1)}, u32[]{:S(2)}, u32[]{:S(2)}) async-start(bf16[8,64,2048]{2,1,0:T(8,128)(2,1)} %get-tuple-element.10), calls=%async_computation.1 | async-start | bytes 4194304 | tf_op jit(solution)/shard_map/all_to_all | solution.py:59
  105.8 0.0 copy-done.4
  105.9 0.0 copy-start.7
  105.9 1.3 reshape.196
  107.2 0.0 copy-done.7
  107.2 3.6 %gather_fusion.4 = bf16[8,64,2048]{2,1,0:T(8,128)(2,1)} fusion(bf16[8,64,2048]{2,1,0:T(8,128)(2,1)} %all_to_all.10, s32[1024]{0:T(1024)S(1)} %pad_clamp_fusion), kind=kCustom, calls=%fused_computation.3.clone | custom fusion | bytes 4194336 | tf_op jit(solution)/shard_map/jit(_take)/gather | solution.py:66
  110.8 0.0 copy-start.5
  110.8 42.3 %all-to-all-done = bf16[8,64,2048]{2,1,0:T(8,128)(2,1)S(1)} async-done(((bf16[8,64,2048]{2,1,0:T(8,128)(2,1)}), bf16[8,64,2048]{2,1,0:T(8,128)(2,1)S(1)}, u32[]{:S(2)}, u32[]{:S(2)}) %all-to-all-start) | async-done | bytes 2097184 | tf_op jit(solution)/shard_map/all_to_all | solution.py:59
  153.1 2.0 %gather_fusion.2 = bf16[8,64,2048]{2,1,0:T(8,128)(2,1)} fusion(bf16[8,64,2048]{2,1,0:T(8,128)(2,1)S(1)} %all-to-all-done, s32[1024]{0:T(1024)S(1)} %pad_clamp_fusion), kind=kCustom, calls=%fused_computation.1.clone | custom fusion | bytes 4194336 | tf_op jit(solution)/shard_map/jit(_take)/gather | solution.py:65
  155.1 0.0 copy-done.5
  155.1 2.3 %fusion.12 = f32[256,64]{0,1:T(8,128)S(1)} fusion(bf16[256,2048,1]{1,0,2:T(8,128)(2,1)S(1)} %copy-done.5, bf16[8,64,2048]{2,1,0:T(8,128)(2,1)} %gather_fusion.2, pred[8]{0:T(512)(128)(4,1)S(1)} %get-tuple-element.6, pred[256,8]{0,1:T(8,128)(4,1)S(1)} %iota_compare_fusion.1), kind=kOutput, calls=%fused_computation.22 | convolution fusion | flops 538165248 | bytes 3213320 | tf_op jit(solution)/shard_map/dot_general | solution.py:72
  157.5 0.0 copy-start.1
  157.5 11.0 %psum.7 = bf16[256,64]{0,1:T(8,128)(2,1)S(1)} all-reduce(f32[256,64]{0,1:T(8,128)S(1)} %fusion.12), channel_id=1, replica_groups=mesh['group'=2,'store'=4,'tensor'=4] {'tensor'}, use_global_device_ids=true, to_apply=%region_6.8 | all-reduce | flops 16384 | bytes 98304 | tf_op jit(solution)/shard_map/psum | solution.py:83
  168.5 0.0 reduce-scatter.2.cloned.1.call-done
  168.6 4.0 %fusion.2 = bf16[256,2048]{1,0:T(8,128)(2,1)} fusion(f32[256,2048]{1,0:T(8,128)} %reduce-scatter.2.cloned.1.call-done, bf16[8,64,2048]{2,1,0:T(8,128)(2,1)} %gather_fusion.4, pred[8]{0:T(512)(128)(4,1)S(1)} %get-tuple-element.6, pred[256,8]{0,1:T(8,128)(4,1)S(1)} %iota_compare_fusion.1, bf16[256,64]{0,1:T(8,128)(2,1)S(1)} %psum.7), kind=kOutput, calls=%fused_computation.8 | convolution fusion | flops 539099136 | bytes 5277704 | tf_op jit(solution)/shard_map/dot_general | solution.py:88
  172.5 0.0 copy-done.1
  (11 shorter events, 0.1 us)
Async XLA Ops:
  6.5 8.9 %copy-start = (bf16[256,2,24,128]{3,2,1,0:T(8,128)(2,1)S(1)}, bf16[256,2,24,128]{3,2,1,0:T(8,128)(2,1)}, u32[]{:S(2)}) copy-start(bf16[256,2,24,128]{3,2,1,0:T(8,128)(2,1)} %param.14) | copy-start | bytes 9437188
  6.5 162.0 %reduce-scatter.2.cloned.1.call-start = ((), (), s32[]{:S(2)}) async-start(), calls=%async_computation.3 | async-start | bytes 10485760 | tf_op jit(solution)/shard_map/reduce_scatter | solution.py:68
  18.2 1.0 copy-start.3
  36.2 0.7 copy-start.6
  36.2 0.8 copy-start.2
  102.1 3.8 %copy-start.4 = (bf16[256,2,8,128]{3,2,1,0:T(8,128)(2,1)S(1)}, bf16[256,2,8,128]{3,2,1,0:T(8,128)(2,1)}, u32[]{:S(2)}) copy-start(bf16[256,2,8,128]{3,2,1,0:T(8,128)(2,1)} %copy-done.3) | copy-start | bytes 3145732
  102.1 51.0 %all-to-all-start = ((bf16[8,64,2048]{2,1,0:T(8,128)(2,1)}), bf16[8,64,2048]{2,1,0:T(8,128)(2,1)S(1)}, u32[]{:S(2)}, u32[]{:S(2)}) async-start(bf16[8,64,2048]{2,1,0:T(8,128)(2,1)} %get-tuple-element.10), calls=%async_computation.1 | async-start | bytes 4194304 | tf_op jit(solution)/shard_map/all_to_all | solution.py:59
  105.9 1.3 copy-start.7
  110.8 44.4 %copy-start.5 = (bf16[256,2048,1]{1,0,2:T(8,128)(2,1)S(1)}, bf16[256,2048,1]{1,0,2:T(8,128)(2,1)}, u32[]{:S(2)}) copy-start(bf16[256,2048,1]{1,0,2:T(8,128)(2,1)} %reshape.196) | copy-start | bytes 3145732
  157.5 15.1 %copy-start.1 = (bf16[256,2,24,128]{3,2,1,0:T(8,128)(2,1)S(1)}, bf16[256,2,24,128]{3,2,1,0:T(8,128)(2,1)}, u32[]{:S(2)}) copy-start(bf16[256,2,24,128]{3,2,1,0:T(8,128)(2,1)} %param.14) | copy-start | bytes 9437188
Sparse Core Ops, SparseCore 0:
  36.3 74.4 reduce-scatter.1
where the time goes:
time: 180 us; the launch traced here: 179 us
  blocking collectives  65.4 us (36%)
  waiting for transfers between devices  42.3 us (24%)
  matrix products  31.6 us (18%)
  local copies, waits for them, and re-layouts  17.9 us (10%)
  between operations  13.5 us (8%)
  other arithmetic  4.84 us (3%)
  starting transfers between devices  3.74 us (2%)
    all_to_all x1, blocking collectives, shards(): lax.all_to_all(send_up, 'store', split_axis=0, concat_axis=0, tiled=True)  54.4 us
    all_to_all x1, waiting for transfers between devices, shards(): lax.all_to_all(send_down, 'store', split_axis=0, concat_axis=0, tiled=True)  42.3 us
    dot_general x1, matrix products, shards(): jnp.dot(attended, output_projection_weight, preferred_element_type=jnp.fl...  17 us
    psum x1, blocking collectives, shards(): shrink = lax.psum(shrink_part, 'tensor')  11 us
    sub x1, matrix products, attend_local(): weights = jax.nn.softmax(scores, axis=-1).astype(jnp.bfloat16)  5.55 us
    unnamed x17, local copies, waits for them, and re-layouts  4.1 us
    dot_general x1, matrix products, shards(): jnp.dot(spread_across, used_up.reshape(USED_PER_STORE * ADAPTER_RANK, loc...  3.98 us
    all_to_all x1, starting transfers between devices, shards(): lax.all_to_all(send_down, 'store', split_axis=0, concat_axis=0, tiled=True)  3.74 us
  transfers between devices with their start and end apart: 2, of which 1 were waited for; matrix products, arithmetic and copies ran while one was open for 11% of the time, Pallas kernels for 0%

commit v1 on v0

v1 whole, which is shorter than its diff:
```python
import functools
import math

import jax
import jax.numpy as jnp
from jax import lax
from jax.experimental import pallas as pl
from jax.experimental.pallas import tpu as pltpu
from jax.sharding import PartitionSpec as P

CAP = 2
ROWS = 8
MASKED = -1e30
MIB = 1 << 20
ANY = pl.BlockSpec(memory_space=pl.ANY)
HBM = pl.BlockSpec(memory_space=pltpu.HBM)
SMEM = pl.BlockSpec(memory_space=pltpu.SMEM)
VMEM = pl.BlockSpec(memory_space=pltpu.VMEM)


SMALL = pl.CostEstimate(flops=1, bytes_accessed=1, transcendentals=0)


def params(mib=56):
    return pltpu.CompilerParams(vmem_limit_bytes=mib * MIB)


def held_index(slots, wanted, row, holder, rank, per_store):
    index = jnp.int32(0)
    count = jnp.int32(0)
    for entry in range(wanted.shape[1]):
        local = slots[wanted[row, entry]] - holder * per_store
        held = jnp.logical_and(local >= 0, local < per_store)
        index = jnp.where(jnp.logical_and(held, count == rank), local, index)
        count = count + held.astype(jnp.int32)
    return index


def fetch_slabs(n_store, slots, wanted, source, held, sems):
    store, group = lax.axis_index("store"), lax.axis_index("group")
    per_store = source.shape[0]
    fetches = []
    for step in range(1, n_store):
        index = held_index(slots, wanted, lax.rem(store + step, n_store), store, group, per_store)
        fetch = pltpu.make_async_copy(source.at[index], held.at[step - 1], sems.at[step - 1])
        fetch.start()
        fetches.append(fetch)
    return fetches


def pass_slabs(fetches, held, outs, sems):
    copies = []
    for number, fetch in enumerate(fetches):
        fetch.wait()
        copy = pltpu.make_async_copy(held.at[number], outs[number], sems.at[number])
        copy.start()
        copies.append(copy)
    return copies


def pick_kernel(n_store, slots, wanted, source, *refs):
    outs, (info, held, in_sem, out_sem) = refs[: n_store - 1], refs[n_store - 1 :]
    store, group = lax.axis_index("store"), lax.axis_index("group")
    per_store = source.shape[0]
    fetches = fetch_slabs(n_store, slots, wanted, source, held, in_sem)
    for rank in range(CAP):
        info[rank] = held_index(slots, wanted, store, store, rank, per_store)
    used = wanted.shape[1]
    holders = [lax.div(slots[wanted[store, entry]], per_store) for entry in range(used)]
    for entry in range(used):
        rank = jnp.int32(0)
        for earlier in range(entry):
            rank = rank + (holders[earlier] == holders[entry]).astype(jnp.int32)
        step = lax.rem(store - holders[entry] + n_store, n_store)
        swapped = jnp.where(step == 0, rank, (rank != group).astype(jnp.int32))
        info[CAP + entry] = step * CAP + swapped
    for copy in pass_slabs(fetches, held, outs, out_sem):
        copy.wait()


def pick(slots, wanted, source):
    count = wanted.shape[0] - 1
    slab = jax.ShapeDtypeStruct(source.shape[1:], source.dtype)
    return pl.pallas_call(
        functools.partial(pick_kernel, count + 1),
        out_shape=[slab] * count + [jax.ShapeDtypeStruct((CAP + wanted.shape[1],), jnp.int32)],
        in_specs=[SMEM, SMEM, HBM],
        out_specs=[ANY] * count + [SMEM],
        scratch_shapes=[
            pltpu.VMEM((count,) + source.shape[1:], source.dtype),
            pltpu.SemaphoreType.DMA((count,)),
            pltpu.SemaphoreType.DMA((count,)),
        ],
        compiler_params=params(8),
        cost_estimate=SMALL,
        name="pick",
    )(slots, wanted, source)


def tie_kernel(*refs):
    pass


def tie(value, *earlier):
    return pl.pallas_call(
        tie_kernel,
        out_shape=jax.ShapeDtypeStruct(value.shape, value.dtype),
        in_specs=[ANY] * (1 + len(earlier)),
        out_specs=ANY,
        input_output_aliases={0: 0},
        compiler_params=params(2),
        cost_estimate=SMALL,
        name="tie",
    )(value, *earlier)


def attend_rows(first, count, lengths, q, k, v, out, slot_count, length, offset, row):
    heads = q.shape[1] // 128
    per_slot = heads // slot_count
    span = ROWS * slot_count * length
    scale = 1.0 / math.sqrt(128)
    finished = []
    for here in range(first, first + count, ROWS):
        limit = jnp.zeros((ROWS, span), jnp.int32)
        for r in range(ROWS):
            limit = jnp.where(row == r, lengths[here + r], limit)
        visible = jnp.logical_and(offset >= 0, offset < limit[None, None])
        rows = q[pl.ds(here // 16 * 16, 16), :].astype(jnp.float32)
        rows = rows[here % 16 : here % 16 + ROWS]
        stacked = jnp.concatenate(
            [rows[:, h * 128 : (h + 1) * 128] for h in range(heads)], axis=0
        ).astype(jnp.bfloat16)
        keys = k[pl.ds(here // ROWS * span, span), :]
        values = v[pl.ds(here // ROWS * span, span), :]
        scores = lax.dot_general(
            stacked, keys, (((1,), (1,)), ((), ())), preferred_element_type=jnp.float32
        ).reshape(slot_count, per_slot, ROWS, span)
        scores = jnp.where(visible, scores, MASKED)
        top = jnp.max(scores, axis=-1, keepdims=True)
        weights = jnp.exp((scores - top) * scale).reshape(heads * ROWS, span).astype(jnp.bfloat16)
        both = jnp.concatenate([values, jnp.ones_like(values)], axis=1)
        summed = jnp.dot(weights, both, preferred_element_type=jnp.float32)
        mean = summed[:, :128] / summed[:, 128:]
        finished.append(
            jnp.concatenate([mean[h * ROWS : (h + 1) * ROWS] for h in range(heads)], axis=1)
        )
        if len(finished) == 2:
            out[pl.ds(here - ROWS, 16), :] = jnp.concatenate(finished, axis=0).astype(out.dtype)
            finished = []


def weight_columns(step, n_chip, width, tile, weight, held, sems):
    tensor = lax.axis_index("tensor")
    chip = lax.rem(lax.div(tensor, 2) + step, n_chip)
    core = lax.rem(tensor, 2)
    fetches = []
    for number in range(2 * width // tile):
        block = chip * 2 + (1 - core if number * tile < width else core)
        start = pl.multiple_of(block * width + number * tile % width, tile)
        fetch = pltpu.make_async_copy(
            weight.at[:, pl.ds(start, tile)], held.at[number], sems.at[number]
        )
        fetch.start()
        fetches.append(fetch)
    return fetches


def project_rows(x, fetches, held, made, outs, sems):
    width, tile = made.shape[2], held.shape[2]
    steps = width // tile
    copies = []
    for block, pieces in enumerate(outs):
        for step in range(steps):
            fetches[block * steps + step].wait()
            total = jnp.dot(x[...], held[block * steps + step], preferred_element_type=jnp.float32)
            made[block, :, step * tile : (step + 1) * tile] = total.astype(made.dtype)
        size = made.shape[1] // len(pieces)
        for number, out in enumerate(pieces):
            copy = pltpu.make_async_copy(
                made.at[block, pl.ds(number * size, size)], out, sems.at[len(copies)]
            )
            copy.start()
            copies.append(copy)
    return copies


def front_kernel(n_store, n_chip, slot_count, length, chunk, slots, wanted, lengths, q_in, k_in, v_in, w_in, up_in, *refs):
    count = n_store - 1
    refs = refs[-(15 + count) :]
    refs[0][...] = jnp.zeros(refs[0].shape, refs[0].dtype)
    refs = refs[1:]
    attended, other, own = refs[:3]
    up_outs, refs = refs[3 : 3 + count], refs[3 + count :]
    qkv_sem, w_sem, up_sem, out_sem = refs[-4:]
    q, k, v, w, up = refs[:5]
    x, made = refs[5:7]
    rows, width = q.shape[0], made.shape[2]
    per_row = slot_count * length
    arrivals = []
    for part in range(rows // chunk):
        here = []
        for number, (source, held, size) in enumerate(
            ((q_in, q, chunk), (k_in, k, chunk * per_row), (v_in, v, chunk * per_row))
        ):
            span = pl.ds(part * size, size)
            fetch = pltpu.make_async_copy(source.at[span], held.at[span], qkv_sem.at[part, number])
            fetch.start()
            here.append(fetch)
        arrivals.append(here)
    columns = weight_columns(1, n_chip, width, w.shape[2], w_in, w, w_sem)
    slabs = fetch_slabs(n_store, slots, wanted, up_in, up, up_sem.at[0])
    span = ROWS * per_row
    shape = (slot_count, 1, ROWS, span)
    offset = (
        lax.broadcasted_iota(jnp.int32, shape, 3)
        - lax.broadcasted_iota(jnp.int32, shape, 2) * per_row
        - lax.broadcasted_iota(jnp.int32, shape, 0) * length
    )
    row = lax.broadcasted_iota(jnp.int32, (ROWS, span), 0)
    for part in range(rows // chunk):
        for fetch in arrivals[part]:
            fetch.wait()
        attend_rows(part * chunk, chunk, lengths, q, k, v, x, slot_count, length, offset, row)
    copies = [pltpu.make_async_copy(x, attended, out_sem.at[2])]
    copies[0].start()
    copies += pass_slabs(slabs, up, up_outs, up_sem.at[1])
    copies += project_rows(x, columns, w, made, ((other,), (own,)), out_sem)
    for copy in copies:
        copy.wait()


def front(n_chip, slots, wanted, lengths, queries, keys, values, weight, up, *earlier):
    rows, slot_count, length, head = keys.shape
    depth = queries.shape[1]
    count = wanted.shape[0] - 1
    width = up.shape[2]
    tile = min(512, width)
    tiles = 2 * width // tile
    chunk = min(64, rows)
    slab = jax.ShapeDtypeStruct(up.shape[1:], up.dtype)
    half = jax.ShapeDtypeStruct((rows, width), jnp.bfloat16)
    return pl.pallas_call(
        functools.partial(front_kernel, count + 1, n_chip, slot_count, length, chunk),
        out_shape=[jax.ShapeDtypeStruct((8, 128), jnp.float32)]
        + [jax.ShapeDtypeStruct((rows, depth), jnp.bfloat16), half, half]
        + [slab] * count,
        in_specs=[SMEM] * 3 + [HBM] * 5 + [SMEM] * len(earlier),
        out_specs=[VMEM] + [ANY] * (3 + count),
        scratch_shapes=[
            pltpu.VMEM((rows, depth), queries.dtype),
            pltpu.VMEM((rows * slot_count * length, head), keys.dtype),
            pltpu.VMEM((rows * slot_count * length, head), values.dtype),
            pltpu.VMEM((tiles, depth, tile), weight.dtype),
            pltpu.VMEM((count,) + up.shape[1:], up.dtype),
            pltpu.VMEM((rows, depth), jnp.bfloat16),
            pltpu.VMEM((2, rows, width), jnp.bfloat16),
            pltpu.SemaphoreType.DMA((rows // chunk, 3)),
            pltpu.SemaphoreType.DMA((tiles,)),
            pltpu.SemaphoreType.DMA((2, count)),
            pltpu.SemaphoreType.DMA((3,)),
        ],
        compiler_params=params(44),
        cost_estimate=SMALL,
        name="front",
    )(
        slots,
        wanted,
        lengths,
        queries,
        keys.reshape(-1, head),
        values.reshape(-1, head),
        weight,
        up,
        *earlier,
    )


def project_kernel(step, n_chip, pieces, x, w_in, *refs):
    refs = refs[-(5 + pieces) :]
    others, (own, w, made, w_sem, out_sem) = refs[:pieces], refs[pieces:]
    columns = weight_columns(step, n_chip, made.shape[2], w.shape[2], w_in, w, w_sem)
    for copy in project_rows(x, columns, w, made, (others, (own,)), out_sem):
        copy.wait()


def project(step, n_chip, pieces, attended, weight, width, *earlier):
    rows, depth = attended.shape
    tile = min(512, width)
    tiles = 2 * width // tile
    half = jax.ShapeDtypeStruct((rows, width), jnp.bfloat16)
    piece = jax.ShapeDtypeStruct((rows // pieces, width), jnp.bfloat16)
    return pl.pallas_call(
        functools.partial(project_kernel, step, n_chip, pieces),
        out_shape=[piece] * pieces + [half],
        in_specs=[VMEM, HBM] + [ANY] * len(earlier),
        out_specs=[ANY] * (pieces + 1),
        scratch_shapes=[
            pltpu.VMEM((tiles, depth, tile), weight.dtype),
            pltpu.VMEM((2, rows, width), jnp.bfloat16),
            pltpu.SemaphoreType.DMA((tiles,)),
            pltpu.SemaphoreType.DMA((pieces + 1,)),
        ],
        compiler_params=params(32),
        cost_estimate=SMALL,
        name="project",
    )(attended, weight, *earlier)


def place_row(info, entries):
    place = jnp.zeros(entries.shape, jnp.int32)
    for entry in range(info.shape[0] - CAP):
        place = jnp.where(entries == entry, info[CAP + entry], place)
    return place


def shrink_kernel(count, info, entries_ref, x_ref, near_ref, *refs):
    slab_refs, (o_ref, near, sem) = refs[:count], refs[-3:]
    fetches = []
    for rank in range(CAP):
        fetch = pltpu.make_async_copy(near_ref.at[info[rank]], near.at[rank], sem.at[rank])
        fetch.start()
        fetches.append(fetch)
    place = place_row(info, entries_ref[...])
    for fetch in fetches:
        fetch.wait()
    slabs = jnp.concatenate(
        [near[rank] for rank in range(CAP)] + [ref[...] for ref in slab_refs], axis=0
    )
    products = lax.dot_general(
        slabs, x_ref[...], (((1,), (1,)), ((), ())), preferred_element_type=jnp.float32
    )
    size = o_ref.shape[0]
    total = jnp.zeros(o_ref.shape, jnp.float32)
    for slot in range(slabs.shape[0] // size):
        total = total + jnp.where(place == slot, products[slot * size : (slot + 1) * size], 0.0)
    o_ref[...] = total


def shrink_part(info, entries, attended, near, slabs, *earlier):
    rows = attended.shape[0]
    _, size, width = near.shape
    return pl.pallas_call(
        functools.partial(shrink_kernel, len(slabs)),
        out_shape=jax.ShapeDtypeStruct((size, rows), jnp.float32),
        in_specs=[SMEM, VMEM, VMEM, HBM] + [VMEM] * len(slabs) + [ANY] * len(earlier),
        out_specs=VMEM,
        scratch_shapes=[
            pltpu.VMEM((CAP, size, width), near.dtype),
            pltpu.SemaphoreType.DMA((CAP,)),
        ],
        compiler_params=params(24),
        cost_estimate=SMALL,
        name="shrink",
    )(info, entries, attended, near, *slabs, *earlier)


def spread_kernel(slot_total, info, entries_ref, parts_ref, o_ref):
    place = place_row(info, entries_ref[...])
    low = jnp.sum(parts_ref[...], axis=0).astype(jnp.bfloat16).astype(jnp.float32)
    wide = jnp.concatenate(
        [jnp.where(place == slot, low, 0.0) for slot in range(slot_total)], axis=0
    )
    o_ref[...] = wide.T.astype(jnp.bfloat16)


def spread(info, entries, parts, slot_total):
    _, size, rows = parts.shape
    return pl.pallas_call(
        functools.partial(spread_kernel, slot_total),
        out_shape=jax.ShapeDtypeStruct((rows, slot_total * size), jnp.bfloat16),
        in_specs=[SMEM, VMEM, VMEM],
        out_specs=VMEM,
        compiler_params=params(12),
        cost_estimate=SMALL,
        name="spread",
    )(info, entries, parts)


def expand_kernel(count, part_count, info, wide_ref, near_ref, *refs):
    slab_refs, parts = refs[:count], refs[count : count + sum(part_count)]
    o_ref, near, sem = refs[-3:]
    fetches = []
    for rank in range(CAP):
        fetch = pltpu.make_async_copy(near_ref.at[info[rank]], near.at[rank], sem.at[rank])
        fetch.start()
        fetches.append(fetch)
    for fetch in fetches:
        fetch.wait()
    slabs = jnp.concatenate(
        [near[rank] for rank in range(CAP)] + [ref[...] for ref in slab_refs], axis=0
    )
    total = jnp.dot(wide_ref[...], slabs, preferred_element_type=jnp.float32)
    rest = iter(parts)
    for pieces in part_count:
        part = jnp.concatenate([next(rest)[...] for _ in range(pieces)], axis=0)
        total = total + part.astype(jnp.float32)
    o_ref[...] = total.astype(o_ref.dtype)


def expand(info, wide, near, slabs, parts):
    rows, width = parts[0][0].shape
    counts = [len(pieces) for pieces in parts]
    flat = [piece for pieces in parts for piece in pieces]
    return pl.pallas_call(
        functools.partial(expand_kernel, len(slabs), counts),
        out_shape=jax.ShapeDtypeStruct((rows, width), jnp.bfloat16),
        in_specs=[SMEM, VMEM, HBM] + [VMEM] * (len(slabs) + len(flat)),
        out_specs=VMEM,
        scratch_shapes=[
            pltpu.VMEM((CAP,) + near.shape[1:], near.dtype),
            pltpu.SemaphoreType.DMA((CAP,)),
        ],
        compiler_params=params(24),
        cost_estimate=SMALL,
        name="expand",
    )(info, wide, near, *slabs, *flat)


def shards(
    mesh,
    queries,
    cached_key_slabs,
    cached_value_slabs,
    request_cache_lengths,
    output_projection_weight,
    adapter_shrink_weight,
    adapter_expand_weight,
    adapter_storage_slot,
    wanted,
    request_wanted_entry,
):
    n_store, n_tensor = mesh.shape["store"], mesh.shape["tensor"]
    n_chip = n_tensor // 2
    local_width = adapter_shrink_weight.shape[2]
    far_steps = range(1, n_chip)

    def along_store(x, step):
        return lax.ppermute(x, "store", [(s, (s + step) % n_store) for s in range(n_store)])

    def swap_group(x):
        return lax.ppermute(x, "group", [(0, 1), (1, 0)])

    def swap_core(x):
        return lax.ppermute(x, "tensor", [(t, t ^ 1) for t in range(n_tensor)])

    def along_chip(x, step):
        return lax.ppermute(x, "tensor", [(t, (t + 2 * step) % n_tensor) for t in range(n_tensor)])

    slots = adapter_storage_slot
    *send_down, info = pick(slots, wanted, adapter_shrink_weight)
    got_down = [along_store(x, step + 1) for step, x in enumerate(send_down)]
    token, attended, other, own, *send_up = front(
        n_chip,
        slots,
        wanted,
        request_cache_lengths,
        queries,
        cached_key_slabs,
        cached_value_slabs,
        output_projection_weight,
        adapter_expand_weight,
        info,
    )
    got_down = [tie(x, token) for x in got_down[:2]] + got_down[2:]
    other = tie(other, *got_down[:2])

    def meet(mine, given):
        return (mine.astype(jnp.float32) + given.astype(jnp.float32)).astype(jnp.bfloat16)

    arrived = []
    for step in far_steps:
        if step > 1:
            other, own = project(step, n_chip, 1, attended, output_projection_weight, local_width, met)
        met = meet(own, swap_core(other))
        arrived.append([along_chip(met, step)])
    got_up = [along_store(tie(x, met), step + 1) for step, x in enumerate(send_up)]
    got_down = got_down[:2] + [tie(x, met) for x in got_down[2:]]
    *others, own = project(0, n_chip, 2, attended, output_projection_weight, local_width, met)
    near = [swap_core(x) for x in others]

    down = []
    for x in got_down:
        down += [x, swap_group(x)]
    part = shrink_part(info, request_wanted_entry, attended, adapter_shrink_weight, down, own)
    wide = spread(
        info, request_wanted_entry, lax.all_gather(part, "tensor"), n_store * CAP
    )
    up = []
    for x, earlier in zip(got_up, [own, part, wide] + [wide] * n_store):
        x = tie(x, earlier)
        up += [x, swap_group(x)]
    return expand(info, wide, adapter_expand_weight, up, [[own], near] + arrived)


def solution(mesh):
    placed = (
        P(("group", "store"), "tensor"),
        P(("group", "store"), "tensor", None, None),
        P(("group", "store"), "tensor", None, None),
        P(("group", "store")),
        P("tensor", None),
        P("store", None, "tensor"),
        P("store", None, "tensor"),
        P(),
        P(),
        P(("group", "store"), None),
    )
    return jax.shard_map(
        functools.partial(shards, mesh),
        mesh=mesh,
        in_specs=placed,
        out_specs=P(("group", "store"), "tensor"),
        check_vma=False,
    )
```

time: 180 us -> 82.5 us (0.46)
  blocking collectives: 65.4 us -> 7.3 us
  matrix products: 31.6 us -> 0 us
  Pallas kernels: 0 us -> 28 us
  waiting for transfers between devices: 42.3 us -> 20.4 us
  starting transfers between devices: 3.74 us -> 19.7 us
  between operations: 13.5 us -> 0.35 us
  local copies, waits for them, and re-layouts: 17.9 us -> 6.06 us
  other arithmetic: 4.84 us -> 0.38 us
    all_to_all x1 -> x0, blocking collectives: 54.4 us -> none  [shards(): lax.all_to_all(send_up, 'store', split_axis=0, concat_axis=0, tiled=True)]
    all_to_all x1 -> x0, waiting for transfers between devices: 42.3 us -> none  [shards(): lax.all_to_all(send_down, 'store', split_axis=0, concat_axis=0, tiled=True)]
    pallas_call x0 -> x16, Pallas kernels: none -> 28 us  [the longest x1 14.1 us: front(): pl.pallas_call(functools.partial(front_kernel, count + 1, n_chip, slot_co...]
    dot_general x4 -> x0, matrix products: 26 us -> none  [the longest x1 17 us: shards(): jnp.dot(attended, output_projection_weight, preferred_element_type=jnp.fl...]
    ppermute x0 -> x16, waiting for transfers between devices: none -> 20.4 us  [the longest x6 16.6 us: swap_group(): return lax.ppermute(x, 'group', [(0, 1), (1, 0)])]
    ppermute x0 -> x16, starting transfers between devices: none -> 19.7 us  [the longest x6 12.7 us: along_store(): lax.ppermute(x, 'store', [(s, (s + step) % n_store) for s in range(n_stor...]
    gather x6 -> x0, local copies, waits for them, and re-layouts: 12.3 us -> none  [the longest x1 3.61 us: shards(): send_up = jnp.take(adapter_expand_weight, send_index, axis=0)]
    psum x1 -> x0, blocking collectives: 11 us -> none  [shards(): shrink = lax.psum(shrink_part, 'tensor')]
  transfers between devices with their start and end apart: 2 -> 16, of which waited for: 1 -> 5; matrix products, arithmetic and copies ran while one was open for 11% -> 0% of each run, Pallas kernels for 0% -> 29%
where the time goes in v1:
time: 82.5 us; the launch traced here: 82.3 us
  Pallas kernels  28 us (34%)
  waiting for transfers between devices  20.4 us (25%)
  starting transfers between devices  19.7 us (24%)
  blocking collectives  7.3 us (9%)
  local copies, waits for them, and re-layouts  6.06 us (7%)
    ppermute x6, waiting for transfers between devices, swap_group(): return lax.ppermute(x, 'group', [(0, 1), (1, 0)])  16.6 us
    pallas_call x1, Pallas kernels, front(): pl.pallas_call(functools.partial(front_kernel, count + 1, n_chip, slot_co...  14.1 us
    ppermute x6, starting transfers between devices, along_store(): lax.ppermute(x, 'store', [(s, (s + step) % n_store) for s in range(n_stor...  12.7 us
    pallas_call x1, Pallas kernels, project(): pl.pallas_call(functools.partial(project_kernel, step, n_chip, pieces), o...  7.79 us
    all_gather x1, blocking collectives, shards(): lax.all_gather(part, 'tensor')  7.3 us
    unnamed x22, local copies, waits for them, and re-layouts  6.06 us
    ppermute x6, starting transfers between devices, swap_group(): return lax.ppermute(x, 'group', [(0, 1), (1, 0)])  5.37 us
    ppermute x6, waiting for transfers between devices, along_store(): lax.ppermute(x, 'store', [(s, (s + step) % n_store) for s in range(n_stor...  3.82 us
  transfers between devices with their start and end apart: 16, of which 5 were waited for; matrix products, arithmetic and copies ran while one was open for 0% of the time, Pallas kernels for 29%

profile of v1, /device:TPU:0, one launch (start us, length us, event | category | flops | bytes accessed | tf_op | source)
XLA Modules:
  0.0 82.3 jit_solution(7175534334212964064)
XLA Ops:
  0.0 1.6 %copy-done = bf16[8,64,2048]{2,1,0:T(8,128)(2,1)S(1)} copy-done((bf16[8,64,2048]{2,1,0:T(8,128)(2,1)S(1)}, bf16[8,64,2048]{2,1,0:T(8,128)(2,1)}, u32[]{:S(2)}) %copy-start) | copy-done | bytes 2097176
  1.6 0.7 copy-done.5
  2.3 0.7 copy-done.8
  2.9 1.6 %pick.1 = (bf16[64,2048]{1,0:T(8,128)(2,1)S(1)}, bf16[64,2048]{1,0:T(8,128)(2,1)S(1)}, bf16[64,2048]{1,0:T(8,128)(2,1)S(1)}, s32[10]{0:T(128)S(1)}) custom-call(s32[32]{0:T(128)S(1)} %copy-done.8, s32[4,8]{1,0:T(4,128)S(1)} %copy-done.5, bf16[8,64,2048]{2,1,0:T(8,128)(2,1)S(1)} %copy-done), custom_call_target="tpu_custom_call" | custom-call | flops 1 | bytes 1 | tf_op jit(solution)/shard_map/pick/pallas_call | solution.py:84
  4.5 4.1 %collective-permute-start.2 = (bf16[64,2048]{1,0:T(8,128)(2,1)S(1)}, bf16[64,2048]{1,0:T(8,128)(2,1)S(1)}, u32[]{:S(2)}, u32[]{:S(2)}) collective-permute-start(bf16[64,2048]{1,0:T(8,128)(2,1)S(1)} %get-tuple-element.23), channel_id=1, source_target_pairs={{0,8},{4,12},{8,0},{12,4},{1,9},{5,13},{9,1},{13,5},{2,10},{6,14},... | collective-permute-start | bytes 786440 | tf_op jit(solution)/shard_map/ppermute | solution.py:438
  8.6 1.6 %collective-permute-start = (bf16[64,2048]{1,0:T(8,128)(2,1)S(1)}, bf16[64,2048]{1,0:T(8,128)(2,1)S(1)}, u32[]{:S(2)}, u32[]{:S(2)}) collective-permute-start(bf16[64,2048]{1,0:T(8,128)(2,1)S(1)} %get-tuple-element.21), channel_id=1, source_target_pairs={{0,4},{4,8},{8,12},{12,0},{1,5},{5,9},{9,13},{13,1},{2,6},{6,10},{... | collective-permute-start | bytes 786440 | tf_op jit(solution)/shard_map/ppermute | solution.py:438
  10.2 0.0 copy-done.6
  10.2 0.0 copy-start.3
  10.2 1.9 %copy-done.3 = bf16[256,2,24,128]{3,2,1,0:T(8,128)(2,1)S(1)} copy-done((bf16[256,2,24,128]{3,2,1,0:T(8,128)(2,1)S(1)}, bf16[256,2,24,128]{3,2,1,0:T(8,128)(2,1)}, u32[]{:S(2)}) %copy-start.3) | copy-done | bytes 3145752
  12.1 1.2 %copy-done.4 = bf16[256,2048]{1,0:T(8,128)(2,1)S(1)} copy-done((bf16[256,2048]{1,0:T(8,128)(2,1)S(1)}, bf16[256,2048]{1,0:T(8,128)(2,1)}, u32[]{:S(2)}) %copy-start.4) | copy-done | bytes 1048600
  13.3 14.1 %front.1 = (f32[8,128]{1,0:T(8,128)S(1)}, bf16[256,2048]{1,0:T(8,128)(2,1)S(1)}, bf16[256,2048]{1,0:T(8,128)(2,1)S(1)}, bf16[256,2048]{1,0:T(8,128)(2,1)S(1)}, b...) custom-call(s32[32]{0:T(128)S(1)} %copy-done.9, s32[4,8]{1,0:T(4,128)S(1)} %copy-done.6, ...), custom_call_target="tpu_custom_call" | custom-call | flops 1 | bytes 1 | tf_op jit(solution)/shard_map/front/pallas_call | solution.py:242
  27.5 0.0 collective-permute-done.2.refs_0_
  27.5 0.0 collective-permute-done.refs_0_
  27.5 0.1 collective-permute-start.5
  27.6 2.3 %collective-permute-start.4 = (bf16[64,2048]{1,0:T(8,128)(2,1)S(1)}, bf16[64,2048]{1,0:T(8,128)(2,1)S(1)}, u32[]{:S(2)}, u32[]{:S(2)}) collective-permute-start(bf16[64,2048]{1,0:T(8,128)(2,1)S(1)} %get-tuple-element.24), channel_id=1, source_target_pairs={{0,12},{4,0},{8,4},{12,8},{1,13},{5,1},{9,5},{13,9},{2,14},{6,2},{... | collective-permute-start | bytes 786440 | tf_op jit(solution)/shard_map/ppermute | solution.py:438
  29.9 1.5 %collective-permute-start.3 = (bf16[64,2048]{1,0:T(8,128)(2,1)S(1)}, bf16[64,2048]{1,0:T(8,128)(2,1)S(1)}, u32[]{:S(2)}, u32[]{:S(2)}) collective-permute-start(bf16[64,2048]{1,0:T(8,128)(2,1)S(1)} %tie.11.refs_2_), channel_id=1, source_target_pairs={{0,16},{16,0},{1,17},{17,1},{2,18},{18,2},{3,19},{19,3},{4,20},{20... | collective-permute-start | bytes 786440 | tf_op jit(solution)/shard_map/ppermute | solution.py:441
  31.4 0.0 collective-permute-done.5
  31.4 0.4 add_convert_fusion.refs_1_.refs_0_
  31.8 1.6 %collective-permute-start.15 = (bf16[256,2048]{1,0:T(8,128)(2,1)S(1)}, bf16[256,2048]{1,0:T(8,128)(2,1)S(1)}, u32[]{:S(2)}, u32[]{:S(2)}) collective-permute-start(bf16[256,2048]{1,0:T(8,128)(2,1)S(1)} %add_convert_fusion.refs_1_.refs_0_), channel_id=1, source_target_pairs={{0,2},{1,3},{2,0},{3,1},{4,6},{5,7},{6,4},{7,5},{8,10},{9,11},{10,... | collective-permute-start | bytes 3145736 | tf_op jit(solution)/shard_map/ppermute | solution.py:447
  33.4 0.5 collective-permute-start.1
  33.9 2.4 %collective-permute-done.4.refs_0_ = bf16[64,2048]{1,0:T(8,128)(2,1)S(1)} collective-permute-done((bf16[64,2048]{1,0:T(8,128)(2,1)S(1)}, bf16[64,2048]{1,0:T(8,128)(2,1)S(1)}, u32[]{:S(2)}, u32[]{:S(2)}) %collective-permute-start.4) | collective-permute-done | bytes 262176 | tf_op jit(solution)/shard_map/ppermute | solution.py:438
  36.3 1.5 %collective-permute-start.6 = (bf16[64,2048]{1,0:T(8,128)(2,1)S(1)}, bf16[64,2048]{1,0:T(8,128)(2,1)S(1)}, u32[]{:S(2)}, u32[]{:S(2)}) collective-permute-start(bf16[64,2048]{1,0:T(8,128)(2,1)S(1)} %tie.13.refs_4_), channel_id=1, source_target_pairs={{0,16},{16,0},{1,17},{17,1},{2,18},{18,2},{3,19},{19,3},{4,20},{20... | collective-permute-start | bytes 786440 | tf_op jit(solution)/shard_map/ppermute | solution.py:441
  37.8 4.0 %collective-permute-start.11 = (bf16[64,2048]{1,0:T(8,128)(2,1)S(1)}, bf16[64,2048]{1,0:T(8,128)(2,1)S(1)}, u32[]{:S(2)}, u32[]{:S(2)}) collective-permute-start(bf16[64,2048]{1,0:T(8,128)(2,1)S(1)} %tie.18), channel_id=1, source_target_pairs={{0,12},{4,0},{8,4},{12,8},{1,13},{5,1},{9,5},{13,9},{2,14},{6,2},{... | collective-permute-start | bytes 786440 | tf_op jit(solution)/shard_map/ppermute | solution.py:438
  41.8 0.0 collective-permute-done.3.refs_3_
  41.8 0.0 collective-permute-start.9
  41.9 0.0 copy-start.7
  41.9 7.8 %project.1 = (bf16[128,2048]{1,0:T(8,128)(2,1)S(1)}, bf16[128,2048]{1,0:T(8,128)(2,1)S(1)}, bf16[256,2048]{1,0:T(8,128)(2,1)S(1)}) custom-call(bf16[256,2048]{1,0:T(8,128)(2,1)S(1)} %get-tuple-element.20.x.x_ref, bf16[2048,8192]{1,0:T(8,128)(2,1)} %w_in.3, bf16[256,2048]{1,0:T(8,128)(2,1)S(1)} %add_convert_fusion.refs_1_.refs_0_), custom_call_target="tpu_custom_call" | custom-call | flops 1 | bytes 1 | tf_op jit(solution)/shard_map/project/pallas_call | solution.py:292
  49.7 0.0 collective-permute-done.1.refs_1_
  49.7 0.7 collective-permute-start.7
  50.3 0.0 collective-permute-done.6.refs_5_
  50.4 0.0 collective-permute-start.13
  50.4 1.4 %shrink.1.refs_1_ = f32[64,256]{1,0:T(8,128)S(1)} custom-call(s32[10]{0:T(128)S(1)} %get-tuple-element.19.refs_0_.info, s32[1,256]{1,0:T(1,128)S(1)} %copy-done.7, bf16[256,2048]{1,0:T(8,128)(2,1)S(1)} %get-tuple-element.20.x.x_ref, bf16[8,64,2048]{2,1,0:T(8,128)(2,1)S(1)} %copy-done.1, bf16[64,2048]{1,0:T(8,128)(2,1)S(1)} %tie.10.refs_1_.refs_0_, ...), custom_call_target="tpu_custom_call" | custom-call | flops 1 | bytes 1 | tf_op jit(solution)/shard_map/shrink/pallas_call | solution.py:342
  51.7 7.3 %all-gather = f32[256,256]{1,0:T(8,128)S(1)} all-gather(f32[64,256]{1,0:T(8,128)S(1)} %shrink.1.refs_1_), channel_id=2, replica_groups=mesh['group'=2,'store'=4,'tensor'=4] {'tensor'}, dimensions={0}, use_global_device_ids=true | all-gather | bytes 327680 | tf_op jit(solution)/shard_map/all_gather | solution.py:486
  59.0 0.7 spread.1.refs_1_.wide_ref
  59.7 0.0 collective-permute-done.11.refs_0_
  59.7 0.7 collective-permute-start.12
  60.4 1.4 %collective-permute-done.9.refs_0_ = bf16[64,2048]{1,0:T(8,128)(2,1)S(1)} collective-permute-done((bf16[64,2048]{1,0:T(8,128)(2,1)S(1)}, bf16[64,2048]{1,0:T(8,128)(2,1)S(1)}, u32[]{:S(2)}, u32[]{:S(2)}) %collective-permute-start.9) | collective-permute-done | bytes 262176 | tf_op jit(solution)/shard_map/ppermute | solution.py:438
  61.8 0.0 collective-permute-start.14
  61.8 0.0 collective-permute-done.7.refs_0_
  61.8 0.6 collective-permute-start.10
  62.4 6.5 %collective-permute-done.12.refs_5_ = bf16[64,2048]{1,0:T(8,128)(2,1)S(1)} collective-permute-done((bf16[64,2048]{1,0:T(8,128)(2,1)S(1)}, bf16[64,2048]{1,0:T(8,128)(2,1)S(1)}, u32[]{:S(2)}, u32[]{:S(2)}) %collective-permute-start.12) | collective-permute-done | bytes 262176 | tf_op jit(solution)/shard_map/ppermute | solution.py:441
  68.9 0.6 collective-permute-start.8
  69.5 5.0 %collective-permute-done.10.refs_3_ = bf16[64,2048]{1,0:T(8,128)(2,1)S(1)} collective-permute-done((bf16[64,2048]{1,0:T(8,128)(2,1)S(1)}, bf16[64,2048]{1,0:T(8,128)(2,1)S(1)}, u32[]{:S(2)}, u32[]{:S(2)}) %collective-permute-start.10) | collective-permute-done | bytes 262176 | tf_op jit(solution)/shard_map/ppermute | solution.py:441
  74.6 5.1 %collective-permute-done.8.refs_1_ = bf16[64,2048]{1,0:T(8,128)(2,1)S(1)} collective-permute-done((bf16[64,2048]{1,0:T(8,128)(2,1)S(1)}, bf16[64,2048]{1,0:T(8,128)(2,1)S(1)}, u32[]{:S(2)}, u32[]{:S(2)}) %collective-permute-start.8) | collective-permute-done | bytes 262176 | tf_op jit(solution)/shard_map/ppermute | solution.py:441
  79.6 0.0 collective-permute-done.13.refs_7_
  79.6 0.0 collective-permute-done.14.refs_8_
  79.6 0.0 collective-permute-done.15.refs_9_
  79.6 2.5 %expand.1 = bf16[256,2048]{1,0:T(8,128)(2,1)} custom-call(s32[10]{0:T(128)S(1)} %get-tuple-element.19.refs_0_.info, bf16[256,512]{1,0:T(8,128)(2,1)S(1)} %spread.1.refs_1_.wide_ref, bf16[8,64,2048]{2,1,0:T(8,128)(2,1)S(1)} %copy-done.2, bf16[64,2048]{1,0:T(8,128)(2,1)S(1)} %tie.15.refs_0_, bf16[64,2048]{1,0:T(8,128)(2,1)S(1)} %collective-permute-done.8.refs_1_, ...), custom_call_target="tpu_custom_call" | custom-call | flops 1 | bytes 1 | tf_op jit(solution)/shard_map/expand/pallas_call | solution.py:404
  (24 shorter events, 0.0 us)
Async XLA Ops:
  0.0 1.6 %copy-start = (bf16[8,64,2048]{2,1,0:T(8,128)(2,1)S(1)}, bf16[8,64,2048]{2,1,0:T(8,128)(2,1)}, u32[]{:S(2)}) copy-start(bf16[8,64,2048]{2,1,0:T(8,128)(2,1)} %near_ref.2) | copy-start | bytes 6291460
  1.6 0.7 copy-start.5
  2.3 0.7 copy-start.8
  2.9 7.3 %copy-start.2 = (bf16[8,64,2048]{2,1,0:T(8,128)(2,1)S(1)}, bf16[8,64,2048]{2,1,0:T(8,128)(2,1)}, u32[]{:S(2)}) copy-start(bf16[8,64,2048]{2,1,0:T(8,128)(2,1)} %near_ref.3) | copy-start | bytes 6291460
  2.9 7.3 %copy-start.6 = (s32[4,8]{1,0:T(4,128)S(1)}, s32[4,8]{1,0:T(4,128)}, u32[]{:S(2)}) copy-start(s32[4,8]{1,0:T(4,128)} %wanted.3) | copy-start | bytes 388
  2.9 7.3 %copy-start.9 = (s32[32]{0:T(128)S(1)}, s32[32]{0:T(128)}, u32[]{:S(2)}) copy-start(s32[32]{0:T(128)} %slots.3) | copy-start | bytes 388
  2.9 7.3 %copy-start.10 = (s32[256]{0:T(256)S(1)}, s32[256]{0:T(256)}, u32[]{:S(2)}) copy-start(s32[256]{0:T(256)} %lengths.1) | copy-start | bytes 3076
  4.5 22.9 %collective-permute-start.2 = (bf16[64,2048]{1,0:T(8,128)(2,1)S(1)}, bf16[64,2048]{1,0:T(8,128)(2,1)S(1)}, u32[]{:S(2)}, u32[]{:S(2)}) collective-permute-start(bf16[64,2048]{1,0:T(8,128)(2,1)S(1)} %get-tuple-element.23), channel_id=1, source_target_pairs={{0,8},{4,12},{8,0},{12,4},{1,9},{5,13},{9,1},{13,5},{2,10},{6,14},... | collective-permute-start | bytes 786440 | tf_op jit(solution)/shard_map/ppermute | solution.py:438
  8.6 18.8 %collective-permute-start = (bf16[64,2048]{1,0:T(8,128)(2,1)S(1)}, bf16[64,2048]{1,0:T(8,128)(2,1)S(1)}, u32[]{:S(2)}, u32[]{:S(2)}) collective-permute-start(bf16[64,2048]{1,0:T(8,128)(2,1)S(1)} %get-tuple-element.21), channel_id=1, source_target_pairs={{0,4},{4,8},{8,12},{12,0},{1,5},{5,9},{9,13},{13,1},{2,6},{6,10},{... | collective-permute-start | bytes 786440 | tf_op jit(solution)/shard_map/ppermute | solution.py:438
  10.2 1.9 %copy-start.3 = (bf16[256,2,24,128]{3,2,1,0:T(8,128)(2,1)S(1)}, bf16[256,2,24,128]{3,2,1,0:T(8,128)(2,1)}, u32[]{:S(2)}) copy-start(bf16[256,2,24,128]{3,2,1,0:T(8,128)(2,1)} %param.11) | copy-start | bytes 9437188
  12.1 1.2 %copy-start.4 = (bf16[256,2048]{1,0:T(8,128)(2,1)S(1)}, bf16[256,2048]{1,0:T(8,128)(2,1)}, u32[]{:S(2)}) copy-start(bf16[256,2048]{1,0:T(8,128)(2,1)} %q_in.1) | copy-start | bytes 3145732
  27.5 3.9 %collective-permute-start.5 = (bf16[256,2048]{1,0:T(8,128)(2,1)S(1)}, bf16[256,2048]{1,0:T(8,128)(2,1)S(1)}, u32[]{:S(2)}, u32[]{:S(2)}) collective-permute-start(bf16[256,2048]{1,0:T(8,128)(2,1)S(1)} %tie.12), channel_id=1, source_target_pairs={{0,1},{1,0},{2,3},{3,2},{4,5},{5,4},{6,7},{7,6},{8,9},{9,8},{10,11... | collective-permute-start | bytes 3145736 | tf_op jit(solution)/shard_map/ppermute | solution.py:444
  27.6 8.7 %collective-permute-start.4 = (bf16[64,2048]{1,0:T(8,128)(2,1)S(1)}, bf16[64,2048]{1,0:T(8,128)(2,1)S(1)}, u32[]{:S(2)}, u32[]{:S(2)}) collective-permute-start(bf16[64,2048]{1,0:T(8,128)(2,1)S(1)} %get-tuple-element.24), channel_id=1, source_target_pairs={{0,12},{4,0},{8,4},{12,8},{1,13},{5,1},{9,5},{13,9},{2,14},{6,2},{... | collective-permute-start | bytes 786440 | tf_op jit(solution)/shard_map/ppermute | solution.py:438
  29.9 12.0 %collective-permute-start.3 = (bf16[64,2048]{1,0:T(8,128)(2,1)S(1)}, bf16[64,2048]{1,0:T(8,128)(2,1)S(1)}, u32[]{:S(2)}, u32[]{:S(2)}) collective-permute-start(bf16[64,2048]{1,0:T(8,128)(2,1)S(1)} %tie.11.refs_2_), channel_id=1, source_target_pairs={{0,16},{16,0},{1,17},{17,1},{2,18},{18,2},{3,19},{19,3},{4,20},{20... | collective-permute-start | bytes 786440 | tf_op jit(solution)/shard_map/ppermute | solution.py:441
  31.8 47.8 %collective-permute-start.15 = (bf16[256,2048]{1,0:T(8,128)(2,1)S(1)}, bf16[256,2048]{1,0:T(8,128)(2,1)S(1)}, u32[]{:S(2)}, u32[]{:S(2)}) collective-permute-start(bf16[256,2048]{1,0:T(8,128)(2,1)S(1)} %add_convert_fusion.refs_1_.refs_0_), channel_id=1, source_target_pairs={{0,2},{1,3},{2,0},{3,1},{4,6},{5,7},{6,4},{7,5},{8,10},{9,11},{10,... | collective-permute-start | bytes 3145736 | tf_op jit(solution)/shard_map/ppermute | solution.py:447
  33.4 16.3 %collective-permute-start.1 = (bf16[64,2048]{1,0:T(8,128)(2,1)S(1)}, bf16[64,2048]{1,0:T(8,128)(2,1)S(1)}, u32[]{:S(2)}, u32[]{:S(2)}) collective-permute-start(bf16[64,2048]{1,0:T(8,128)(2,1)S(1)} %tie.10.refs_1_.refs_0_), channel_id=1, source_target_pairs={{0,16},{16,0},{1,17},{17,1},{2,18},{18,2},{3,19},{19,3},{4,20},{20... | collective-permute-start | bytes 786440 | tf_op jit(solution)/shard_map/ppermute | solution.py:441
  36.3 14.0 %collective-permute-start.6 = (bf16[64,2048]{1,0:T(8,128)(2,1)S(1)}, bf16[64,2048]{1,0:T(8,128)(2,1)S(1)}, u32[]{:S(2)}, u32[]{:S(2)}) collective-permute-start(bf16[64,2048]{1,0:T(8,128)(2,1)S(1)} %tie.13.refs_4_), channel_id=1, source_target_pairs={{0,16},{16,0},{1,17},{17,1},{2,18},{18,2},{3,19},{19,3},{4,20},{20... | collective-permute-start | bytes 786440 | tf_op jit(solution)/shard_map/ppermute | solution.py:441
  37.8 21.9 %collective-permute-start.11 = (bf16[64,2048]{1,0:T(8,128)(2,1)S(1)}, bf16[64,2048]{1,0:T(8,128)(2,1)S(1)}, u32[]{:S(2)}, u32[]{:S(2)}) collective-permute-start(bf16[64,2048]{1,0:T(8,128)(2,1)S(1)} %tie.18), channel_id=1, source_target_pairs={{0,12},{4,0},{8,4},{12,8},{1,13},{5,1},{9,5},{13,9},{2,14},{6,2},{... | collective-permute-start | bytes 786440 | tf_op jit(solution)/shard_map/ppermute | solution.py:438
  41.8 20.0 %collective-permute-start.9 = (bf16[64,2048]{1,0:T(8,128)(2,1)S(1)}, bf16[64,2048]{1,0:T(8,128)(2,1)S(1)}, u32[]{:S(2)}, u32[]{:S(2)}) collective-permute-start(bf16[64,2048]{1,0:T(8,128)(2,1)S(1)} %tie.16), channel_id=1, source_target_pairs={{0,8},{4,12},{8,0},{12,4},{1,9},{5,13},{9,1},{13,5},{2,10},{6,14},... | collective-permute-start | bytes 786440 | tf_op jit(solution)/shard_map/ppermute | solution.py:438
  41.8 8.5 %copy-start.1 = (bf16[8,64,2048]{2,1,0:T(8,128)(2,1)S(1)}, bf16[8,64,2048]{2,1,0:T(8,128)(2,1)}, u32[]{:S(2)}) copy-start(bf16[8,64,2048]{2,1,0:T(8,128)(2,1)} %near_ref.2) | copy-start | bytes 6291460
  41.9 8.5 %copy-start.7 = (s32[1,256]{1,0:T(1,128)S(1)}, s32[1,256]{1,0:T(1,128)}, u32[]{:S(2)}) copy-start(s32[1,256]{1,0:T(1,128)} %entries_ref.3) | copy-start | bytes 3076
  49.7 12.1 %collective-permute-start.7 = (bf16[64,2048]{1,0:T(8,128)(2,1)S(1)}, bf16[64,2048]{1,0:T(8,128)(2,1)S(1)}, u32[]{:S(2)}, u32[]{:S(2)}) collective-permute-start(bf16[64,2048]{1,0:T(8,128)(2,1)S(1)} %tie.14), channel_id=1, source_target_pairs={{0,4},{4,8},{8,12},{12,0},{1,5},{5,9},{9,13},{13,1},{2,6},{6,10},{... | collective-permute-start | bytes 786440 | tf_op jit(solution)/shard_map/ppermute | solution.py:438
  50.4 29.3 %collective-permute-start.13 = (bf16[128,2048]{1,0:T(8,128)(2,1)S(1)}, bf16[128,2048]{1,0:T(8,128)(2,1)S(1)}, u32[]{:S(2)}, u32[]{:S(2)}) collective-permute-start(bf16[128,2048]{1,0:T(8,128)(2,1)S(1)} %get-tuple-element.31), channel_id=1, source_target_pairs={{0,1},{1,0},{2,3},{3,2},{4,5},{5,4},{6,7},{7,6},{8,9},{9,8},{10,11... | collective-permute-start | bytes 1572872 | tf_op jit(solution)/shard_map/ppermute | solution.py:444
  59.7 9.2 %collective-permute-start.12 = (bf16[64,2048]{1,0:T(8,128)(2,1)S(1)}, bf16[64,2048]{1,0:T(8,128)(2,1)S(1)}, u32[]{:S(2)}, u32[]{:S(2)}) collective-permute-start(bf16[64,2048]{1,0:T(8,128)(2,1)S(1)} %tie.19.refs_4_), channel_id=1, source_target_pairs={{0,16},{16,0},{1,17},{17,1},{2,18},{18,2},{3,19},{19,3},{4,20},{20... | collective-permute-start | bytes 786440 | tf_op jit(solution)/shard_map/ppermute | solution.py:441
  61.8 17.8 %collective-permute-start.14 = (bf16[128,2048]{1,0:T(8,128)(2,1)S(1)}, bf16[128,2048]{1,0:T(8,128)(2,1)S(1)}, u32[]{:S(2)}, u32[]{:S(2)}) collective-permute-start(bf16[128,2048]{1,0:T(8,128)(2,1)S(1)} %get-tuple-element.32), channel_id=1, source_target_pairs={{0,1},{1,0},{2,3},{3,2},{4,5},{5,4},{6,7},{7,6},{8,9},{9,8},{10,11... | collective-permute-start | bytes 1572872 | tf_op jit(solution)/shard_map/ppermute | solution.py:444
  61.8 12.7 %collective-permute-start.10 = (bf16[64,2048]{1,0:T(8,128)(2,1)S(1)}, bf16[64,2048]{1,0:T(8,128)(2,1)S(1)}, u32[]{:S(2)}, u32[]{:S(2)}) collective-permute-start(bf16[64,2048]{1,0:T(8,128)(2,1)S(1)} %tie.17.refs_2_), channel_id=1, source_target_pairs={{0,16},{16,0},{1,17},{17,1},{2,18},{18,2},{3,19},{19,3},{4,20},{20... | collective-permute-start | bytes 786440 | tf_op jit(solution)/shard_map/ppermute | solution.py:441
  68.9 10.7 %collective-permute-start.8 = (bf16[64,2048]{1,0:T(8,128)(2,1)S(1)}, bf16[64,2048]{1,0:T(8,128)(2,1)S(1)}, u32[]{:S(2)}, u32[]{:S(2)}) collective-permute-start(bf16[64,2048]{1,0:T(8,128)(2,1)S(1)} %tie.15.refs_0_), channel_id=1, source_target_pairs={{0,16},{16,0},{1,17},{17,1},{2,18},{18,2},{3,19},{19,3},{4,20},{20... | collective-permute-start | bytes 786440 | tf_op jit(solution)/shard_map/ppermute | solution.py:441

commit v2 on v1

v2 whole, which is shorter than its diff:
```python
import functools
import math

import jax
import jax.numpy as jnp
from jax import lax
from jax.experimental import pallas as pl
from jax.experimental.pallas import tpu as pltpu
from jax.sharding import PartitionSpec as P

CAP = 2
ROWS = 8
MASKED = -1e30
AHEAD = 4
CHUNK = 32
MIB = 1 << 20
ANY = pl.BlockSpec(memory_space=pl.ANY)
HBM = pl.BlockSpec(memory_space=pltpu.HBM)
SMEM = pl.BlockSpec(memory_space=pltpu.SMEM)
VMEM = pl.BlockSpec(memory_space=pltpu.VMEM)


SMALL = pl.CostEstimate(flops=1, bytes_accessed=1, transcendentals=0)


def params(mib=56):
    return pltpu.CompilerParams(vmem_limit_bytes=mib * MIB)


def held_index(slots, wanted, row, holder, rank, per_store):
    index = jnp.int32(0)
    count = jnp.int32(0)
    for entry in range(wanted.shape[1]):
        local = slots[wanted[row, entry]] - holder * per_store
        held = jnp.logical_and(local >= 0, local < per_store)
        index = jnp.where(jnp.logical_and(held, count == rank), local, index)
        count = count + held.astype(jnp.int32)
    return index


def pick_kernel(n_store, slots_in, wanted_in, down, up, *refs):
    targets, (info, slots, wanted, held, table_sem, in_sem, out_sem) = refs[:-7], refs[-7:]
    tables = [
        pltpu.make_async_copy(slots_in, slots, table_sem.at[0]),
        pltpu.make_async_copy(wanted_in, wanted, table_sem.at[1]),
    ]
    for table in tables:
        table.start()
    for table in tables:
        table.wait()
    store, group = lax.axis_index("store"), lax.axis_index("group")
    per_store = down.shape[0]
    indices = [
        held_index(slots, wanted, store ^ step, store, group, per_store)
        for step in range(CAP, n_store)
    ]
    indices += [
        held_index(slots, wanted, store ^ 1, store, rank, per_store) for rank in range(CAP)
    ]
    count = len(indices)
    targets = (
        list(targets[:count])
        + list(targets[count:-1])
        + [targets[-1].at[rank] for rank in range(CAP)]
    )
    fetches = []
    for source in (down, up):
        for index in indices:
            slot = len(fetches)
            fetch = pltpu.make_async_copy(source.at[index], held.at[slot], in_sem.at[slot])
            fetch.start()
            fetches.append(fetch)
    for rank in range(CAP):
        info[rank] = held_index(slots, wanted, store, store, rank, per_store)
    used = wanted.shape[1]
    holders = [lax.div(slots[wanted[store, entry]], per_store) for entry in range(used)]
    for entry in range(used):
        rank = jnp.int32(0)
        for earlier in range(entry):
            rank = rank + (holders[earlier] == holders[entry]).astype(jnp.int32)
        step = store ^ holders[entry]
        far = CAP + step + jnp.where(rank == group, 0, n_store - CAP)
        info[CAP + entry] = jnp.where(step <= 1, step * CAP + rank, far)
    copies = []
    for slot, target in enumerate(targets):
        fetches[slot].wait()
        copies.append(pltpu.make_async_copy(held.at[slot], target, out_sem.at[slot]))
        copies[-1].start()
    for copy in copies:
        copy.wait()


def pick(slots, wanted, down, up):
    n_store = wanted.shape[0]
    slab = jax.ShapeDtypeStruct(down.shape[1:], down.dtype)
    pair = jax.ShapeDtypeStruct((CAP,) + down.shape[1:], down.dtype)
    outs = [slab] * n_store + [slab] * (n_store - CAP) + [pair]
    return pl.pallas_call(
        functools.partial(pick_kernel, n_store),
        out_shape=outs + [jax.ShapeDtypeStruct((CAP + wanted.shape[1],), jnp.int32)],
        in_specs=[ANY, ANY, HBM, HBM],
        out_specs=[ANY] * len(outs) + [SMEM],
        scratch_shapes=[
            pltpu.SMEM(slots.shape, slots.dtype),
            pltpu.SMEM(wanted.shape, wanted.dtype),
            pltpu.VMEM((2 * n_store,) + down.shape[1:], down.dtype),
            pltpu.SemaphoreType.DMA((2,)),
            pltpu.SemaphoreType.DMA((2 * n_store,)),
            pltpu.SemaphoreType.DMA((2 * n_store,)),
        ],
        compiler_params=params(60),
        cost_estimate=SMALL,
        name="pick",
    )(slots, wanted, down, up)


def stack_kernel(count, *refs):
    o_ref = refs[-1]
    for number in range(count):
        o_ref[number] = refs[number][...]


def stack(slabs, *earlier):
    return pl.pallas_call(
        functools.partial(stack_kernel, len(slabs)),
        out_shape=jax.ShapeDtypeStruct((len(slabs),) + slabs[0].shape, slabs[0].dtype),
        in_specs=[VMEM] * len(slabs) + [ANY] * len(earlier),
        out_specs=VMEM,
        compiler_params=params(8),
        cost_estimate=SMALL,
        name="stack",
    )(*slabs, *earlier)


def tie_kernel(*refs):
    pass


def tie(value, *earlier):
    return pl.pallas_call(
        tie_kernel,
        out_shape=jax.ShapeDtypeStruct(value.shape, value.dtype),
        in_specs=[ANY] * (1 + len(earlier)),
        out_specs=ANY,
        input_output_aliases={0: 0},
        compiler_params=params(2),
        cost_estimate=SMALL,
        name="tie",
    )(value, *earlier)


def attend_rows(first, count, lengths, q, k, v, out, slot_count, length, offset, row):
    heads = q.shape[1] // 128
    per_slot = heads // slot_count
    span = ROWS * slot_count * length
    scale = 1.0 / math.sqrt(128)
    finished = []
    for here in range(first, first + count, ROWS):
        limit = jnp.zeros((ROWS, span), jnp.int32)
        for r in range(ROWS):
            limit = jnp.where(row == r, lengths[here + r], limit)
        visible = jnp.logical_and(offset >= 0, offset < limit[None, None])
        rows = q[pl.ds(here // 16 * 16, 16), :].astype(jnp.float32)
        rows = rows[here % 16 : here % 16 + ROWS]
        stacked = jnp.concatenate(
            [rows[:, h * 128 : (h + 1) * 128] for h in range(heads)], axis=0
        ).astype(jnp.bfloat16)
        keys = k[pl.ds(here // ROWS * span, span), :]
        values = v[pl.ds(here // ROWS * span, span), :]
        scores = lax.dot_general(
            stacked, keys, (((1,), (1,)), ((), ())), preferred_element_type=jnp.float32
        ).reshape(slot_count, per_slot, ROWS, span)
        scores = jnp.where(visible, scores, MASKED)
        top = jnp.max(scores, axis=-1, keepdims=True)
        weights = jnp.exp((scores - top) * scale).reshape(heads * ROWS, span).astype(jnp.bfloat16)
        both = jnp.concatenate([values, jnp.ones_like(values)], axis=1)
        summed = jnp.dot(weights, both, preferred_element_type=jnp.float32)
        mean = summed[:, :128] / summed[:, 128:]
        finished.append(
            jnp.concatenate([mean[h * ROWS : (h + 1) * ROWS] for h in range(heads)], axis=1)
        )
        if len(finished) == 2:
            out[pl.ds(here - ROWS, 16), :] = jnp.concatenate(finished, axis=0).astype(out.dtype)
            finished = []


class Stream:
    def __init__(self, jobs, ahead):
        self.jobs, self.ahead, self.next = jobs, ahead, 0
        for job in jobs[:ahead]:
            self.start(job)

    def start(self, job):
        for copy in job:
            copy.start()

    def take(self):
        for copy in self.jobs[self.next]:
            copy.wait()
        for job in self.jobs[self.next + self.ahead : self.next + self.ahead + 1]:
            self.start(job)
        self.next += 1


def weight_columns(step, n_chip, width, tile, weight, held, sems):
    tensor = lax.axis_index("tensor")
    chip = lax.rem(lax.div(tensor, 2) + step, n_chip)
    core = lax.rem(tensor, 2)
    jobs = []
    for number in range(2 * width // tile):
        block = chip * 2 + (1 - core if number * tile < width else core)
        start = pl.multiple_of(block * width + number * tile % width, tile)
        jobs.append(
            [
                pltpu.make_async_copy(
                    weight.at[:, pl.ds(start, tile)], held.at[number], sems.at[number]
                )
            ]
        )
    return jobs


def project_rows(x, stream, held, made, outs, sems):
    width, tile = made.shape[2], held.shape[2]
    steps = width // tile
    copies = []
    for block, out in enumerate(outs):
        for step in range(steps):
            stream.take()
            total = jnp.dot(x[...], held[block * steps + step], preferred_element_type=jnp.float32)
            made[block, :, step * tile : (step + 1) * tile] = total.astype(made.dtype)
        copy = pltpu.make_async_copy(made.at[block], out, sems.at[block])
        copy.start()
        copies.append(copy)
    return copies


def front_kernel(n_chip, slot_count, length, chunk, lengths_in, q_in, k_in, v_in, w_in, *refs):
    flag, attended, other, own = refs[-15:-11]
    lengths, q, k, v, w, x, made, lengths_sem, qkv_sem, w_sem, out_sem = refs[-11:]
    rows, width = q.shape[0], made.shape[2]
    per_row = slot_count * length
    jobs = []
    for part in range(rows // chunk):
        job = []
        for number, (source, held, size) in enumerate(
            ((q_in, q, chunk), (k_in, k, chunk * per_row), (v_in, v, chunk * per_row))
        ):
            span = pl.ds(part * size, size)
            job.append(
                pltpu.make_async_copy(source.at[span], held.at[span], qkv_sem.at[part, number])
            )
        jobs.append(job)
    jobs[0].append(pltpu.make_async_copy(lengths_in, lengths, lengths_sem.at[0]))
    stream = Stream(
        jobs + weight_columns(1, n_chip, width, w.shape[2], w_in, w, w_sem), AHEAD
    )
    span = ROWS * per_row
    shape = (slot_count, 1, ROWS, span)
    offset = (
        lax.broadcasted_iota(jnp.int32, shape, 3)
        - lax.broadcasted_iota(jnp.int32, shape, 2) * per_row
        - lax.broadcasted_iota(jnp.int32, shape, 0) * length
    )
    row = lax.broadcasted_iota(jnp.int32, (ROWS, span), 0)
    for part in range(rows // chunk):
        stream.take()
        attend_rows(part * chunk, chunk, lengths, q, k, v, x, slot_count, length, offset, row)
    flag[0] = lengths[0]
    copies = [pltpu.make_async_copy(x, attended, out_sem.at[2])]
    copies[0].start()
    copies += project_rows(x, stream, w, made, (other, own), out_sem)
    for copy in copies:
        copy.wait()


def front(n_chip, lengths, queries, keys, values, weight, width, *earlier):
    rows, slot_count, length, head = keys.shape
    depth = queries.shape[1]
    tile = min(512, width)
    tiles = 2 * width // tile
    chunk = min(CHUNK, rows)
    half = jax.ShapeDtypeStruct((rows, width), jnp.bfloat16)
    return pl.pallas_call(
        functools.partial(front_kernel, n_chip, slot_count, length, chunk),
        out_shape=[
            jax.ShapeDtypeStruct((1,), jnp.int32),
            jax.ShapeDtypeStruct((rows, depth), jnp.bfloat16),
            half,
            half,
        ],
        in_specs=[ANY] + [HBM] * 4 + [ANY] * len(earlier),
        out_specs=[SMEM] + [ANY] * 3,
        scratch_shapes=[
            pltpu.SMEM(lengths.shape, lengths.dtype),
            pltpu.VMEM((rows, depth), queries.dtype),
            pltpu.VMEM((rows * slot_count * length, head), keys.dtype),
            pltpu.VMEM((rows * slot_count * length, head), values.dtype),
            pltpu.VMEM((tiles, depth, tile), weight.dtype),
            pltpu.VMEM((rows, depth), jnp.bfloat16),
            pltpu.VMEM((2, rows, width), jnp.bfloat16),
            pltpu.SemaphoreType.DMA((1,)),
            pltpu.SemaphoreType.DMA((rows // chunk, 3)),
            pltpu.SemaphoreType.DMA((tiles,)),
            pltpu.SemaphoreType.DMA((3,)),
        ],
        compiler_params=params(58),
        cost_estimate=SMALL,
        name="front",
    )(
        lengths,
        queries,
        keys.reshape(-1, head),
        values.reshape(-1, head),
        weight,
        *earlier,
    )


def project_kernel(step, n_chip, x, w_in, *refs):
    other, own, w, made, w_sem, out_sem = refs[-6:]
    stream = Stream(
        weight_columns(step, n_chip, made.shape[2], w.shape[2], w_in, w, w_sem), AHEAD
    )
    for copy in project_rows(x, stream, w, made, (other, own), out_sem):
        copy.wait()


def project(step, n_chip, attended, weight, width, *earlier):
    rows, depth = attended.shape
    tile = min(512, width)
    tiles = 2 * width // tile
    half = jax.ShapeDtypeStruct((rows, width), jnp.bfloat16)
    return pl.pallas_call(
        functools.partial(project_kernel, step, n_chip),
        out_shape=[half, half],
        in_specs=[VMEM, HBM] + [ANY] * len(earlier),
        out_specs=[ANY] * 2,
        scratch_shapes=[
            pltpu.VMEM((tiles, depth, tile), weight.dtype),
            pltpu.VMEM((2, rows, width), jnp.bfloat16),
            pltpu.SemaphoreType.DMA((tiles,)),
            pltpu.SemaphoreType.DMA((2,)),
        ],
        compiler_params=params(32),
        cost_estimate=SMALL,
        name="project",
    )(attended, weight, *earlier)


def place_row(info, entries):
    place = jnp.zeros(entries.shape, jnp.int32)
    for entry in range(info.shape[0] - CAP):
        place = jnp.where(entries == entry, info[CAP + entry], place)
    return place


def shrink_kernel(count, info, entries_ref, x_ref, near_ref, *refs):
    slab_refs, (o_ref, near, sem) = refs[:count], refs[-3:]
    fetches = []
    for rank in range(CAP):
        fetch = pltpu.make_async_copy(near_ref.at[info[rank]], near.at[rank], sem.at[rank])
        fetch.start()
        fetches.append(fetch)
    place = place_row(info, entries_ref[...])
    for fetch in fetches:
        fetch.wait()
    slabs = jnp.concatenate(
        [near[rank] for rank in range(CAP)]
        + [ref[...].reshape(-1, ref.shape[-1]) for ref in slab_refs],
        axis=0,
    )
    products = lax.dot_general(
        slabs, x_ref[...], (((1,), (1,)), ((), ())), preferred_element_type=jnp.float32
    )
    size = o_ref.shape[0]
    total = jnp.zeros(o_ref.shape, jnp.float32)
    for slot in range(slabs.shape[0] // size):
        total = total + jnp.where(place == slot, products[slot * size : (slot + 1) * size], 0.0)
    o_ref[...] = total


def shrink_part(info, entries, attended, near, slabs, *earlier):
    rows = attended.shape[0]
    _, size, width = near.shape
    return pl.pallas_call(
        functools.partial(shrink_kernel, len(slabs)),
        out_shape=jax.ShapeDtypeStruct((size, rows), jnp.float32),
        in_specs=[SMEM, VMEM, VMEM, HBM] + [VMEM] * len(slabs) + [ANY] * len(earlier),
        out_specs=VMEM,
        scratch_shapes=[
            pltpu.VMEM((CAP, size, width), near.dtype),
            pltpu.SemaphoreType.DMA((CAP,)),
        ],
        compiler_params=params(24),
        cost_estimate=SMALL,
        name="shrink",
    )(info, entries, attended, near, *slabs, *earlier)


def spread_kernel(slot_total, info, entries_ref, parts_ref, *refs):
    o_ref = refs[-1]
    place = place_row(info, entries_ref[...])
    low = jnp.sum(parts_ref[...], axis=0).astype(jnp.bfloat16).astype(jnp.float32)
    wide = jnp.concatenate(
        [jnp.where(place == slot, low, 0.0) for slot in range(slot_total)], axis=0
    )
    o_ref[...] = wide.T.astype(jnp.bfloat16)


def spread(info, entries, parts, slot_total, *earlier):
    _, size, rows = parts.shape
    return pl.pallas_call(
        functools.partial(spread_kernel, slot_total),
        out_shape=jax.ShapeDtypeStruct((rows, slot_total * size), jnp.bfloat16),
        in_specs=[SMEM, VMEM, VMEM] + [ANY] * len(earlier),
        out_specs=VMEM,
        compiler_params=params(12),
        cost_estimate=SMALL,
        name="spread",
    )(info, entries, parts, *earlier)


def expand_kernel(count, part_count, info, wide_ref, near_ref, *refs):
    slab_refs, parts = refs[:count], refs[count : count + sum(part_count)]
    o_ref, near, sem = refs[-3:]
    fetches = []
    for rank in range(CAP):
        fetch = pltpu.make_async_copy(near_ref.at[info[rank]], near.at[rank], sem.at[rank])
        fetch.start()
        fetches.append(fetch)
    for fetch in fetches:
        fetch.wait()
    slabs = jnp.concatenate(
        [near[rank] for rank in range(CAP)]
        + [ref[...].reshape(-1, ref.shape[-1]) for ref in slab_refs],
        axis=0,
    )
    total = jnp.dot(
        wide_ref[:, : slabs.shape[0]], slabs, preferred_element_type=jnp.float32
    )
    rest = iter(parts)
    for pieces in part_count:
        part = jnp.concatenate([next(rest)[...] for _ in range(pieces)], axis=0)
        total = total + part.astype(jnp.float32)
    o_ref[...] = total.astype(o_ref.dtype)


def expand(info, wide, near, slabs, parts, *earlier):
    rows, width = parts[0][0].shape
    counts = [len(pieces) for pieces in parts]
    flat = [piece for pieces in parts for piece in pieces]
    return pl.pallas_call(
        functools.partial(expand_kernel, len(slabs), counts),
        out_shape=jax.ShapeDtypeStruct((rows, width), jnp.float32),
        in_specs=[SMEM, VMEM, HBM] + [VMEM] * (len(slabs) + len(flat)) + [ANY] * len(earlier),
        out_specs=VMEM,
        scratch_shapes=[
            pltpu.VMEM((CAP,) + near.shape[1:], near.dtype),
            pltpu.SemaphoreType.DMA((CAP,)),
        ],
        compiler_params=params(24),
        cost_estimate=SMALL,
        name="expand",
    )(info, wide, near, *slabs, *flat, *earlier)


def finish_kernel(wide_ref, total_ref, *refs):
    slab_refs, o_ref = refs[:-1], refs[-1]
    slabs = jnp.concatenate([ref[...] for ref in slab_refs], axis=0)
    first = wide_ref.shape[1] - slabs.shape[0]
    delta = jnp.dot(wide_ref[:, first:], slabs, preferred_element_type=jnp.float32)
    o_ref[...] = (total_ref[...] + delta).astype(o_ref.dtype)


def finish(wide, total, slabs):
    return pl.pallas_call(
        finish_kernel,
        out_shape=jax.ShapeDtypeStruct(total.shape, jnp.bfloat16),
        in_specs=[VMEM] * (2 + len(slabs)),
        out_specs=VMEM,
        compiler_params=params(24),
        cost_estimate=SMALL,
        name="finish",
    )(wide, total, *slabs)


def shards(
    mesh,
    queries,
    cached_key_slabs,
    cached_value_slabs,
    request_cache_lengths,
    output_projection_weight,
    adapter_shrink_weight,
    adapter_expand_weight,
    adapter_storage_slot,
    wanted,
    request_wanted_entry,
):
    n_store, n_tensor = mesh.shape["store"], mesh.shape["tensor"]
    n_chip = n_tensor // 2
    local_width = adapter_shrink_weight.shape[2]
    far_steps = range(1, n_chip)

    def along_store(x, step):
        return lax.ppermute(x, "store", [(s, s ^ step) for s in range(n_store)])

    def swap_group(x):
        return lax.ppermute(x, "group", [(0, 1), (1, 0)])

    def swap_core(x):
        return lax.ppermute(x, "tensor", [(t, t ^ 1) for t in range(n_tensor)])

    def along_chip(x, step):
        return lax.ppermute(x, "tensor", [(t, (t + 2 * step) % n_tensor) for t in range(n_tensor)])

    weight = output_projection_weight
    *picked, send_pair, info = pick(
        adapter_storage_slot, wanted, adapter_shrink_weight, adapter_expand_weight
    )
    steps = range(CAP, n_store)
    own_down = [along_store(x, step) for step, x in zip(steps, picked)]
    next_down = [along_store(x, 1) for x in picked[len(steps) : n_store]]
    send_up = picked[n_store:]
    flag, attended, other, own = front(
        n_chip,
        request_cache_lengths,
        queries,
        cached_key_slabs,
        cached_value_slabs,
        weight,
        local_width,
        info,
    )

    def meet(mine, given):
        return (mine.astype(jnp.float32) + given.astype(jnp.float32)).astype(jnp.bfloat16)

    def join(other, own):
        return lax.cond(
            flag[0] > 0,
            lambda: meet(own, swap_core(other)),
            lambda: meet(swap_core(other), own),
        )

    arrived = []
    for step in far_steps:
        if step > 1:
            other, own = project(step, n_chip, attended, weight, local_width, met)
        met = join(other, own)
        arrived.append([along_chip(met, step)])
    own_up = [along_store(tie(x, met), step) for step, x in zip(steps, send_up)]
    next_up = along_store(tie(send_pair, met), 1)
    own_down = stack(own_down, met, *next_down)
    swapped_down = swap_group(own_down)
    other, own = project(0, n_chip, attended, weight, local_width, met)

    def middle(first):
        given = swap_core(other)
        swapped = [swap_group(x) for x in own_up[:-1]]
        part = shrink_part(
            info,
            request_wanted_entry,
            attended,
            adapter_shrink_weight,
            [*next_down, own_down, swapped_down],
        )
        base = meet(own, given) if first else meet(given, own)
        return base, swapped, lax.all_gather(part, "tensor")

    base, swapped_up, gathered = lax.cond(
        flag[0] > 0, lambda: middle(True), lambda: middle(False)
    )
    wide = spread(info, request_wanted_entry, gathered, n_store * CAP)
    last = tie(own_up[-1], wide)
    swapped = swap_group(last)
    total = expand(
        info,
        wide,
        adapter_expand_weight,
        [next_up] + own_up[:-1] + [last] + swapped_up,
        [[base]] + arrived,
    )
    return finish(wide, total, [swapped])


def solution(mesh):
    placed = (
        P(("group", "store"), "tensor"),
        P(("group", "store"), "tensor", None, None),
        P(("group", "store"), "tensor", None, None),
        P(("group", "store")),
        P("tensor", None),
        P("store", None, "tensor"),
        P("store", None, "tensor"),
        P(),
        P(),
        P(("group", "store"), None),
    )
    return jax.shard_map(
        functools.partial(shards, mesh),
        mesh=mesh,
        in_specs=placed,
        out_specs=P(("group", "store"), "tensor"),
        check_vma=False,
    )
```

time: 82.5 us -> 70 us (0.85)
  waiting for transfers between devices: 20.4 us -> 9.69 us
  local copies, waits for them, and re-layouts: 6.06 us -> 1.02 us
  Pallas kernels: 28 us -> 32.1 us
  starting transfers between devices: 19.7 us -> 17.3 us
  other arithmetic: 0.38 us -> 1.75 us
    ppermute x6 -> x3, waiting for transfers between devices: 16.6 us -> 4.83 us  [swap_group(): return lax.ppermute(x, 'group', [(0, 1), (1, 0)])]
    unnamed x22 -> x20, local copies, waits for them, and re-layouts: 6.06 us -> 1.02 us
    pallas_call x3 -> x5, Pallas kernels: 23.5 us -> 26.9 us  [the longest x1 13.5 us: front(): pl.pallas_call(functools.partial(front_kernel, n_chip, slot_count, length...]
    ppermute x3 -> x2, waiting for transfers between devices: 0.01 us -> 2.65 us  [swap_core(): return lax.ppermute(x, 'tensor', [(t, t ^ 1) for t in range(n_tensor)])]
    ppermute x6 -> x3, starting transfers between devices: 5.37 us -> 3.35 us  [swap_group(): return lax.ppermute(x, 'group', [(0, 1), (1, 0)])]
    ppermute x6 -> x7, waiting for transfers between devices: 3.82 us -> 2.2 us  [along_store(): return lax.ppermute(x, 'store', [(s, s ^ step) for s in range(n_store)])]
    convert_element_type x1 -> x2, other arithmetic: 0.38 us -> 1.75 us  [meet(): (mine.astype(jnp.float32) + given.astype(jnp.float32)).astype(jnp.bfloat16)]
    pallas_call x1, Pallas kernels: 1.36 us -> 2.19 us  [shrink_part(): pl.pallas_call(functools.partial(shrink_kernel, len(slabs)), out_shape=ja...]
  transfers between devices with their start and end apart: 16 -> 13, of which waited for: 5 -> 4; matrix products, arithmetic and copies ran while one was open for 0% -> 2% of each run, Pallas kernels for 29% -> 38%
where the time goes in v2:
time: 70 us
  Pallas kernels  32.1 us (46%)
  starting transfers between devices  17.3 us (25%)
  waiting for transfers between devices  9.69 us (14%)
  blocking collectives  7.28 us (10%)
  other arithmetic  1.75 us (2%)
  local copies, waits for them, and re-layouts  1.02 us (1%)
  between operations  0.81 us (1%)
    pallas_call x1, Pallas kernels, front(): pl.pallas_call(functools.partial(front_kernel, n_chip, slot_count, length...  13.5 us
    ppermute x7, starting transfers between devices, along_store(): return lax.ppermute(x, 'store', [(s, s ^ step) for s in range(n_store)])  12.2 us
    pallas_call x1, Pallas kernels, project(): pl.pallas_call(functools.partial(project_kernel, step, n_chip), out_shape...  7.67 us
    all_gather x1, blocking collectives, middle(): return (base, swapped, lax.all_gather(part, 'tensor'))  7.28 us
    ppermute x3, waiting for transfers between devices, swap_group(): return lax.ppermute(x, 'group', [(0, 1), (1, 0)])  4.83 us
    pallas_call x1, Pallas kernels, pick(): pl.pallas_call(functools.partial(pick_kernel, n_store), out_shape=outs +...  4.27 us
    ppermute x3, starting transfers between devices, swap_group(): return lax.ppermute(x, 'group', [(0, 1), (1, 0)])  3.35 us
    ppermute x2, waiting for transfers between devices, swap_core(): return lax.ppermute(x, 'tensor', [(t, t ^ 1) for t in range(n_tensor)])  2.65 us
  transfers between devices with their start and end apart: 13, of which 4 were waited for; matrix products, arithmetic and copies ran while one was open for 2% of the time, Pallas kernels for 38%

profile of v2, /device:TPU:0, one launch (start us, length us, event | category | flops | bytes accessed | tf_op | source)
XLA Modules:
  0.0 70.0 jit_solution(10260723821937588762)
XLA Ops:
  0.0 4.3 %pick.1 = (bf16[64,2048]{1,0:T(8,128)(2,1)}, bf16[64,2048]{1,0:T(8,128)(2,1)}, bf16[64,2048]{1,0:T(8,128)(2,1)}, bf16[64,2048]{1,0:T(8,128)(2,1)}, bf16[64,2048]...) custom-call(s32[32]{0:T(128)} %slots_in.1, s32[4,8]{1,0:T(4,128)} %wanted_in.1, ...), custom_call_target="tpu_custom_call" | custom-call | flops 1 | bytes 1 | tf_op jit(solution)/shard_map/pick/pallas_call | solution.py:98
  4.3 3.3 %collective-permute-start.7 = (bf16[64,2048]{1,0:T(8,128)(2,1)}, bf16[64,2048]{1,0:T(8,128)(2,1)S(1)}, u32[]{:S(2)}, u32[]{:S(2)}) collective-permute-start(bf16[64,2048]{1,0:T(8,128)(2,1)} %get-tuple-element.125), channel_id=1, source_target_pairs={{0,4},{4,0},{8,12},{12,8},{1,5},{5,1},{9,13},{13,9},{2,6},{6,2},{1... | collective-permute-start | bytes 786440 | tf_op jit(solution)/shard_map/ppermute | solution.py:507
  7.5 0.1 collective-permute-start.8
  7.6 2.4 %collective-permute-start.9 = (bf16[64,2048]{1,0:T(8,128)(2,1)}, bf16[64,2048]{1,0:T(8,128)(2,1)S(1)}, u32[]{:S(2)}, u32[]{:S(2)}) collective-permute-start(bf16[64,2048]{1,0:T(8,128)(2,1)} %get-tuple-element.127), channel_id=1, source_target_pairs={{0,8},{4,12},{8,0},{12,4},{1,9},{5,13},{9,1},{13,5},{2,10},{6,14},... | collective-permute-start | bytes 786440 | tf_op jit(solution)/shard_map/ppermute | solution.py:507
  10.0 1.9 %collective-permute-start.10 = (bf16[64,2048]{1,0:T(8,128)(2,1)}, bf16[64,2048]{1,0:T(8,128)(2,1)S(1)}, u32[]{:S(2)}, u32[]{:S(2)}) collective-permute-start(bf16[64,2048]{1,0:T(8,128)(2,1)} %get-tuple-element.128), channel_id=1, source_target_pairs={{0,12},{4,8},{8,4},{12,0},{1,13},{5,9},{9,5},{13,1},{2,14},{6,10},... | collective-permute-start | bytes 786440 | tf_op jit(solution)/shard_map/ppermute | solution.py:507
  11.9 13.5 %front.1 = (s32[1]{0:T(128)}, bf16[256,2048]{1,0:T(8,128)(2,1)S(1)}, bf16[256,2048]{1,0:T(8,128)(2,1)S(1)}, bf16[256,2048]{1,0:T(8,128)(2,1)S(1)}) custom-call(s32[256]{0:T(256)} %lengths_in.1, bf16[256,2048]{1,0:T(8,128)(2,1)} %q_in.1, bf16[12288,128]{1,0:T(8,128)(2,1)} %bitcast.5, bf16[12288,128]{1,0:T(8,128)(2,1)} %bitcast.6, bf16[2048,8192]{1,0:T(8,128)(2,1)} %w_in.3, ...), custom_call_target="tpu_custom_call" | custom-call | flops 1 | bytes 1 | tf_op jit(solution)/shard_map/front/pallas_call | solution.py:284
  25.4 0.0 copy-start.3
  26.0 4.1 %conditional.6 = (bf16[256,2048]{1,0:T(8,128)(2,1)}) conditional(s32[]{:T(128)} %bitcast.4, (bf16[256,2048]{1,0:T(8,128)(2,1)S(1)}, bf16[256,2048]{1,0:T(8,128)(2,1)S(1)}) %tuple.39, (bf16[256,2048]{1,0:T(8,128)(2,1)S(1)}, bf16[256,2048]{1,0:T(8,128)(2,1)S(1)}) %tuple.40), branch_computations={%region_0.0_spmd, %region_1.0_spmd} | conditional | flops 2097152 | bytes 7340080
  26.1 0.1 collective-permute-start.1
  26.1 2.6 %collective-permute-done.1 = bf16[256,2048]{1,0:T(8,128)(2,1)S(1)} collective-permute-done((bf16[256,2048]{1,0:T(8,128)(2,1)S(1)}, bf16[256,2048]{1,0:T(8,128)(2,1)S(1)}, u32[]{:S(2)}, u32[]{:S(2)}) %collective-permute-start.1) | collective-permute-done | bytes 1048608 | tf_op jit(solution)/shard_map/cond/branch_1_fun/ppermute | solution.py:513
  28.8 1.4 %add_convert_fusion.1 = bf16[256,2048]{1,0:T(8,128)(2,1)} fusion(bf16[256,2048]{1,0:T(8,128)(2,1)S(1)} %collective-permute-done.1, bf16[256,2048]{1,0:T(8,128)(2,1)S(1)} %get-tuple-element.78), kind=kLoop, calls=%fused_computation.1 | loop fusion | flops 2097152 | bytes 3145728 | tf_op jit(solution)/shard_map/cond/branch_0_fun/convert_element_type | solution.py:538
  30.2 1.5 %collective-permute-start.14 = (bf16[256,2048]{1,0:T(8,128)(2,1)}, bf16[256,2048]{1,0:T(8,128)(2,1)S(1)}, u32[]{:S(2)}, u32[]{:S(2)}) collective-permute-start(bf16[256,2048]{1,0:T(8,128)(2,1)} %get-tuple-element.147.refs_1_.refs_2_.refs_0_), channel_id=1, source_target_pairs={{0,2},{1,3},{2,0},{3,1},{4,6},{5,7},{6,4},{7,5},{8,10},{9,11},{10,... | collective-permute-start | bytes 3145736 | tf_op jit(solution)/shard_map/ppermute | solution.py:516
  31.7 0.0 collective-permute-done.7.refs_3_
  31.7 0.0 collective-permute-done.8.refs_4_
  31.7 0.0 copy-start.7
  31.7 0.0 collective-permute-done.9.refs_0_
  31.7 0.9 %collective-permute-done.10.refs_1_ = bf16[64,2048]{1,0:T(8,128)(2,1)S(1)} collective-permute-done((bf16[64,2048]{1,0:T(8,128)(2,1)}, bf16[64,2048]{1,0:T(8,128)(2,1)S(1)}, u32[]{:S(2)}, u32[]{:S(2)}) %collective-permute-start.10) | collective-permute-done | bytes 262176 | tf_op jit(solution)/shard_map/ppermute | solution.py:507
  32.7 1.6 %collective-permute-start.11 = (bf16[2,64,2048]{2,1,0:T(8,128)(2,1)S(1)}, bf16[2,64,2048]{2,1,0:T(8,128)(2,1)S(1)}, u32[]{:S(2)}, u32[]{:S(2)}) collective-permute-start(bf16[2,64,2048]{2,1,0:T(8,128)(2,1)S(1)} %stack.1), channel_id=1, source_target_pairs={{0,16},{16,0},{1,17},{17,1},{2,18},{18,2},{3,19},{19,3},{4,20},{20... | collective-permute-start | bytes 1572872 | tf_op jit(solution)/shard_map/ppermute | solution.py:510
  34.2 0.0 copy-done.1
  34.2 0.0 copy-done.5
  34.2 0.0 copy-done.7
  34.2 3.0 %collective-permute-start.6 = (bf16[64,2048]{1,0:T(8,128)(2,1)S(1)}, bf16[64,2048]{1,0:T(8,128)(2,1)}, u32[]{:S(2)}, u32[]{:S(2)}) collective-permute-start(bf16[64,2048]{1,0:T(8,128)(2,1)S(1)} %tie.4), channel_id=1, source_target_pairs={{0,8},{4,12},{8,0},{12,4},{1,9},{5,13},{9,1},{13,5},{2,10},{6,14},... | collective-permute-start | bytes 786440 | tf_op jit(solution)/shard_map/ppermute | solution.py:507
  37.3 0.0 collective-permute-start.12
  37.3 1.5 %collective-permute-start.13 = (bf16[64,2048]{1,0:T(8,128)(2,1)}, bf16[64,2048]{1,0:T(8,128)(2,1)S(1)}, u32[]{:S(2)}, u32[]{:S(2)}) collective-permute-start(bf16[64,2048]{1,0:T(8,128)(2,1)} %tie.6), channel_id=1, source_target_pairs={{0,12},{4,8},{8,4},{12,0},{1,13},{5,9},{9,5},{13,1},{2,14},{6,10},... | collective-permute-start | bytes 786440 | tf_op jit(solution)/shard_map/ppermute | solution.py:507
  38.8 0.0 copy-done.3
  38.8 0.0 copy-start.9
  38.9 7.7 %project.1 = (bf16[256,2048]{1,0:T(8,128)(2,1)S(1)}, bf16[256,2048]{1,0:T(8,128)(2,1)S(1)}) custom-call(bf16[256,2048]{1,0:T(8,128)(2,1)S(1)} %get-tuple-element.124.x, bf16[2048,8192]{1,0:T(8,128)(2,1)} %w_in.3, bf16[256,2048]{1,0:T(8,128)(2,1)} %get-tuple-element.147.refs_1_.refs_2_.refs_0_), custom_call_target="tpu_custom_call" | custom-call | flops 1 | bytes 1 | tf_op jit(solution)/shard_map/project/pallas_call | solution.py:334
  46.5 1.3 %collective-permute-done.6.refs_1_ = bf16[64,2048]{1,0:T(8,128)(2,1)} collective-permute-done((bf16[64,2048]{1,0:T(8,128)(2,1)S(1)}, bf16[64,2048]{1,0:T(8,128)(2,1)}, u32[]{:S(2)}, u32[]{:S(2)}) %collective-permute-start.6) | collective-permute-done | bytes 262176 | tf_op jit(solution)/shard_map/ppermute | solution.py:507
  47.8 0.0 collective-permute-done.11
  47.8 0.0 copy-done.6
  47.8 0.0 copy-start
  47.9 10.4 %conditional.8 = (bf16[64,2048]{1,0:T(8,128)(2,1)}, f32[4,64,256]{2,1,0:T(8,128)S(1)}, bf16[256,2048]{1,0:T(8,128)(2,1)S(1)}) conditional(s32[]{:T(128)} %bitcast.4, (bf16[64,2048]{1,0:T(8,128)(2,1)}, s32[10]{0:T(128)S(1)}, s32[1,256]{1,0:T(1,128)S(1)}, bf16[256,2048]{1,0:T(8,128)(2,1)}, bf16[8,64,2048]{2,1,0:T(8,128)(2,1)S(1)}, ...), branch_computations={%region_2.0_spmd, %region_3.0_spmd} | conditional | flops 2097153 | bytes 8716393
  47.9 0.1 collective-permute-start.5
  48.0 0.4 collective-permute-start.4
  48.3 2.2 %shrink.3 = f32[64,256]{1,0:T(8,128)S(1)} custom-call(s32[10]{0:T(128)S(1)} %get-tuple-element.92.info, s32[1,256]{1,0:T(1,128)S(1)} %get-tuple-element.93.entries_ref, bf16[256,2048]{1,0:T(8,128)(2,1)} %get-tuple-element.94.x_ref, bf16[8,64,2048]{2,1,0:T(8,128)(2,1)S(1)} %get-tuple-element.95.near_ref, bf16[64,2048]{1,0:T(8,128)(2,1)S(1)} %get-tuple-element.96.refs_0_, ...), custom_call_target="tpu_custom_call" | custom-call | flops 1 | bytes 1 | tf_op jit(solution)/shard_map/cond/branch_1_fun/shrink/pallas_call | solution.py:386
  50.5 7.3 %all-gather.1 = f32[256,256]{1,0:T(8,128)S(1)} all-gather(f32[64,256]{1,0:T(8,128)S(1)} %shrink.3), channel_id=3, replica_groups=mesh['group'=2,'store'=4,'tensor'=4] {'tensor'}, dimensions={0}, use_global_device_ids=true | all-gather | bytes 327680 | tf_op jit(solution)/shard_map/cond/branch_1_fun/all_gather | solution.py:570
  57.8 0.0 collective-permute-done.5
  57.8 0.4 add_convert_fusion.3
  58.2 0.0 collective-permute-done.4
  58.2 1.0 %copy-done.4 = bf16[256,2048]{1,0:T(8,128)(2,1)} copy-done((bf16[256,2048]{1,0:T(8,128)(2,1)}, bf16[256,2048]{1,0:T(8,128)(2,1)S(1)}, u32[]{:S(2)}) %copy-start.4) | copy-done | bytes 1048600
  59.2 0.7 spread.1.refs_1_.wide_ref
  59.9 0.0 collective-permute-done.13.refs_0_
  59.9 1.4 %collective-permute-start.15 = (bf16[64,2048]{1,0:T(8,128)(2,1)S(1)}, bf16[64,2048]{1,0:T(8,128)(2,1)S(1)}, u32[]{:S(2)}, u32[]{:S(2)}) collective-permute-start(bf16[64,2048]{1,0:T(8,128)(2,1)S(1)} %tie.7.refs_2_), channel_id=1, source_target_pairs={{0,16},{16,0},{1,17},{17,1},{2,18},{18,2},{3,19},{19,3},{4,20},{20... | collective-permute-start | bytes 786440 | tf_op jit(solution)/shard_map/ppermute | solution.py:510
  61.3 0.0 collective-permute-done.12.refs_0_
  61.3 0.0 collective-permute-done.14.refs_5_
  61.3 2.4 %expand.1.total_ref = f32[256,2048]{1,0:T(8,128)S(1)} custom-call(s32[10]{0:T(128)S(1)} %get-tuple-element.119.refs_0_.info, bf16[256,512]{1,0:T(8,128)(2,1)S(1)} %spread.1.refs_1_.wide_ref, bf16[8,64,2048]{2,1,0:T(8,128)(2,1)S(1)} %copy-done, bf16[2,64,2048]{2,1,0:T(8,128)(2,1)} %collective-permute-done.12.refs_0_, ...), custom_call_target="tpu_custom_call" | custom-call | flops 1 | bytes 1 | tf_op jit(solution)/shard_map/expand/pallas_call | solution.py:453
  63.7 4.8 %collective-permute-done.15.refs_0_ = bf16[64,2048]{1,0:T(8,128)(2,1)S(1)} collective-permute-done((bf16[64,2048]{1,0:T(8,128)(2,1)S(1)}, bf16[64,2048]{1,0:T(8,128)(2,1)S(1)}, u32[]{:S(2)}, u32[]{:S(2)}) %collective-permute-start.15) | collective-permute-done | bytes 262176 | tf_op jit(solution)/shard_map/ppermute | solution.py:510
  68.5 1.4 %finish.1 = bf16[256,2048]{1,0:T(8,128)(2,1)} custom-call(bf16[256,512]{1,0:T(8,128)(2,1)S(1)} %spread.1.refs_1_.wide_ref, f32[256,2048]{1,0:T(8,128)S(1)} %expand.1.total_ref, bf16[64,2048]{1,0:T(8,128)(2,1)S(1)} %collective-permute-done.15.refs_0_), custom_call_target="tpu_custom_call" | custom-call | flops 1 | bytes 1 | tf_op jit(solution)/shard_map/finish/pallas_call | solution.py:477
  (15 shorter events, 0.1 us)
Async XLA Ops:
  4.3 27.4 %collective-permute-start.7 = (bf16[64,2048]{1,0:T(8,128)(2,1)}, bf16[64,2048]{1,0:T(8,128)(2,1)S(1)}, u32[]{:S(2)}, u32[]{:S(2)}) collective-permute-start(bf16[64,2048]{1,0:T(8,128)(2,1)} %get-tuple-element.125), channel_id=1, source_target_pairs={{0,4},{4,0},{8,12},{12,8},{1,5},{5,1},{9,13},{13,9},{2,6},{6,2},{1... | collective-permute-start | bytes 786440 | tf_op jit(solution)/shard_map/ppermute | solution.py:507
  7.5 24.1 %collective-permute-start.8 = (bf16[64,2048]{1,0:T(8,128)(2,1)}, bf16[64,2048]{1,0:T(8,128)(2,1)S(1)}, u32[]{:S(2)}, u32[]{:S(2)}) collective-permute-start(bf16[64,2048]{1,0:T(8,128)(2,1)} %get-tuple-element.126), channel_id=1, source_target_pairs={{0,4},{4,0},{8,12},{12,8},{1,5},{5,1},{9,13},{13,9},{2,6},{6,2},{1... | collective-permute-start | bytes 786440 | tf_op jit(solution)/shard_map/ppermute | solution.py:507
  7.6 24.1 %collective-permute-start.9 = (bf16[64,2048]{1,0:T(8,128)(2,1)}, bf16[64,2048]{1,0:T(8,128)(2,1)S(1)}, u32[]{:S(2)}, u32[]{:S(2)}) collective-permute-start(bf16[64,2048]{1,0:T(8,128)(2,1)} %get-tuple-element.127), channel_id=1, source_target_pairs={{0,8},{4,12},{8,0},{12,4},{1,9},{5,13},{9,1},{13,5},{2,10},{6,14},... | collective-permute-start | bytes 786440 | tf_op jit(solution)/shard_map/ppermute | solution.py:507
  10.0 22.6 %collective-permute-start.10 = (bf16[64,2048]{1,0:T(8,128)(2,1)}, bf16[64,2048]{1,0:T(8,128)(2,1)S(1)}, u32[]{:S(2)}, u32[]{:S(2)}) collective-permute-start(bf16[64,2048]{1,0:T(8,128)(2,1)} %get-tuple-element.128), channel_id=1, source_target_pairs={{0,12},{4,8},{8,4},{12,0},{1,13},{5,9},{9,5},{13,1},{2,14},{6,10},... | collective-permute-start | bytes 786440 | tf_op jit(solution)/shard_map/ppermute | solution.py:507
  25.4 13.4 %copy-start.3 = (bf16[256,2048]{1,0:T(8,128)(2,1)}, bf16[256,2048]{1,0:T(8,128)(2,1)S(1)}, u32[]{:S(2)}) copy-start(bf16[256,2048]{1,0:T(8,128)(2,1)S(1)} %get-tuple-element.124.x) | copy-start | bytes 3145732
  26.1 2.7 %collective-permute-start.1 = (bf16[256,2048]{1,0:T(8,128)(2,1)S(1)}, bf16[256,2048]{1,0:T(8,128)(2,1)S(1)}, u32[]{:S(2)}, u32[]{:S(2)}) collective-permute-start(bf16[256,2048]{1,0:T(8,128)(2,1)S(1)} %get-tuple-element.79), channel_id=1, source_target_pairs={{0,1},{1,0},{2,3},{3,2},{4,5},{5,4},{6,7},{7,6},{8,9},{9,8},{10,11... | collective-permute-start | bytes 3145736 | tf_op jit(solution)/shard_map/cond/branch_1_fun/ppermute | solution.py:513
  30.2 4.1 %copy-start.1 = (bf16[64,2048]{1,0:T(8,128)(2,1)S(1)}, bf16[64,2048]{1,0:T(8,128)(2,1)}, u32[]{:S(2)}) copy-start(bf16[64,2048]{1,0:T(8,128)(2,1)} %get-tuple-element.121.refs_0_) | copy-start | bytes 786436
  30.2 31.2 %collective-permute-start.14 = (bf16[256,2048]{1,0:T(8,128)(2,1)}, bf16[256,2048]{1,0:T(8,128)(2,1)S(1)}, u32[]{:S(2)}, u32[]{:S(2)}) collective-permute-start(bf16[256,2048]{1,0:T(8,128)(2,1)} %get-tuple-element.147.refs_1_.refs_2_.refs_0_), channel_id=1, source_target_pairs={{0,2},{1,3},{2,0},{3,1},{4,6},{5,7},{6,4},{7,5},{8,10},{9,11},{10,... | collective-permute-start | bytes 3145736 | tf_op jit(solution)/shard_map/ppermute | solution.py:516
  31.7 2.5 %copy-start.5 = (bf16[64,2048]{1,0:T(8,128)(2,1)}, bf16[64,2048]{1,0:T(8,128)(2,1)S(1)}, u32[]{:S(2)}) copy-start(bf16[64,2048]{1,0:T(8,128)(2,1)S(1)} %collective-permute-done.7.refs_3_) | copy-start | bytes 786436
  31.7 2.5 %copy-start.7 = (bf16[64,2048]{1,0:T(8,128)(2,1)}, bf16[64,2048]{1,0:T(8,128)(2,1)S(1)}, u32[]{:S(2)}) copy-start(bf16[64,2048]{1,0:T(8,128)(2,1)S(1)} %collective-permute-done.8.refs_4_) | copy-start | bytes 786436
  32.7 15.2 %collective-permute-start.11 = (bf16[2,64,2048]{2,1,0:T(8,128)(2,1)S(1)}, bf16[2,64,2048]{2,1,0:T(8,128)(2,1)S(1)}, u32[]{:S(2)}, u32[]{:S(2)}) collective-permute-start(bf16[2,64,2048]{2,1,0:T(8,128)(2,1)S(1)} %stack.1), channel_id=1, source_target_pairs={{0,16},{16,0},{1,17},{17,1},{2,18},{18,2},{3,19},{19,3},{4,20},{20... | collective-permute-start | bytes 1572872 | tf_op jit(solution)/shard_map/ppermute | solution.py:510
  34.2 13.6 %collective-permute-start.6 = (bf16[64,2048]{1,0:T(8,128)(2,1)S(1)}, bf16[64,2048]{1,0:T(8,128)(2,1)}, u32[]{:S(2)}, u32[]{:S(2)}) collective-permute-start(bf16[64,2048]{1,0:T(8,128)(2,1)S(1)} %tie.4), channel_id=1, source_target_pairs={{0,8},{4,12},{8,0},{12,4},{1,9},{5,13},{9,1},{13,5},{2,10},{6,14},... | collective-permute-start | bytes 786440 | tf_op jit(solution)/shard_map/ppermute | solution.py:507
  37.3 24.0 %collective-permute-start.12 = (bf16[2,64,2048]{2,1,0:T(8,128)(2,1)}, bf16[2,64,2048]{2,1,0:T(8,128)(2,1)}, u32[]{:S(2)}, u32[]{:S(2)}) collective-permute-start(bf16[2,64,2048]{2,1,0:T(8,128)(2,1)} %tie.5), channel_id=1, source_target_pairs={{0,4},{4,0},{8,12},{12,8},{1,5},{5,1},{9,13},{13,9},{2,6},{6,2},{1... | collective-permute-start | bytes 1572872 | tf_op jit(solution)/shard_map/ppermute | solution.py:507
  37.3 22.6 %collective-permute-start.13 = (bf16[64,2048]{1,0:T(8,128)(2,1)}, bf16[64,2048]{1,0:T(8,128)(2,1)S(1)}, u32[]{:S(2)}, u32[]{:S(2)}) collective-permute-start(bf16[64,2048]{1,0:T(8,128)(2,1)} %tie.6), channel_id=1, source_target_pairs={{0,12},{4,8},{8,4},{12,0},{1,13},{5,9},{9,5},{13,1},{2,14},{6,10},... | collective-permute-start | bytes 786440 | tf_op jit(solution)/shard_map/ppermute | solution.py:507
  38.8 9.0 %copy-start.2 = (bf16[8,64,2048]{2,1,0:T(8,128)(2,1)S(1)}, bf16[8,64,2048]{2,1,0:T(8,128)(2,1)}, u32[]{:S(2)}) copy-start(bf16[8,64,2048]{2,1,0:T(8,128)(2,1)} %down.1) | copy-start | bytes 6291460
  38.8 9.0 %copy-start.6 = (bf16[64,2048]{1,0:T(8,128)(2,1)S(1)}, bf16[64,2048]{1,0:T(8,128)(2,1)}, u32[]{:S(2)}) copy-start(bf16[64,2048]{1,0:T(8,128)(2,1)} %copy-done.5) | copy-start | bytes 786436
  38.8 9.0 %copy-start.8 = (bf16[64,2048]{1,0:T(8,128)(2,1)S(1)}, bf16[64,2048]{1,0:T(8,128)(2,1)}, u32[]{:S(2)}) copy-start(bf16[64,2048]{1,0:T(8,128)(2,1)} %copy-done.7) | copy-start | bytes 786436
  38.8 9.0 %copy-start.9 = (s32[1,256]{1,0:T(1,128)S(1)}, s32[1,256]{1,0:T(1,128)}, u32[]{:S(2)}) copy-start(s32[1,256]{1,0:T(1,128)} %entries_ref.1) | copy-start | bytes 3076
  47.8 13.5 %copy-start = (bf16[8,64,2048]{2,1,0:T(8,128)(2,1)S(1)}, bf16[8,64,2048]{2,1,0:T(8,128)(2,1)}, u32[]{:S(2)}) copy-start(bf16[8,64,2048]{2,1,0:T(8,128)(2,1)} %near_ref.1) | copy-start | bytes 6291460
  47.9 9.9 %collective-permute-start.5 = (bf16[256,2048]{1,0:T(8,128)(2,1)S(1)}, bf16[256,2048]{1,0:T(8,128)(2,1)S(1)}, u32[]{:S(2)}, u32[]{:S(2)}) collective-permute-start(bf16[256,2048]{1,0:T(8,128)(2,1)S(1)} %get-tuple-element.101), channel_id=1, source_target_pairs={{0,1},{1,0},{2,3},{3,2},{4,5},{5,4},{6,7},{7,6},{8,9},{9,8},{10,11... | collective-permute-start | bytes 3145736 | tf_op jit(solution)/shard_map/cond/branch_1_fun/ppermute | solution.py:513
  48.0 10.3 %collective-permute-start.4 = (bf16[64,2048]{1,0:T(8,128)(2,1)}, bf16[64,2048]{1,0:T(8,128)(2,1)}, u32[]{:S(2)}, u32[]{:S(2)}) collective-permute-start(bf16[64,2048]{1,0:T(8,128)(2,1)} %get-tuple-element.91), channel_id=1, source_target_pairs={{0,16},{16,0},{1,17},{17,1},{2,18},{18,2},{3,19},{19,3},{4,20},{20... | collective-permute-start | bytes 786440 | tf_op jit(solution)/shard_map/cond/branch_1_fun/ppermute | solution.py:510
  58.2 1.0 %copy-start.4 = (bf16[256,2048]{1,0:T(8,128)(2,1)}, bf16[256,2048]{1,0:T(8,128)(2,1)S(1)}, u32[]{:S(2)}) copy-start(bf16[256,2048]{1,0:T(8,128)(2,1)S(1)} %get-tuple-element.140.refs_4_) | copy-start | bytes 3145732
  59.9 8.6 %collective-permute-start.15 = (bf16[64,2048]{1,0:T(8,128)(2,1)S(1)}, bf16[64,2048]{1,0:T(8,128)(2,1)S(1)}, u32[]{:S(2)}, u32[]{:S(2)}) collective-permute-start(bf16[64,2048]{1,0:T(8,128)(2,1)S(1)} %tie.7.refs_2_), channel_id=1, source_target_pairs={{0,16},{16,0},{1,17},{17,1},{2,18},{18,2},{3,19},{19,3},{4,20},{20... | collective-permute-start | bytes 786440 | tf_op jit(solution)/shard_map/ppermute | solution.py:510

commit v3 on v2

--- a/solution.py
+++ b/solution.py
@@ -12,7 +12,7 @@
 ROWS = 8
 MASKED = -1e30
 AHEAD = 4
-CHUNK = 32
+CHUNK = 64
 MIB = 1 << 20
 ANY = pl.BlockSpec(memory_space=pl.ANY)
 HBM = pl.BlockSpec(memory_space=pltpu.HBM)
@@ -38,8 +38,8 @@
     return index
 
 
-def pick_kernel(n_store, slots_in, wanted_in, down, up, *refs):
-    targets, (info, slots, wanted, held, table_sem, in_sem, out_sem) = refs[:-7], refs[-7:]
+def pick_kernel(n_store, slots_in, wanted_in, down, *refs):
+    outs, (info, sends, slots, wanted, held, table_sem, in_sem, out_sem) = refs[:-8], refs[-8:]
     tables = [
         pltpu.make_async_copy(slots_in, slots, table_sem.at[0]),
         pltpu.make_async_copy(wanted_in, wanted, table_sem.at[1]),
@@ -57,19 +57,12 @@
     indices += [
         held_index(slots, wanted, store ^ 1, store, rank, per_store) for rank in range(CAP)
     ]
-    count = len(indices)
-    targets = (
-        list(targets[:count])
-        + list(targets[count:-1])
-        + [targets[-1].at[rank] for rank in range(CAP)]
-    )
     fetches = []
-    for source in (down, up):
-        for index in indices:
-            slot = len(fetches)
-            fetch = pltpu.make_async_copy(source.at[index], held.at[slot], in_sem.at[slot])
-            fetch.start()
-            fetches.append(fetch)
+    for slot, index in enumerate(indices):
+        fetch = pltpu.make_async_copy(down.at[index], held.at[slot], in_sem.at[slot])
+        fetch.start()
+        fetches.append(fetch)
+        sends[slot] = index
     for rank in range(CAP):
         info[rank] = held_index(slots, wanted, store, store, rank, per_store)
     used = wanted.shape[1]
@@ -82,7 +75,7 @@
         far = CAP + step + jnp.where(rank == group, 0, n_store - CAP)
         info[CAP + entry] = jnp.where(step <= 1, step * CAP + rank, far)
     copies = []
-    for slot, target in enumerate(targets):
+    for slot, target in enumerate(outs):
         fetches[slot].wait()
         copies.append(pltpu.make_async_copy(held.at[slot], target, out_sem.at[slot]))
         copies[-1].start()
@@ -90,46 +83,49 @@
         copy.wait()
 
 
-def pick(slots, wanted, down, up):
+def pick(slots, wanted, down):
     n_store = wanted.shape[0]
     slab = jax.ShapeDtypeStruct(down.shape[1:], down.dtype)
-    pair = jax.ShapeDtypeStruct((CAP,) + down.shape[1:], down.dtype)
-    outs = [slab] * n_store + [slab] * (n_store - CAP) + [pair]
     return pl.pallas_call(
         functools.partial(pick_kernel, n_store),
-        out_shape=outs + [jax.ShapeDtypeStruct((CAP + wanted.shape[1],), jnp.int32)],
-        in_specs=[ANY, ANY, HBM, HBM],
-        out_specs=[ANY] * len(outs) + [SMEM],
+        out_shape=[slab] * n_store
+        + [
+            jax.ShapeDtypeStruct((CAP + wanted.shape[1],), jnp.int32),
+            jax.ShapeDtypeStruct((n_store,), jnp.int32),
+        ],
+        in_specs=[ANY, ANY, HBM],
+        out_specs=[ANY] * n_store + [SMEM, SMEM],
         scratch_shapes=[
             pltpu.SMEM(slots.shape, slots.dtype),
             pltpu.SMEM(wanted.shape, wanted.dtype),
-            pltpu.VMEM((2 * n_store,) + down.shape[1:], down.dtype),
+            pltpu.VMEM((n_store,) + down.shape[1:], down.dtype),
             pltpu.SemaphoreType.DMA((2,)),
-            pltpu.SemaphoreType.DMA((2 * n_store,)),
-            pltpu.SemaphoreType.DMA((2 * n_store,)),
+            pltpu.SemaphoreType.DMA((n_store,)),
+            pltpu.SemaphoreType.DMA((n_store,)),
         ],
-        compiler_params=params(60),
+        compiler_params=params(62),
         cost_estimate=SMALL,
         name="pick",
-    )(slots, wanted, down, up)
+    )(slots, wanted, down)
 
 
 def stack_kernel(count, *refs):
     o_ref = refs[-1]
+    slabs = refs[-1 - count : -1]
     for number in range(count):
-        o_ref[number] = refs[number][...]
+        o_ref[number] = slabs[number][...]
 
 
 def stack(slabs, *earlier):
     return pl.pallas_call(
         functools.partial(stack_kernel, len(slabs)),
         out_shape=jax.ShapeDtypeStruct((len(slabs),) + slabs[0].shape, slabs[0].dtype),
-        in_specs=[VMEM] * len(slabs) + [ANY] * len(earlier),
+        in_specs=[ANY] * len(earlier) + [VMEM] * len(slabs),
         out_specs=VMEM,
         compiler_params=params(8),
         cost_estimate=SMALL,
         name="stack",
-    )(*slabs, *earlier)
+    )(*earlier, *slabs)
 
 
 def tie_kernel(*refs):
@@ -220,7 +216,7 @@
     return jobs
 
 
-def project_rows(x, stream, held, made, outs, sems):
+def project_rows(x, stream, held, made, outs, sems, others=()):
     width, tile = made.shape[2], held.shape[2]
     steps = width // tile
     copies = []
@@ -232,12 +228,17 @@
         copy = pltpu.make_async_copy(made.at[block], out, sems.at[block])
         copy.start()
         copies.append(copy)
+    for other in others:
+        other.wait()
     return copies
 
 
-def front_kernel(n_chip, slot_count, length, chunk, lengths_in, q_in, k_in, v_in, w_in, *refs):
-    flag, attended, other, own = refs[-15:-11]
-    lengths, q, k, v, w, x, made, lengths_sem, qkv_sem, w_sem, out_sem = refs[-11:]
+def front_kernel(
+    n_chip, n_store, slot_count, length, chunk, sends_in, lengths_in, q_in, k_in, v_in, w_in, up_in, *refs
+):
+    flag, attended, other, own = refs[:4]
+    *singles, pair = refs[4 : 5 + n_store - CAP]
+    sends, lengths, q, k, v, w, up, x, made, table_sem, qkv_sem, w_sem, up_sem, out_sem = refs[-14:]
     rows, width = q.shape[0], made.shape[2]
     per_row = slot_count * length
     jobs = []
@@ -251,7 +252,8 @@
                 pltpu.make_async_copy(source.at[span], held.at[span], qkv_sem.at[part, number])
             )
         jobs.append(job)
-    jobs[0].append(pltpu.make_async_copy(lengths_in, lengths, lengths_sem.at[0]))
+    jobs[0].append(pltpu.make_async_copy(lengths_in, lengths, table_sem.at[0]))
+    jobs[0].append(pltpu.make_async_copy(sends_in, sends, table_sem.at[1]))
     stream = Stream(
         jobs + weight_columns(1, n_chip, width, w.shape[2], w_in, w, w_sem), AHEAD
     )
@@ -267,14 +269,26 @@
         stream.take()
         attend_rows(part * chunk, chunk, lengths, q, k, v, x, slot_count, length, offset, row)
     flag[0] = lengths[0]
+    slabs = []
+    for slot in range(n_store):
+        slab = pltpu.make_async_copy(up_in.at[sends[slot]], up.at[slot], up_sem.at[slot])
+        slab.start()
+        slabs.append(slab)
     copies = [pltpu.make_async_copy(x, attended, out_sem.at[2])]
     copies[0].start()
-    copies += project_rows(x, stream, w, made, (other, own), out_sem)
+    copies += project_rows(x, stream, w, made, (other, own), out_sem, slabs)
+    targets = list(singles) + [pair.at[rank] for rank in range(CAP)]
+    for slot, target in enumerate(targets):
+        copies.append(pltpu.make_async_copy(up.at[slot], target, up_sem.at[slot]))
+        copies[-1].start()
     for copy in copies:
         copy.wait()
 
 
-def front(n_chip, lengths, queries, keys, values, weight, width, *earlier):
+def front(n_chip, n_store, sends, lengths, queries, keys, values, weight, up):
+    width = up.shape[2]
+    slab = jax.ShapeDtypeStruct(up.shape[1:], up.dtype)
+    pair = jax.ShapeDtypeStruct((CAP,) + up.shape[1:], up.dtype)
     rows, slot_count, length, head = keys.shape
     depth = queries.shape[1]
     tile = min(512, width)
@@ -282,38 +296,44 @@
     chunk = min(CHUNK, rows)
     half = jax.ShapeDtypeStruct((rows, width), jnp.bfloat16)
     return pl.pallas_call(
-        functools.partial(front_kernel, n_chip, slot_count, length, chunk),
+        functools.partial(front_kernel, n_chip, n_store, slot_count, length, chunk),
         out_shape=[
             jax.ShapeDtypeStruct((1,), jnp.int32),
             jax.ShapeDtypeStruct((rows, depth), jnp.bfloat16),
             half,
             half,
-        ],
-        in_specs=[ANY] + [HBM] * 4 + [ANY] * len(earlier),
-        out_specs=[SMEM] + [ANY] * 3,
+        ]
+        + [slab] * (n_store - CAP)
+        + [pair],
+        in_specs=[ANY] * 2 + [HBM] * 5,
+        out_specs=[SMEM] + [ANY] * (4 + n_store - CAP),
         scratch_shapes=[
+            pltpu.SMEM(sends.shape, sends.dtype),
             pltpu.SMEM(lengths.shape, lengths.dtype),
             pltpu.VMEM((rows, depth), queries.dtype),
             pltpu.VMEM((rows * slot_count * length, head), keys.dtype),
             pltpu.VMEM((rows * slot_count * length, head), values.dtype),
             pltpu.VMEM((tiles, depth, tile), weight.dtype),
+            pltpu.VMEM((n_store,) + up.shape[1:], up.dtype),
             pltpu.VMEM((rows, depth), jnp.bfloat16),
             pltpu.VMEM((2, rows, width), jnp.bfloat16),
-            pltpu.SemaphoreType.DMA((1,)),
+            pltpu.SemaphoreType.DMA((2,)),
             pltpu.SemaphoreType.DMA((rows // chunk, 3)),
             pltpu.SemaphoreType.DMA((tiles,)),
+            pltpu.SemaphoreType.DMA((n_store,)),
             pltpu.SemaphoreType.DMA((3,)),
         ],
         compiler_params=params(58),
         cost_estimate=SMALL,
         name="front",
     )(
+        sends,
         lengths,
         queries,
         keys.reshape(-1, head),
         values.reshape(-1, head),
         weight,
-        *earlier,
+        up,
     )
 
 
@@ -342,7 +362,7 @@
             pltpu.SemaphoreType.DMA((tiles,)),
             pltpu.SemaphoreType.DMA((2,)),
         ],
-        compiler_params=params(32),
+        compiler_params=params(26),
         cost_estimate=SMALL,
         name="project",
     )(attended, weight, *earlier)
@@ -392,7 +412,7 @@
             pltpu.VMEM((CAP, size, width), near.dtype),
             pltpu.SemaphoreType.DMA((CAP,)),
         ],
-        compiler_params=params(24),
+        compiler_params=params(14),
         cost_estimate=SMALL,
         name="shrink",
     )(info, entries, attended, near, *slabs, *earlier)
@@ -401,7 +421,7 @@
 def spread_kernel(slot_total, info, entries_ref, parts_ref, *refs):
     o_ref = refs[-1]
     place = place_row(info, entries_ref[...])
-    low = jnp.sum(parts_ref[...], axis=0).astype(jnp.bfloat16).astype(jnp.float32)
+    low = jnp.sum(parts_ref[...].astype(jnp.float32), axis=0).astype(jnp.bfloat16).astype(jnp.float32)
     wide = jnp.concatenate(
         [jnp.where(place == slot, low, 0.0) for slot in range(slot_total)], axis=0
     )
@@ -416,7 +436,7 @@
         in_specs=[SMEM, VMEM, VMEM] + [ANY] * len(earlier),
         out_specs=VMEM,
         compiler_params=params(12),
-        cost_estimate=SMALL,
+        cost_estimate=pl.CostEstimate(flops=1, bytes_accessed=8000000, transcendentals=0),
         name="spread",
     )(info, entries, parts, *earlier)
 
@@ -459,30 +479,45 @@
             pltpu.VMEM((CAP,) + near.shape[1:], near.dtype),
             pltpu.SemaphoreType.DMA((CAP,)),
         ],
-        compiler_params=params(24),
+        compiler_params=params(14),
         cost_estimate=SMALL,
         name="expand",
     )(info, wide, near, *slabs, *flat, *earlier)
 
 
 def finish_kernel(wide_ref, total_ref, *refs):
-    slab_refs, o_ref = refs[:-1], refs[-1]
-    slabs = jnp.concatenate([ref[...] for ref in slab_refs], axis=0)
-    first = wide_ref.shape[1] - slabs.shape[0]
-    delta = jnp.dot(wide_ref[:, first:], slabs, preferred_element_type=jnp.float32)
-    o_ref[...] = (total_ref[...] + delta).astype(o_ref.dtype)
-
-
-def finish(wide, total, slabs):
+    slab_ref, o_ref, made, sems = refs
+    first = wide_ref.shape[1] - slab_ref.shape[0]
+    width = made.shape[1]
+    tile = min(512, width)
+    copies = []
+    for number in range(width // tile):
+        span = pl.ds(number * tile, tile)
+        delta = jnp.dot(
+            wide_ref[:, first:], slab_ref[:, span], preferred_element_type=jnp.float32
+        )
+        made[:, span] = (total_ref[:, span] + delta).astype(made.dtype)
+        copies.append(pltpu.make_async_copy(made.at[:, span], o_ref.at[:, span], sems.at[number]))
+        copies[-1].start()
+    for copy in copies:
+        copy.wait()
+
+
+def finish(wide, total, slab):
+    width = total.shape[1]
     return pl.pallas_call(
         finish_kernel,
         out_shape=jax.ShapeDtypeStruct(total.shape, jnp.bfloat16),
-        in_specs=[VMEM] * (2 + len(slabs)),
-        out_specs=VMEM,
-        compiler_params=params(24),
+        in_specs=[VMEM] * 3,
+        out_specs=ANY,
+        scratch_shapes=[
+            pltpu.VMEM(total.shape, jnp.bfloat16),
+            pltpu.SemaphoreType.DMA((width // min(512, width),)),
+        ],
+        compiler_params=params(14),
         cost_estimate=SMALL,
         name="finish",
-    )(wide, total, *slabs)
+    )(wide, total, slab)
 
 
 def shards(
@@ -516,22 +551,20 @@
         return lax.ppermute(x, "tensor", [(t, (t + 2 * step) % n_tensor) for t in range(n_tensor)])
 
     weight = output_projection_weight
-    *picked, send_pair, info = pick(
-        adapter_storage_slot, wanted, adapter_shrink_weight, adapter_expand_weight
-    )
+    *picked, info, sends = pick(adapter_storage_slot, wanted, adapter_shrink_weight)
     steps = range(CAP, n_store)
+    next_down = [along_store(x, 1) for x in picked[len(steps) : n_store]]
     own_down = [along_store(x, step) for step, x in zip(steps, picked)]
-    next_down = [along_store(x, 1) for x in picked[len(steps) : n_store]]
-    send_up = picked[n_store:]
-    flag, attended, other, own = front(
+    flag, attended, other, own, *send_up, send_pair = front(
         n_chip,
+        n_store,
+        sends,
         request_cache_lengths,
         queries,
         cached_key_slabs,
         cached_value_slabs,
         weight,
-        local_width,
-        info,
+        adapter_expand_weight,
     )
 
     def meet(mine, given):
@@ -552,7 +585,7 @@
         arrived.append([along_chip(met, step)])
     own_up = [along_store(tie(x, met), step) for step, x in zip(steps, send_up)]
     next_up = along_store(tie(send_pair, met), 1)
-    own_down = stack(own_down, met, *next_down)
+    own_down = tie(stack(own_down, met), *next_down)
     swapped_down = swap_group(own_down)
     other, own = project(0, n_chip, attended, weight, local_width, met)
 
@@ -567,7 +600,7 @@
             [*next_down, own_down, swapped_down],
         )
         base = meet(own, given) if first else meet(given, own)
-        return base, swapped, lax.all_gather(part, "tensor")
+        return base, swapped, lax.all_gather(part.astype(jnp.bfloat16), "tensor")
 
     base, swapped_up, gathered = lax.cond(
         flag[0] > 0, lambda: middle(True), lambda: middle(False)
@@ -582,7 +615,7 @@
         [next_up] + own_up[:-1] + [last] + swapped_up,
         [[base]] + arrived,
     )
-    return finish(wide, total, [swapped])
+    return finish(wide, total, swapped)
 
 
 def solution(mesh):

time: 70 us -> 67.2 us (0.960)
  waiting for transfers between devices: 9.69 us -> 11.6 us
  blocking collectives: 7.28 us -> 5.43 us
  Pallas kernels: 32.1 us -> 30.6 us
  local copies, waits for them, and re-layouts: 1.02 us -> 0.03 us
  starting transfers between devices: 17.3 us -> 16.4 us
    ppermute x7, waiting for transfers between devices: 2.2 us -> 5.23 us  [along_store(): return lax.ppermute(x, 'store', [(s, s ^ step) for s in range(n_store)])]
    all_gather x1, blocking collectives: 7.28 us -> 5.43 us  [middle(): return (base, swapped, lax.all_gather(part.astype(jnp.bfloat16), 'tensor'))]
    pallas_call x2, Pallas kernels: 17.7 us -> 16.5 us  [the longest x1 13.1 us: front(): pl.pallas_call(functools.partial(front_kernel, n_chip, n_store, slot_coun...]
    ppermute x3, waiting for transfers between devices: 4.83 us -> 3.73 us  [swap_group(): return lax.ppermute(x, 'group', [(0, 1), (1, 0)])]
    unnamed x20 -> x16, local copies, waits for them, and re-layouts: 1.02 us -> 0.03 us
  transfers between devices with their start and end apart: 13 -> 13, of which waited for: 4 -> 7; matrix products, arithmetic and copies ran while one was open for 2% -> 3% of each run, Pallas kernels for 38% -> 39%
where the time goes in v3:
time: 67.2 us; the launch traced here: 67 us
  Pallas kernels  30.6 us (46%)
  starting transfers between devices  16.4 us (24%)
  waiting for transfers between devices  11.6 us (17%)
  blocking collectives  5.43 us (8%)
  other arithmetic  1.75 us (3%)
  between operations  0.9 us (1%)
    pallas_call x1, Pallas kernels, front(): pl.pallas_call(functools.partial(front_kernel, n_chip, n_store, slot_coun...  13.1 us
    ppermute x7, starting transfers between devices, along_store(): return lax.ppermute(x, 'store', [(s, s ^ step) for s in range(n_store)])  11.9 us
    pallas_call x1, Pallas kernels, project(): pl.pallas_call(functools.partial(project_kernel, step, n_chip), out_shape...  7.67 us
    all_gather x1, blocking collectives, middle(): return (base, swapped, lax.all_gather(part.astype(jnp.bfloat16), 'tensor'))  5.43 us
    ppermute x7, waiting for transfers between devices, along_store(): return lax.ppermute(x, 'store', [(s, s ^ step) for s in range(n_store)])  5.23 us
    ppermute x3, waiting for transfers between devices, swap_group(): return lax.ppermute(x, 'group', [(0, 1), (1, 0)])  3.73 us
    pallas_call x1, Pallas kernels, pick(): pl.pallas_call(functools.partial(pick_kernel, n_store), out_shape=[slab]...  3.45 us
    ppermute x3, starting transfers between devices, swap_group(): return lax.ppermute(x, 'group', [(0, 1), (1, 0)])  2.85 us
  transfers between devices with their start and end apart: 13, of which 7 were waited for; matrix products, arithmetic and copies ran while one was open for 3% of the time, Pallas kernels for 39%

profile of v3, /device:TPU:0, one launch (start us, length us, event | category | flops | bytes accessed | tf_op | source)
XLA Modules:
  0.0 67.0 jit_solution(3004692150547582356)
XLA Ops:
  0.0 3.4 %pick.1 = (bf16[64,2048]{1,0:T(8,128)(2,1)}, bf16[64,2048]{1,0:T(8,128)(2,1)}, bf16[64,2048]{1,0:T(8,128)(2,1)}, bf16[64,2048]{1,0:T(8,128)(2,1)}, s32[10]{0:T(128)S(1)}, /*index=5*/s32[4]{0:T(128)}) custom-call(s32[32]{0:T(128)} %slots_in.1, s32[4,8]{1,0:T(4,128)} %wanted_in.1, bf16[8,64,2048]{2,1,0:T(8,128)(2,1)} %down.1), custom_call_target="tpu_custom_call" | custom-call | flops 1 | bytes 1 | tf_op jit(solution)/shard_map/pick/pallas_call | solution.py:89
  3.5 3.1 %collective-permute-start.7 = (bf16[64,2048]{1,0:T(8,128)(2,1)}, bf16[64,2048]{1,0:T(8,128)(2,1)S(1)}, u32[]{:S(2)}, u32[]{:S(2)}) collective-permute-start(bf16[64,2048]{1,0:T(8,128)(2,1)} %get-tuple-element.127), channel_id=1, source_target_pairs={{0,4},{4,0},{8,12},{12,8},{1,5},{5,1},{9,13},{13,9},{2,6},{6,2},{1... | collective-permute-start | bytes 786440 | tf_op jit(solution)/shard_map/ppermute | solution.py:542
  6.5 0.1 collective-permute-start.8
  6.6 3.0 %collective-permute-start.9 = (bf16[64,2048]{1,0:T(8,128)(2,1)}, bf16[64,2048]{1,0:T(8,128)(2,1)S(1)}, u32[]{:S(2)}, u32[]{:S(2)}) collective-permute-start(bf16[64,2048]{1,0:T(8,128)(2,1)} %get-tuple-element.129), channel_id=1, source_target_pairs={{0,8},{4,12},{8,0},{12,4},{1,9},{5,13},{9,1},{13,5},{2,10},{6,14},... | collective-permute-start | bytes 786440 | tf_op jit(solution)/shard_map/ppermute | solution.py:542
  9.6 1.3 %collective-permute-start.10 = (bf16[64,2048]{1,0:T(8,128)(2,1)}, bf16[64,2048]{1,0:T(8,128)(2,1)S(1)}, u32[]{:S(2)}, u32[]{:S(2)}) collective-permute-start(bf16[64,2048]{1,0:T(8,128)(2,1)} %get-tuple-element.130), channel_id=1, source_target_pairs={{0,12},{4,8},{8,4},{12,0},{1,13},{5,9},{9,5},{13,1},{2,14},{6,10},... | collective-permute-start | bytes 786440 | tf_op jit(solution)/shard_map/ppermute | solution.py:542
  10.9 13.1 %front.1 = (s32[1]{0:T(128)}, bf16[256,2048]{1,0:T(8,128)(2,1)S(1)}, bf16[256,2048]{1,0:T(8,128)(2,1)S(1)}, bf16[256,2048]{1,0:T(8,128)(2,1)S(1)}, bf16[64,2048]...) custom-call(s32[4]{0:T(128)} %get-tuple-element.121.sends_in, s32[256]{0:T(256)} %lengths_in.1, ...), custom_call_target="tpu_custom_call" | custom-call | flops 1 | bytes 1 | tf_op jit(solution)/shard_map/front/pallas_call | solution.py:298
  24.0 0.0 copy-start.3
  24.6 4.1 %conditional.6 = (bf16[256,2048]{1,0:T(8,128)(2,1)}) conditional(s32[]{:T(128)} %bitcast.4, (bf16[256,2048]{1,0:T(8,128)(2,1)S(1)}, bf16[256,2048]{1,0:T(8,128)(2,1)S(1)}) %tuple.39, (bf16[256,2048]{1,0:T(8,128)(2,1)S(1)}, bf16[256,2048]{1,0:T(8,128)(2,1)S(1)}) %tuple.40), branch_computations={%region_0.0_spmd, %region_1.0_spmd} | conditional | flops 2097152 | bytes 7340080
  24.7 0.1 collective-permute-start.1
  24.7 2.6 %collective-permute-done.1 = bf16[256,2048]{1,0:T(8,128)(2,1)S(1)} collective-permute-done((bf16[256,2048]{1,0:T(8,128)(2,1)S(1)}, bf16[256,2048]{1,0:T(8,128)(2,1)S(1)}, u32[]{:S(2)}, u32[]{:S(2)}) %collective-permute-start.1) | collective-permute-done | bytes 1048608 | tf_op jit(solution)/shard_map/cond/branch_1_fun/ppermute | solution.py:548
  27.4 1.4 %add_convert_fusion.1 = bf16[256,2048]{1,0:T(8,128)(2,1)} fusion(bf16[256,2048]{1,0:T(8,128)(2,1)S(1)} %collective-permute-done.1, bf16[256,2048]{1,0:T(8,128)(2,1)S(1)} %get-tuple-element.78), kind=kLoop, calls=%fused_computation.1 | loop fusion | flops 2097152 | bytes 3145728 | tf_op jit(solution)/shard_map/cond/branch_0_fun/convert_element_type | solution.py:571
  28.7 1.5 %collective-permute-start.14 = (bf16[256,2048]{1,0:T(8,128)(2,1)}, bf16[256,2048]{1,0:T(8,128)(2,1)S(1)}, u32[]{:S(2)}, u32[]{:S(2)}) collective-permute-start(bf16[256,2048]{1,0:T(8,128)(2,1)} %get-tuple-element.149.refs_1_.refs_0_), channel_id=1, source_target_pairs={{0,2},{1,3},{2,0},{3,1},{4,6},{5,7},{6,4},{7,5},{8,10},{9,11},{10,... | collective-permute-start | bytes 3145736 | tf_op jit(solution)/shard_map/ppermute | solution.py:551
  30.3 0.0 collective-permute-done.9.refs_1_
  30.3 1.9 %collective-permute-done.10.refs_2_ = bf16[64,2048]{1,0:T(8,128)(2,1)S(1)} collective-permute-done((bf16[64,2048]{1,0:T(8,128)(2,1)}, bf16[64,2048]{1,0:T(8,128)(2,1)S(1)}, u32[]{:S(2)}, u32[]{:S(2)}) %collective-permute-start.10) | collective-permute-done | bytes 262176 | tf_op jit(solution)/shard_map/ppermute | solution.py:542
  32.2 0.0 collective-permute-done.7.refs_1_
  32.3 0.0 copy-start.5
  32.3 0.0 collective-permute-done.8.refs_2_
  32.3 1.7 %collective-permute-start.11 = (bf16[2,64,2048]{2,1,0:T(8,128)(2,1)S(1)}, bf16[2,64,2048]{2,1,0:T(8,128)(2,1)S(1)}, u32[]{:S(2)}, u32[]{:S(2)}) collective-permute-start(bf16[2,64,2048]{2,1,0:T(8,128)(2,1)S(1)} %tie.6), channel_id=1, source_target_pairs={{0,16},{16,0},{1,17},{17,1},{2,18},{18,2},{3,19},{19,3},{4,20},{20... | collective-permute-start | bytes 1572872 | tf_op jit(solution)/shard_map/ppermute | solution.py:545
  34.0 0.0 copy-done.1
  34.0 2.8 %collective-permute-start.6 = (bf16[64,2048]{1,0:T(8,128)(2,1)S(1)}, bf16[64,2048]{1,0:T(8,128)(2,1)}, u32[]{:S(2)}, u32[]{:S(2)}) collective-permute-start(bf16[64,2048]{1,0:T(8,128)(2,1)S(1)} %tie.5), channel_id=1, source_target_pairs={{0,8},{4,12},{8,0},{12,4},{1,9},{5,13},{9,1},{13,5},{2,10},{6,14},... | collective-permute-start | bytes 786440 | tf_op jit(solution)/shard_map/ppermute | solution.py:542
  36.8 0.0 copy-done.5
  36.8 0.0 collective-permute-start.12
  36.8 1.6 %collective-permute-start.13 = (bf16[64,2048]{1,0:T(8,128)(2,1)}, bf16[64,2048]{1,0:T(8,128)(2,1)S(1)}, u32[]{:S(2)}, u32[]{:S(2)}) collective-permute-start(bf16[64,2048]{1,0:T(8,128)(2,1)} %tie.8), channel_id=1, source_target_pairs={{0,12},{4,8},{8,4},{12,0},{1,13},{5,9},{9,5},{13,1},{2,14},{6,10},... | collective-permute-start | bytes 786440 | tf_op jit(solution)/shard_map/ppermute | solution.py:542
  38.4 0.0 copy-done.3
  38.4 7.7 %project.1 = (bf16[256,2048]{1,0:T(8,128)(2,1)S(1)}, bf16[256,2048]{1,0:T(8,128)(2,1)S(1)}) custom-call(bf16[256,2048]{1,0:T(8,128)(2,1)S(1)} %get-tuple-element.126.x, bf16[2048,8192]{1,0:T(8,128)(2,1)} %w_in.3, bf16[256,2048]{1,0:T(8,128)(2,1)} %get-tuple-element.149.refs_1_.refs_0_), custom_call_target="tpu_custom_call" | custom-call | flops 1 | bytes 1 | tf_op jit(solution)/shard_map/project/pallas_call | solution.py:354
  46.1 1.3 %collective-permute-done.6.refs_1_ = bf16[64,2048]{1,0:T(8,128)(2,1)} collective-permute-done((bf16[64,2048]{1,0:T(8,128)(2,1)S(1)}, bf16[64,2048]{1,0:T(8,128)(2,1)}, u32[]{:S(2)}, u32[]{:S(2)}) %collective-permute-start.6) | collective-permute-done | bytes 262176 | tf_op jit(solution)/shard_map/ppermute | solution.py:542
  47.4 0.0 collective-permute-done.11
  47.4 0.0 copy-done.2
  47.4 0.0 copy-done.6
  47.4 0.0 copy-done.7
  47.4 0.0 copy-start
  47.4 9.3 %conditional.8 = (bf16[64,2048]{1,0:T(8,128)(2,1)}, bf16[4,64,256]{2,1,0:T(8,128)(2,1)S(1)}, bf16[256,2048]{1,0:T(8,128)(2,1)S(1)}) conditional(s32[]{:T(128)} %bitcast.4, (bf16[64,2048]{1,0:T(8,128)(2,1)}, s32[10]{0:T(128)S(1)}, s32[1,256]{1,0:T(1,128)S(1)}, bf16[256,2048]{1,0:T(8,128)(2,1)}, bf16[8,64,2048]{2,1,0:T(8,128)(2,1)S(1)}, ...), branch_computations={%region_2.0_spmd, %region_3.0_spmd} | conditional | flops 2113537 | bytes 8650857
  47.6 0.1 collective-permute-start.5
  47.7 0.6 collective-permute-start.4
  48.3 2.1 %shrink.3 = f32[64,256]{1,0:T(8,128)S(1)} custom-call(s32[10]{0:T(128)S(1)} %get-tuple-element.92.info, s32[1,256]{1,0:T(1,128)S(1)} %get-tuple-element.93.entries_ref, bf16[256,2048]{1,0:T(8,128)(2,1)} %get-tuple-element.94.x_ref, bf16[8,64,2048]{2,1,0:T(8,128)(2,1)S(1)} %get-tuple-element.95.near_ref, bf16[64,2048]{1,0:T(8,128)(2,1)S(1)} %get-tuple-element.96.refs_0_, ...), custom_call_target="tpu_custom_call" | custom-call | flops 1 | bytes 1 | tf_op jit(solution)/shard_map/cond/branch_1_fun/shrink/pallas_call | solution.py:406
  50.4 5.4 %all-gather.1 = bf16[256,256]{1,0:T(8,128)(2,1)S(1)} all-gather(bf16[64,256]{1,0:T(8,128)(2,1)S(1)} %convert_element_type.55), channel_id=3, replica_groups=mesh['group'=2,'store'=4,'tensor'=4] {'tensor'}, dimensions={0}, use_global_device_ids=true | all-gather | bytes 163840 | tf_op jit(solution)/shard_map/cond/branch_1_fun/all_gather | solution.py:603
  55.8 0.0 collective-permute-done.5
  55.8 0.4 add_convert_fusion.3
  56.2 0.5 collective-permute-done.4
  56.7 0.7 %spread.1.refs_1_.wide_ref = bf16[256,512]{1,0:T(8,128)(2,1)S(1)} custom-call(s32[10]{0:T(128)S(1)} %get-tuple-element.120.info, s32[1,256]{1,0:T(1,128)S(1)} %copy-done.7, bf16[4,64,256]{2,1,0:T(8,128)(2,1)S(1)} %get-tuple-element.133.parts_ref), custom_call_target="tpu_custom_call" | custom-call | flops 1 | bytes 8000000 | tf_op jit(solution)/shard_map/spread/pallas_call | solution.py:433
  57.4 1.1 %collective-permute-done.13.refs_0_ = bf16[64,2048]{1,0:T(8,128)(2,1)S(1)} collective-permute-done((bf16[64,2048]{1,0:T(8,128)(2,1)}, bf16[64,2048]{1,0:T(8,128)(2,1)S(1)}, u32[]{:S(2)}, u32[]{:S(2)}) %collective-permute-start.13) | collective-permute-done | bytes 262176 | tf_op jit(solution)/shard_map/ppermute | solution.py:542
  58.5 0.5 collective-permute-start.15
  59.1 0.9 %collective-permute-done.12.refs_0_ = bf16[2,64,2048]{2,1,0:T(8,128)(2,1)} collective-permute-done((bf16[2,64,2048]{2,1,0:T(8,128)(2,1)}, bf16[2,64,2048]{2,1,0:T(8,128)(2,1)}, u32[]{:S(2)}, u32[]{:S(2)}) %collective-permute-start.12) | collective-permute-done | bytes 524320 | tf_op jit(solution)/shard_map/ppermute | solution.py:542
  60.0 0.0 collective-permute-done.14.refs_5_
  60.0 0.0 copy-done.4
  60.0 2.4 %expand.1.total_ref = f32[256,2048]{1,0:T(8,128)S(1)} custom-call(s32[10]{0:T(128)S(1)} %get-tuple-element.120.info, bf16[256,512]{1,0:T(8,128)(2,1)S(1)} %spread.1.refs_1_.wide_ref, bf16[8,64,2048]{2,1,0:T(8,128)(2,1)S(1)} %copy-done, bf16[2,64,2048]{2,1,0:T(8,128)(2,1)} %collective-permute-done.12.refs_0_, ...), custom_call_target="tpu_custom_call" | custom-call | flops 1 | bytes 1 | tf_op jit(solution)/shard_map/expand/pallas_call | solution.py:473
  62.3 3.2 %collective-permute-done.15.refs_0_ = bf16[64,2048]{1,0:T(8,128)(2,1)S(1)} collective-permute-done((bf16[64,2048]{1,0:T(8,128)(2,1)S(1)}, bf16[64,2048]{1,0:T(8,128)(2,1)S(1)}, u32[]{:S(2)}, u32[]{:S(2)}) %collective-permute-start.15) | collective-permute-done | bytes 262176 | tf_op jit(solution)/shard_map/ppermute | solution.py:545
  65.6 1.3 %finish.1 = bf16[256,2048]{1,0:T(8,128)(2,1)} custom-call(bf16[256,512]{1,0:T(8,128)(2,1)S(1)} %spread.1.refs_1_.wide_ref, f32[256,2048]{1,0:T(8,128)S(1)} %expand.1.total_ref, bf16[64,2048]{1,0:T(8,128)(2,1)S(1)} %collective-permute-done.15.refs_0_), custom_call_target="tpu_custom_call" | custom-call | flops 1 | bytes 1 | tf_op jit(solution)/shard_map/finish/pallas_call | solution.py:508
  (13 shorter events, 0.1 us)
Async XLA Ops:
  3.5 28.8 %collective-permute-start.7 = (bf16[64,2048]{1,0:T(8,128)(2,1)}, bf16[64,2048]{1,0:T(8,128)(2,1)S(1)}, u32[]{:S(2)}, u32[]{:S(2)}) collective-permute-start(bf16[64,2048]{1,0:T(8,128)(2,1)} %get-tuple-element.127), channel_id=1, source_target_pairs={{0,4},{4,0},{8,12},{12,8},{1,5},{5,1},{9,13},{13,9},{2,6},{6,2},{1... | collective-permute-start | bytes 786440 | tf_op jit(solution)/shard_map/ppermute | solution.py:542
  6.5 25.7 %collective-permute-start.8 = (bf16[64,2048]{1,0:T(8,128)(2,1)}, bf16[64,2048]{1,0:T(8,128)(2,1)}, u32[]{:S(2)}, u32[]{:S(2)}) collective-permute-start(bf16[64,2048]{1,0:T(8,128)(2,1)} %get-tuple-element.128), channel_id=1, source_target_pairs={{0,4},{4,0},{8,12},{12,8},{1,5},{5,1},{9,13},{13,9},{2,6},{6,2},{1... | collective-permute-start | bytes 786440 | tf_op jit(solution)/shard_map/ppermute | solution.py:542
  6.6 23.6 %collective-permute-start.9 = (bf16[64,2048]{1,0:T(8,128)(2,1)}, bf16[64,2048]{1,0:T(8,128)(2,1)S(1)}, u32[]{:S(2)}, u32[]{:S(2)}) collective-permute-start(bf16[64,2048]{1,0:T(8,128)(2,1)} %get-tuple-element.129), channel_id=1, source_target_pairs={{0,8},{4,12},{8,0},{12,4},{1,9},{5,13},{9,1},{13,5},{2,10},{6,14},... | collective-permute-start | bytes 786440 | tf_op jit(solution)/shard_map/ppermute | solution.py:542
  9.6 22.6 %collective-permute-start.10 = (bf16[64,2048]{1,0:T(8,128)(2,1)}, bf16[64,2048]{1,0:T(8,128)(2,1)S(1)}, u32[]{:S(2)}, u32[]{:S(2)}) collective-permute-start(bf16[64,2048]{1,0:T(8,128)(2,1)} %get-tuple-element.130), channel_id=1, source_target_pairs={{0,12},{4,8},{8,4},{12,0},{1,13},{5,9},{9,5},{13,1},{2,14},{6,10},... | collective-permute-start | bytes 786440 | tf_op jit(solution)/shard_map/ppermute | solution.py:542
  24.0 14.4 %copy-start.3 = (bf16[256,2048]{1,0:T(8,128)(2,1)}, bf16[256,2048]{1,0:T(8,128)(2,1)S(1)}, u32[]{:S(2)}) copy-start(bf16[256,2048]{1,0:T(8,128)(2,1)S(1)} %get-tuple-element.126.x) | copy-start | bytes 3145732
  24.7 2.7 %collective-permute-start.1 = (bf16[256,2048]{1,0:T(8,128)(2,1)S(1)}, bf16[256,2048]{1,0:T(8,128)(2,1)S(1)}, u32[]{:S(2)}, u32[]{:S(2)}) collective-permute-start(bf16[256,2048]{1,0:T(8,128)(2,1)S(1)} %get-tuple-element.79), channel_id=1, source_target_pairs={{0,1},{1,0},{2,3},{3,2},{4,5},{5,4},{6,7},{7,6},{8,9},{9,8},{10,11... | collective-permute-start | bytes 3145736 | tf_op jit(solution)/shard_map/cond/branch_1_fun/ppermute | solution.py:548
  28.7 5.3 %copy-start.1 = (bf16[64,2048]{1,0:T(8,128)(2,1)S(1)}, bf16[64,2048]{1,0:T(8,128)(2,1)}, u32[]{:S(2)}) copy-start(bf16[64,2048]{1,0:T(8,128)(2,1)} %get-tuple-element.123.refs_0_) | copy-start | bytes 786436
  28.7 31.2 %collective-permute-start.14 = (bf16[256,2048]{1,0:T(8,128)(2,1)}, bf16[256,2048]{1,0:T(8,128)(2,1)S(1)}, u32[]{:S(2)}, u32[]{:S(2)}) collective-permute-start(bf16[256,2048]{1,0:T(8,128)(2,1)} %get-tuple-element.149.refs_1_.refs_0_), channel_id=1, source_target_pairs={{0,2},{1,3},{2,0},{3,1},{4,6},{5,7},{6,4},{7,5},{8,10},{9,11},{10,... | collective-permute-start | bytes 3145736 | tf_op jit(solution)/shard_map/ppermute | solution.py:551
  32.3 4.6 %copy-start.5 = (bf16[64,2048]{1,0:T(8,128)(2,1)}, bf16[64,2048]{1,0:T(8,128)(2,1)S(1)}, u32[]{:S(2)}) copy-start(bf16[64,2048]{1,0:T(8,128)(2,1)S(1)} %collective-permute-done.7.refs_1_) | copy-start | bytes 786436
  32.3 15.1 %collective-permute-start.11 = (bf16[2,64,2048]{2,1,0:T(8,128)(2,1)S(1)}, bf16[2,64,2048]{2,1,0:T(8,128)(2,1)S(1)}, u32[]{:S(2)}, u32[]{:S(2)}) collective-permute-start(bf16[2,64,2048]{2,1,0:T(8,128)(2,1)S(1)} %tie.6), channel_id=1, source_target_pairs={{0,16},{16,0},{1,17},{17,1},{2,18},{18,2},{3,19},{19,3},{4,20},{20... | collective-permute-start | bytes 1572872 | tf_op jit(solution)/shard_map/ppermute | solution.py:545
  34.0 13.4 %collective-permute-start.6 = (bf16[64,2048]{1,0:T(8,128)(2,1)S(1)}, bf16[64,2048]{1,0:T(8,128)(2,1)}, u32[]{:S(2)}, u32[]{:S(2)}) collective-permute-start(bf16[64,2048]{1,0:T(8,128)(2,1)S(1)} %tie.5), channel_id=1, source_target_pairs={{0,8},{4,12},{8,0},{12,4},{1,9},{5,13},{9,1},{13,5},{2,10},{6,14},... | collective-permute-start | bytes 786440 | tf_op jit(solution)/shard_map/ppermute | solution.py:542
  36.8 23.1 %collective-permute-start.12 = (bf16[2,64,2048]{2,1,0:T(8,128)(2,1)}, bf16[2,64,2048]{2,1,0:T(8,128)(2,1)}, u32[]{:S(2)}, u32[]{:S(2)}) collective-permute-start(bf16[2,64,2048]{2,1,0:T(8,128)(2,1)} %tie.7), channel_id=1, source_target_pairs={{0,4},{4,0},{8,12},{12,8},{1,5},{5,1},{9,13},{13,9},{2,6},{6,2},{1... | collective-permute-start | bytes 1572872 | tf_op jit(solution)/shard_map/ppermute | solution.py:542
  36.8 21.7 %collective-permute-start.13 = (bf16[64,2048]{1,0:T(8,128)(2,1)}, bf16[64,2048]{1,0:T(8,128)(2,1)S(1)}, u32[]{:S(2)}, u32[]{:S(2)}) collective-permute-start(bf16[64,2048]{1,0:T(8,128)(2,1)} %tie.8), channel_id=1, source_target_pairs={{0,12},{4,8},{8,4},{12,0},{1,13},{5,9},{9,5},{13,1},{2,14},{6,10},... | collective-permute-start | bytes 786440 | tf_op jit(solution)/shard_map/ppermute | solution.py:542
  38.4 9.0 %copy-start.2 = (bf16[8,64,2048]{2,1,0:T(8,128)(2,1)S(1)}, bf16[8,64,2048]{2,1,0:T(8,128)(2,1)}, u32[]{:S(2)}) copy-start(bf16[8,64,2048]{2,1,0:T(8,128)(2,1)} %down.1) | copy-start | bytes 6291460
  38.4 9.0 %copy-start.6 = (bf16[64,2048]{1,0:T(8,128)(2,1)S(1)}, bf16[64,2048]{1,0:T(8,128)(2,1)}, u32[]{:S(2)}) copy-start(bf16[64,2048]{1,0:T(8,128)(2,1)} %copy-done.5) | copy-start | bytes 786436
  38.4 9.0 %copy-start.7 = (s32[1,256]{1,0:T(1,128)S(1)}, s32[1,256]{1,0:T(1,128)}, u32[]{:S(2)}) copy-start(s32[1,256]{1,0:T(1,128)} %entries_ref.1) | copy-start | bytes 3076
  47.4 12.6 %copy-start = (bf16[8,64,2048]{2,1,0:T(8,128)(2,1)S(1)}, bf16[8,64,2048]{2,1,0:T(8,128)(2,1)}, u32[]{:S(2)}) copy-start(bf16[8,64,2048]{2,1,0:T(8,128)(2,1)} %near_ref.1) | copy-start | bytes 6291460
  47.6 8.2 %collective-permute-start.5 = (bf16[256,2048]{1,0:T(8,128)(2,1)S(1)}, bf16[256,2048]{1,0:T(8,128)(2,1)S(1)}, u32[]{:S(2)}, u32[]{:S(2)}) collective-permute-start(bf16[256,2048]{1,0:T(8,128)(2,1)S(1)} %get-tuple-element.101), channel_id=1, source_target_pairs={{0,1},{1,0},{2,3},{3,2},{4,5},{5,4},{6,7},{7,6},{8,9},{9,8},{10,11... | collective-permute-start | bytes 3145736 | tf_op jit(solution)/shard_map/cond/branch_1_fun/ppermute | solution.py:548
  47.7 9.0 %collective-permute-start.4 = (bf16[64,2048]{1,0:T(8,128)(2,1)}, bf16[64,2048]{1,0:T(8,128)(2,1)}, u32[]{:S(2)}, u32[]{:S(2)}) collective-permute-start(bf16[64,2048]{1,0:T(8,128)(2,1)} %get-tuple-element.91), channel_id=1, source_target_pairs={{0,16},{16,0},{1,17},{17,1},{2,18},{18,2},{3,19},{19,3},{4,20},{20... | collective-permute-start | bytes 786440 | tf_op jit(solution)/shard_map/cond/branch_1_fun/ppermute | solution.py:545
  56.7 3.2 %copy-start.4 = (bf16[256,2048]{1,0:T(8,128)(2,1)}, bf16[256,2048]{1,0:T(8,128)(2,1)S(1)}, u32[]{:S(2)}) copy-start(bf16[256,2048]{1,0:T(8,128)(2,1)S(1)} %get-tuple-element.142.refs_4_) | copy-start | bytes 3145732
  58.5 7.0 %collective-permute-start.15 = (bf16[64,2048]{1,0:T(8,128)(2,1)S(1)}, bf16[64,2048]{1,0:T(8,128)(2,1)S(1)}, u32[]{:S(2)}, u32[]{:S(2)}) collective-permute-start(bf16[64,2048]{1,0:T(8,128)(2,1)S(1)} %tie.9.refs_2_), channel_id=1, source_target_pairs={{0,16},{16,0},{1,17},{17,1},{2,18},{18,2},{3,19},{19,3},{4,20},{20... | collective-permute-start | bytes 786440 | tf_op jit(solution)/shard_map/ppermute | solution.py:545

commit v4 on v3

--- a/solution.py
+++ b/solution.py
@@ -12,7 +12,7 @@
 ROWS = 8
 MASKED = -1e30
 AHEAD = 4
-CHUNK = 64
+CHUNK = 128
 MIB = 1 << 20
 ANY = pl.BlockSpec(memory_space=pl.ANY)
 HBM = pl.BlockSpec(memory_space=pltpu.HBM)
@@ -65,6 +65,11 @@
         sends[slot] = index
     for rank in range(CAP):
         info[rank] = held_index(slots, wanted, store, store, rank, per_store)
+    copies = []
+    for slot, target in enumerate(outs):
+        fetches[slot].wait()
+        copies.append(pltpu.make_async_copy(held.at[slot], target, out_sem.at[slot]))
+        copies[-1].start()
     used = wanted.shape[1]
     holders = [lax.div(slots[wanted[store, entry]], per_store) for entry in range(used)]
     for entry in range(used):
@@ -74,11 +79,6 @@
         step = store ^ holders[entry]
         far = CAP + step + jnp.where(rank == group, 0, n_store - CAP)
         info[CAP + entry] = jnp.where(step <= 1, step * CAP + rank, far)
-    copies = []
-    for slot, target in enumerate(outs):
-        fetches[slot].wait()
-        copies.append(pltpu.make_async_copy(held.at[slot], target, out_sem.at[slot]))
-        copies[-1].start()
     for copy in copies:
         copy.wait()
 
@@ -605,7 +605,7 @@
     base, swapped_up, gathered = lax.cond(
         flag[0] > 0, lambda: middle(True), lambda: middle(False)
     )
-    wide = spread(info, request_wanted_entry, gathered, n_store * CAP)
+    wide = spread(info, request_wanted_entry, gathered, n_store * CAP, own_up[-1])
     last = tie(own_up[-1], wide)
     swapped = swap_group(last)
     total = expand(

time: 67.2 us -> 67.3 us (level)
  transfers between devices with their start and end apart: 13 -> 13, of which waited for: 7 -> 7; matrix products, arithmetic and copies ran while one was open for 3% -> 3% of each run, Pallas kernels for 39% -> 38%
where the time goes in v4:
time: 67.3 us; the launch traced here: 67 us
  Pallas kernels  30.5 us (45%)
  starting transfers between devices  16.1 us (24%)
  waiting for transfers between devices  12.1 us (18%)
  blocking collectives  5.43 us (8%)
  other arithmetic  1.75 us (3%)
  between operations  0.84 us (1%)
    pallas_call x1, Pallas kernels, front(): pl.pallas_call(functools.partial(front_kernel, n_chip, n_store, slot_coun...  12.8 us
    ppermute x7, starting transfers between devices, along_store(): return lax.ppermute(x, 'store', [(s, s ^ step) for s in range(n_store)])  11.8 us
    pallas_call x1, Pallas kernels, project(): pl.pallas_call(functools.partial(project_kernel, step, n_chip), out_shape...  7.65 us
    ppermute x7, waiting for transfers between devices, along_store(): return lax.ppermute(x, 'store', [(s, s ^ step) for s in range(n_store)])  5.69 us
    all_gather x1, blocking collectives, middle(): return (base, swapped, lax.all_gather(part.astype(jnp.bfloat16), 'tensor'))  5.43 us
    ppermute x3, waiting for transfers between devices, swap_group(): return lax.ppermute(x, 'group', [(0, 1), (1, 0)])  3.77 us
    pallas_call x1, Pallas kernels, pick(): pl.pallas_call(functools.partial(pick_kernel, n_store), out_shape=[slab]...  3.54 us
    ppermute x2, waiting for transfers between devices, swap_core(): return lax.ppermute(x, 'tensor', [(t, t ^ 1) for t in range(n_tensor)])  2.65 us
  transfers between devices with their start and end apart: 13, of which 7 were waited for; matrix products, arithmetic and copies ran while one was open for 3% of the time, Pallas kernels for 38%

profile of v4, /device:TPU:0, one launch (start us, length us, event | category | flops | bytes accessed | tf_op | source)
XLA Modules:
  0.0 67.0 jit_solution(14535093773818678885)
XLA Ops:
  0.0 3.5 %pick.1 = (bf16[64,2048]{1,0:T(8,128)(2,1)}, bf16[64,2048]{1,0:T(8,128)(2,1)}, bf16[64,2048]{1,0:T(8,128)(2,1)}, bf16[64,2048]{1,0:T(8,128)(2,1)}, s32[10]{0:T(128)S(1)}, /*index=5*/s32[4]{0:T(128)}) custom-call(s32[32]{0:T(128)} %slots_in.1, s32[4,8]{1,0:T(4,128)} %wanted_in.1, bf16[8,64,2048]{2,1,0:T(8,128)(2,1)} %down.1), custom_call_target="tpu_custom_call" | custom-call | flops 1 | bytes 1 | tf_op jit(solution)/shard_map/pick/pallas_call | solution.py:89
  3.5 2.9 %collective-permute-start.7 = (bf16[64,2048]{1,0:T(8,128)(2,1)}, bf16[64,2048]{1,0:T(8,128)(2,1)}, u32[]{:S(2)}, u32[]{:S(2)}) collective-permute-start(bf16[64,2048]{1,0:T(8,128)(2,1)} %get-tuple-element.127), channel_id=1, source_target_pairs={{0,4},{4,0},{8,12},{12,8},{1,5},{5,1},{9,13},{13,9},{2,6},{6,2},{1... | collective-permute-start | bytes 786440 | tf_op jit(solution)/shard_map/ppermute | solution.py:542
  6.5 0.1 collective-permute-start.8
  6.6 3.1 %collective-permute-start.9 = (bf16[64,2048]{1,0:T(8,128)(2,1)}, bf16[64,2048]{1,0:T(8,128)(2,1)S(1)}, u32[]{:S(2)}, u32[]{:S(2)}) collective-permute-start(bf16[64,2048]{1,0:T(8,128)(2,1)} %get-tuple-element.129), channel_id=1, source_target_pairs={{0,8},{4,12},{8,0},{12,4},{1,9},{5,13},{9,1},{13,5},{2,10},{6,14},... | collective-permute-start | bytes 786440 | tf_op jit(solution)/shard_map/ppermute | solution.py:542
  9.6 1.2 %collective-permute-start.10 = (bf16[64,2048]{1,0:T(8,128)(2,1)}, bf16[64,2048]{1,0:T(8,128)(2,1)S(1)}, u32[]{:S(2)}, u32[]{:S(2)}) collective-permute-start(bf16[64,2048]{1,0:T(8,128)(2,1)} %get-tuple-element.130), channel_id=1, source_target_pairs={{0,12},{4,8},{8,4},{12,0},{1,13},{5,9},{9,5},{13,1},{2,14},{6,10},... | collective-permute-start | bytes 786440 | tf_op jit(solution)/shard_map/ppermute | solution.py:542
  10.9 12.8 %front.1 = (s32[1]{0:T(128)}, bf16[256,2048]{1,0:T(8,128)(2,1)S(1)}, bf16[256,2048]{1,0:T(8,128)(2,1)S(1)}, bf16[256,2048]{1,0:T(8,128)(2,1)S(1)}, bf16[64,2048]...) custom-call(s32[4]{0:T(128)} %get-tuple-element.121.sends_in, s32[256]{0:T(256)} %lengths_in.1, ...), custom_call_target="tpu_custom_call" | custom-call | flops 1 | bytes 1 | tf_op jit(solution)/shard_map/front/pallas_call | solution.py:298
  23.7 0.0 copy-start.3
  24.2 4.1 %conditional.6 = (bf16[256,2048]{1,0:T(8,128)(2,1)}) conditional(s32[]{:T(128)} %bitcast.4, (bf16[256,2048]{1,0:T(8,128)(2,1)S(1)}, bf16[256,2048]{1,0:T(8,128)(2,1)S(1)}) %tuple.39, (bf16[256,2048]{1,0:T(8,128)(2,1)S(1)}, bf16[256,2048]{1,0:T(8,128)(2,1)S(1)}) %tuple.40), branch_computations={%region_0.0_spmd, %region_1.0_spmd} | conditional | flops 2097152 | bytes 7340080
  24.3 0.1 collective-permute-start.1
  24.3 2.6 %collective-permute-done.1 = bf16[256,2048]{1,0:T(8,128)(2,1)S(1)} collective-permute-done((bf16[256,2048]{1,0:T(8,128)(2,1)S(1)}, bf16[256,2048]{1,0:T(8,128)(2,1)S(1)}, u32[]{:S(2)}, u32[]{:S(2)}) %collective-permute-start.1) | collective-permute-done | bytes 1048608 | tf_op jit(solution)/shard_map/cond/branch_1_fun/ppermute | solution.py:548
  27.0 1.4 %add_convert_fusion.1 = bf16[256,2048]{1,0:T(8,128)(2,1)} fusion(bf16[256,2048]{1,0:T(8,128)(2,1)S(1)} %collective-permute-done.1, bf16[256,2048]{1,0:T(8,128)(2,1)S(1)} %get-tuple-element.78), kind=kLoop, calls=%fused_computation.1 | loop fusion | flops 2097152 | bytes 3145728 | tf_op jit(solution)/shard_map/cond/branch_0_fun/convert_element_type | solution.py:571
  28.3 0.0 copy-start.1
  28.3 1.5 %collective-permute-start.14 = (bf16[256,2048]{1,0:T(8,128)(2,1)}, bf16[256,2048]{1,0:T(8,128)(2,1)S(1)}, u32[]{:S(2)}, u32[]{:S(2)}) collective-permute-start(bf16[256,2048]{1,0:T(8,128)(2,1)} %get-tuple-element.149.refs_1_.refs_0_), channel_id=1, source_target_pairs={{0,2},{1,3},{2,0},{3,1},{4,6},{5,7},{6,4},{7,5},{8,10},{9,11},{10,... | collective-permute-start | bytes 3145736 | tf_op jit(solution)/shard_map/ppermute | solution.py:551
  29.9 0.0 collective-permute-done.9.refs_1_
  29.9 2.4 %collective-permute-done.10.refs_2_ = bf16[64,2048]{1,0:T(8,128)(2,1)S(1)} collective-permute-done((bf16[64,2048]{1,0:T(8,128)(2,1)}, bf16[64,2048]{1,0:T(8,128)(2,1)S(1)}, u32[]{:S(2)}, u32[]{:S(2)}) %collective-permute-start.10) | collective-permute-done | bytes 262176 | tf_op jit(solution)/shard_map/ppermute | solution.py:542
  32.3 0.0 collective-permute-done.7.refs_1_
  32.3 0.0 collective-permute-done.8.refs_2_
  32.3 1.4 %collective-permute-start.11 = (bf16[2,64,2048]{2,1,0:T(8,128)(2,1)S(1)}, bf16[2,64,2048]{2,1,0:T(8,128)(2,1)S(1)}, u32[]{:S(2)}, u32[]{:S(2)}) collective-permute-start(bf16[2,64,2048]{2,1,0:T(8,128)(2,1)S(1)} %tie.6), channel_id=1, source_target_pairs={{0,16},{16,0},{1,17},{17,1},{2,18},{18,2},{3,19},{19,3},{4,20},{20... | collective-permute-start | bytes 1572872 | tf_op jit(solution)/shard_map/ppermute | solution.py:545
  33.8 0.0 copy-done.1
  33.8 3.0 %collective-permute-start.6 = (bf16[64,2048]{1,0:T(8,128)(2,1)S(1)}, bf16[64,2048]{1,0:T(8,128)(2,1)}, u32[]{:S(2)}, u32[]{:S(2)}) collective-permute-start(bf16[64,2048]{1,0:T(8,128)(2,1)S(1)} %tie.5), channel_id=1, source_target_pairs={{0,8},{4,12},{8,0},{12,4},{1,9},{5,13},{9,1},{13,5},{2,10},{6,14},... | collective-permute-start | bytes 786440 | tf_op jit(solution)/shard_map/ppermute | solution.py:542
  36.8 0.0 collective-permute-start.13
  36.8 1.5 %collective-permute-start.12 = (bf16[64,2048]{1,0:T(8,128)(2,1)}, bf16[64,2048]{1,0:T(8,128)(2,1)S(1)}, u32[]{:S(2)}, u32[]{:S(2)}) collective-permute-start(bf16[64,2048]{1,0:T(8,128)(2,1)} %tie.7), channel_id=1, source_target_pairs={{0,12},{4,8},{8,4},{12,0},{1,13},{5,9},{9,5},{13,1},{2,14},{6,10},... | collective-permute-start | bytes 786440 | tf_op jit(solution)/shard_map/ppermute | solution.py:542
  38.3 0.0 copy-done.3
  38.3 0.0 copy-start.2
  38.3 7.7 %project.1 = (bf16[256,2048]{1,0:T(8,128)(2,1)S(1)}, bf16[256,2048]{1,0:T(8,128)(2,1)S(1)}) custom-call(bf16[256,2048]{1,0:T(8,128)(2,1)S(1)} %get-tuple-element.126.x, bf16[2048,8192]{1,0:T(8,128)(2,1)} %w_in.3, bf16[256,2048]{1,0:T(8,128)(2,1)} %get-tuple-element.149.refs_1_.refs_0_), custom_call_target="tpu_custom_call" | custom-call | flops 1 | bytes 1 | tf_op jit(solution)/shard_map/project/pallas_call | solution.py:354
  46.0 1.3 %collective-permute-done.6.refs_1_ = bf16[64,2048]{1,0:T(8,128)(2,1)} collective-permute-done((bf16[64,2048]{1,0:T(8,128)(2,1)S(1)}, bf16[64,2048]{1,0:T(8,128)(2,1)}, u32[]{:S(2)}, u32[]{:S(2)}) %collective-permute-start.6) | collective-permute-done | bytes 262176 | tf_op jit(solution)/shard_map/ppermute | solution.py:542
  47.3 0.0 collective-permute-done.11
  47.3 0.0 copy-done.2
  47.3 0.0 copy-done.5
  47.3 0.0 copy-start
  47.3 9.3 %conditional.8 = (bf16[64,2048]{1,0:T(8,128)(2,1)}, bf16[4,64,256]{2,1,0:T(8,128)(2,1)S(1)}, bf16[256,2048]{1,0:T(8,128)(2,1)S(1)}) conditional(s32[]{:T(128)} %bitcast.4, (bf16[64,2048]{1,0:T(8,128)(2,1)}, s32[10]{0:T(128)S(1)}, s32[1,256]{1,0:T(1,128)S(1)}, bf16[256,2048]{1,0:T(8,128)(2,1)}, bf16[8,64,2048]{2,1,0:T(8,128)(2,1)S(1)}, ...), branch_computations={%region_2.0_spmd, %region_3.0_spmd} | conditional | flops 2113537 | bytes 8650857
  47.5 0.1 collective-permute-start.5
  47.6 0.6 collective-permute-start.4
  48.2 2.2 %shrink.3 = f32[64,256]{1,0:T(8,128)S(1)} custom-call(s32[10]{0:T(128)S(1)} %get-tuple-element.92.info, s32[1,256]{1,0:T(1,128)S(1)} %get-tuple-element.93.entries_ref, bf16[256,2048]{1,0:T(8,128)(2,1)} %get-tuple-element.94.x_ref, bf16[8,64,2048]{2,1,0:T(8,128)(2,1)S(1)} %get-tuple-element.95.near_ref, bf16[64,2048]{1,0:T(8,128)(2,1)} %get-tuple-element.96.refs_0_, ...), custom_call_target="tpu_custom_call" | custom-call | flops 1 | bytes 1 | tf_op jit(solution)/shard_map/cond/branch_1_fun/shrink/pallas_call | solution.py:406
  50.4 5.4 %all-gather.1 = bf16[256,256]{1,0:T(8,128)(2,1)S(1)} all-gather(bf16[64,256]{1,0:T(8,128)(2,1)S(1)} %convert_element_type.55), channel_id=3, replica_groups=mesh['group'=2,'store'=4,'tensor'=4] {'tensor'}, dimensions={0}, use_global_device_ids=true | all-gather | bytes 163840 | tf_op jit(solution)/shard_map/cond/branch_1_fun/all_gather | solution.py:603
  55.8 0.0 collective-permute-done.5
  55.8 0.4 add_convert_fusion.3
  56.2 0.4 collective-permute-done.4
  56.6 1.8 %collective-permute-done.12.refs_0_ = bf16[64,2048]{1,0:T(8,128)(2,1)S(1)} collective-permute-done((bf16[64,2048]{1,0:T(8,128)(2,1)}, bf16[64,2048]{1,0:T(8,128)(2,1)S(1)}, u32[]{:S(2)}, u32[]{:S(2)}) %collective-permute-start.12) | collective-permute-done | bytes 262176 | tf_op jit(solution)/shard_map/ppermute | solution.py:542
  58.5 0.7 %spread.1.refs_1_.wide_ref = bf16[256,512]{1,0:T(8,128)(2,1)S(1)} custom-call(s32[10]{0:T(128)S(1)} %get-tuple-element.120.info, s32[1,256]{1,0:T(1,128)S(1)} %copy-done.5, bf16[4,64,256]{2,1,0:T(8,128)(2,1)S(1)} %get-tuple-element.133.parts_ref, bf16[64,2048]{1,0:T(8,128)(2,1)S(1)} %collective-permute-done.12.refs_0_), custom_call_target="tpu_custom_call" | custom-call | flops 1 | bytes 8000000 | tf_op jit(solution)/shard_map/spread/pallas_call | solution.py:433
  59.2 0.6 collective-permute-start.15
  59.8 0.1 collective-permute-done.13.refs_0_
  59.9 0.0 collective-permute-done.14.refs_5_
  59.9 0.0 copy-done.4
  59.9 0.0 copy-done
  59.9 2.4 %expand.1.total_ref = f32[256,2048]{1,0:T(8,128)S(1)} custom-call(s32[10]{0:T(128)S(1)} %get-tuple-element.120.info, bf16[256,512]{1,0:T(8,128)(2,1)S(1)} %spread.1.refs_1_.wide_ref, bf16[8,64,2048]{2,1,0:T(8,128)(2,1)S(1)} %copy-done, bf16[2,64,2048]{2,1,0:T(8,128)(2,1)} %collective-permute-done.13.refs_0_, ...), custom_call_target="tpu_custom_call" | custom-call | flops 1 | bytes 1 | tf_op jit(solution)/shard_map/expand/pallas_call | solution.py:473
  62.3 3.3 %collective-permute-done.15.refs_0_ = bf16[64,2048]{1,0:T(8,128)(2,1)S(1)} collective-permute-done((bf16[64,2048]{1,0:T(8,128)(2,1)S(1)}, bf16[64,2048]{1,0:T(8,128)(2,1)S(1)}, u32[]{:S(2)}, u32[]{:S(2)}) %collective-permute-start.15) | collective-permute-done | bytes 262176 | tf_op jit(solution)/shard_map/ppermute | solution.py:545
  65.6 1.3 %finish.1 = bf16[256,2048]{1,0:T(8,128)(2,1)} custom-call(bf16[256,512]{1,0:T(8,128)(2,1)S(1)} %spread.1.refs_1_.wide_ref, f32[256,2048]{1,0:T(8,128)S(1)} %expand.1.total_ref, bf16[64,2048]{1,0:T(8,128)(2,1)S(1)} %collective-permute-done.15.refs_0_), custom_call_target="tpu_custom_call" | custom-call | flops 1 | bytes 1 | tf_op jit(solution)/shard_map/finish/pallas_call | solution.py:508
  (9 shorter events, 0.0 us)
Async XLA Ops:
  3.5 28.8 %collective-permute-start.7 = (bf16[64,2048]{1,0:T(8,128)(2,1)}, bf16[64,2048]{1,0:T(8,128)(2,1)}, u32[]{:S(2)}, u32[]{:S(2)}) collective-permute-start(bf16[64,2048]{1,0:T(8,128)(2,1)} %get-tuple-element.127), channel_id=1, source_target_pairs={{0,4},{4,0},{8,12},{12,8},{1,5},{5,1},{9,13},{13,9},{2,6},{6,2},{1... | collective-permute-start | bytes 786440 | tf_op jit(solution)/shard_map/ppermute | solution.py:542
  6.5 25.8 %collective-permute-start.8 = (bf16[64,2048]{1,0:T(8,128)(2,1)}, bf16[64,2048]{1,0:T(8,128)(2,1)}, u32[]{:S(2)}, u32[]{:S(2)}) collective-permute-start(bf16[64,2048]{1,0:T(8,128)(2,1)} %get-tuple-element.128), channel_id=1, source_target_pairs={{0,4},{4,0},{8,12},{12,8},{1,5},{5,1},{9,13},{13,9},{2,6},{6,2},{1... | collective-permute-start | bytes 786440 | tf_op jit(solution)/shard_map/ppermute | solution.py:542
  6.6 23.3 %collective-permute-start.9 = (bf16[64,2048]{1,0:T(8,128)(2,1)}, bf16[64,2048]{1,0:T(8,128)(2,1)S(1)}, u32[]{:S(2)}, u32[]{:S(2)}) collective-permute-start(bf16[64,2048]{1,0:T(8,128)(2,1)} %get-tuple-element.129), channel_id=1, source_target_pairs={{0,8},{4,12},{8,0},{12,4},{1,9},{5,13},{9,1},{13,5},{2,10},{6,14},... | collective-permute-start | bytes 786440 | tf_op jit(solution)/shard_map/ppermute | solution.py:542
  9.6 22.6 %collective-permute-start.10 = (bf16[64,2048]{1,0:T(8,128)(2,1)}, bf16[64,2048]{1,0:T(8,128)(2,1)S(1)}, u32[]{:S(2)}, u32[]{:S(2)}) collective-permute-start(bf16[64,2048]{1,0:T(8,128)(2,1)} %get-tuple-element.130), channel_id=1, source_target_pairs={{0,12},{4,8},{8,4},{12,0},{1,13},{5,9},{9,5},{13,1},{2,14},{6,10},... | collective-permute-start | bytes 786440 | tf_op jit(solution)/shard_map/ppermute | solution.py:542
  23.7 14.6 %copy-start.3 = (bf16[256,2048]{1,0:T(8,128)(2,1)}, bf16[256,2048]{1,0:T(8,128)(2,1)S(1)}, u32[]{:S(2)}) copy-start(bf16[256,2048]{1,0:T(8,128)(2,1)S(1)} %get-tuple-element.126.x) | copy-start | bytes 3145732
  24.3 2.7 %collective-permute-start.1 = (bf16[256,2048]{1,0:T(8,128)(2,1)S(1)}, bf16[256,2048]{1,0:T(8,128)(2,1)S(1)}, u32[]{:S(2)}, u32[]{:S(2)}) collective-permute-start(bf16[256,2048]{1,0:T(8,128)(2,1)S(1)} %get-tuple-element.79), channel_id=1, source_target_pairs={{0,1},{1,0},{2,3},{3,2},{4,5},{5,4},{6,7},{7,6},{8,9},{9,8},{10,11... | collective-permute-start | bytes 3145736 | tf_op jit(solution)/shard_map/cond/branch_1_fun/ppermute | solution.py:548
  28.3 5.4 %copy-start.1 = (bf16[64,2048]{1,0:T(8,128)(2,1)S(1)}, bf16[64,2048]{1,0:T(8,128)(2,1)}, u32[]{:S(2)}) copy-start(bf16[64,2048]{1,0:T(8,128)(2,1)} %get-tuple-element.123.refs_0_) | copy-start | bytes 786436
  28.3 31.5 %collective-permute-start.14 = (bf16[256,2048]{1,0:T(8,128)(2,1)}, bf16[256,2048]{1,0:T(8,128)(2,1)S(1)}, u32[]{:S(2)}, u32[]{:S(2)}) collective-permute-start(bf16[256,2048]{1,0:T(8,128)(2,1)} %get-tuple-element.149.refs_1_.refs_0_), channel_id=1, source_target_pairs={{0,2},{1,3},{2,0},{3,1},{4,6},{5,7},{6,4},{7,5},{8,10},{9,11},{10,... | collective-permute-start | bytes 3145736 | tf_op jit(solution)/shard_map/ppermute | solution.py:551
  32.3 14.9 %collective-permute-start.11 = (bf16[2,64,2048]{2,1,0:T(8,128)(2,1)S(1)}, bf16[2,64,2048]{2,1,0:T(8,128)(2,1)S(1)}, u32[]{:S(2)}, u32[]{:S(2)}) collective-permute-start(bf16[2,64,2048]{2,1,0:T(8,128)(2,1)S(1)} %tie.6), channel_id=1, source_target_pairs={{0,16},{16,0},{1,17},{17,1},{2,18},{18,2},{3,19},{19,3},{4,20},{20... | collective-permute-start | bytes 1572872 | tf_op jit(solution)/shard_map/ppermute | solution.py:545
  33.8 13.5 %collective-permute-start.6 = (bf16[64,2048]{1,0:T(8,128)(2,1)S(1)}, bf16[64,2048]{1,0:T(8,128)(2,1)}, u32[]{:S(2)}, u32[]{:S(2)}) collective-permute-start(bf16[64,2048]{1,0:T(8,128)(2,1)S(1)} %tie.5), channel_id=1, source_target_pairs={{0,8},{4,12},{8,0},{12,4},{1,9},{5,13},{9,1},{13,5},{2,10},{6,14},... | collective-permute-start | bytes 786440 | tf_op jit(solution)/shard_map/ppermute | solution.py:542
  36.8 23.1 %collective-permute-start.13 = (bf16[2,64,2048]{2,1,0:T(8,128)(2,1)}, bf16[2,64,2048]{2,1,0:T(8,128)(2,1)}, u32[]{:S(2)}, u32[]{:S(2)}) collective-permute-start(bf16[2,64,2048]{2,1,0:T(8,128)(2,1)} %tie.8), channel_id=1, source_target_pairs={{0,4},{4,0},{8,12},{12,8},{1,5},{5,1},{9,13},{13,9},{2,6},{6,2},{1... | collective-permute-start | bytes 1572872 | tf_op jit(solution)/shard_map/ppermute | solution.py:542
  36.8 21.7 %collective-permute-start.12 = (bf16[64,2048]{1,0:T(8,128)(2,1)}, bf16[64,2048]{1,0:T(8,128)(2,1)S(1)}, u32[]{:S(2)}, u32[]{:S(2)}) collective-permute-start(bf16[64,2048]{1,0:T(8,128)(2,1)} %tie.7), channel_id=1, source_target_pairs={{0,12},{4,8},{8,4},{12,0},{1,13},{5,9},{9,5},{13,1},{2,14},{6,10},... | collective-permute-start | bytes 786440 | tf_op jit(solution)/shard_map/ppermute | solution.py:542
  38.3 9.0 %copy-start.2 = (bf16[8,64,2048]{2,1,0:T(8,128)(2,1)S(1)}, bf16[8,64,2048]{2,1,0:T(8,128)(2,1)}, u32[]{:S(2)}) copy-start(bf16[8,64,2048]{2,1,0:T(8,128)(2,1)} %down.1) | copy-start | bytes 6291460
  38.3 9.0 %copy-start.5 = (s32[1,256]{1,0:T(1,128)S(1)}, s32[1,256]{1,0:T(1,128)}, u32[]{:S(2)}) copy-start(s32[1,256]{1,0:T(1,128)} %entries_ref.1) | copy-start | bytes 3076
  47.3 12.6 %copy-start = (bf16[8,64,2048]{2,1,0:T(8,128)(2,1)S(1)}, bf16[8,64,2048]{2,1,0:T(8,128)(2,1)}, u32[]{:S(2)}) copy-start(bf16[8,64,2048]{2,1,0:T(8,128)(2,1)} %near_ref.1) | copy-start | bytes 6291460
  47.5 8.3 %collective-permute-start.5 = (bf16[256,2048]{1,0:T(8,128)(2,1)S(1)}, bf16[256,2048]{1,0:T(8,128)(2,1)S(1)}, u32[]{:S(2)}, u32[]{:S(2)}) collective-permute-start(bf16[256,2048]{1,0:T(8,128)(2,1)S(1)} %get-tuple-element.101), channel_id=1, source_target_pairs={{0,1},{1,0},{2,3},{3,2},{4,5},{5,4},{6,7},{7,6},{8,9},{9,8},{10,11... | collective-permute-start | bytes 3145736 | tf_op jit(solution)/shard_map/cond/branch_1_fun/ppermute | solution.py:548
  47.6 9.0 %collective-permute-start.4 = (bf16[64,2048]{1,0:T(8,128)(2,1)}, bf16[64,2048]{1,0:T(8,128)(2,1)}, u32[]{:S(2)}, u32[]{:S(2)}) collective-permute-start(bf16[64,2048]{1,0:T(8,128)(2,1)} %get-tuple-element.91), channel_id=1, source_target_pairs={{0,16},{16,0},{1,17},{17,1},{2,18},{18,2},{3,19},{19,3},{4,20},{20... | collective-permute-start | bytes 786440 | tf_op jit(solution)/shard_map/cond/branch_1_fun/ppermute | solution.py:545
  56.6 3.3 %copy-start.4 = (bf16[256,2048]{1,0:T(8,128)(2,1)}, bf16[256,2048]{1,0:T(8,128)(2,1)S(1)}, u32[]{:S(2)}) copy-start(bf16[256,2048]{1,0:T(8,128)(2,1)S(1)} %get-tuple-element.142.refs_4_) | copy-start | bytes 3145732
  59.2 6.4 %collective-permute-start.15 = (bf16[64,2048]{1,0:T(8,128)(2,1)S(1)}, bf16[64,2048]{1,0:T(8,128)(2,1)S(1)}, u32[]{:S(2)}, u32[]{:S(2)}) collective-permute-start(bf16[64,2048]{1,0:T(8,128)(2,1)S(1)} %tie.9.refs_2_), channel_id=1, source_target_pairs={{0,16},{16,0},{1,17},{17,1},{2,18},{18,2},{3,19},{19,3},{4,20},{20... | collective-permute-start | bytes 786440 | tf_op jit(solution)/shard_map/ppermute | solution.py:545
